TPU v7x, 256 devices: a whole 4x4x8 slice. The times are simulated.
256 devices in a mesh: ctx: 16 (over x, y), head: 16 (over z, core).
Axes of the slice: x: 4, y: 4, z: 8, core: 2. Of those that a mesh axis runs over, the one named last changes fastest.
Arguments:
- lin_q: bfloat16 [4096, 64, 128], P('ctx', 'head'), may hold values from -6 to 6
- lin_k: bfloat16 [4096, 64, 128], P('ctx', 'head'), may hold values from -6 to 6
- lin_v: bfloat16 [4096, 64, 128], P('ctx', 'head'), may hold values from -6 to 6
- log_decay: float32 [64, 4096], P('head', 'ctx'), may hold values from -2.2 to 0
- lin_gain: float32 [64, 128], P('head'), may hold values from 0.1 to 1.9
- lin_grad: bfloat16 [4096, 64, 128], P('ctx', 'head'), may hold values from -6 to 6
- soft_q: bfloat16 [4096, 64, 128], P('ctx', 'head'), may hold values from -170 to 170
- soft_k: bfloat16 [4096, 8, 128], P('ctx'), may hold values from -6 to 6
- soft_v: bfloat16 [4096, 8, 128], P('ctx'), may hold values from -6 to 6
- soft_grad: bfloat16 [4096, 64, 128], P('ctx', 'head'), may hold values from -6 to 6
- span_reach: int32 [32], replicated, may hold values from 0 to 32, as said below
Outputs:
- lin_out: bfloat16 [4096, 64, 128], P('ctx', 'head')
- lin_dq: bfloat16 [4096, 64, 128], P('ctx', 'head')
- lin_dk: bfloat16 [4096, 64, 128], P('ctx', 'head')
- lin_dv: bfloat16 [4096, 64, 128], P('ctx', 'head')
- soft_out: bfloat16 [4096, 64, 128], P('ctx', 'head')
- soft_dq: bfloat16 [4096, 64, 128], P('ctx', 'head')
- soft_dk: bfloat16 [4096, 8, 128], P('ctx')
- soft_dv: bfloat16 [4096, 8, 128], P('ctx')
Inputs may be any that keep to these rules, and one draw needn't show every extreme that they name: span_reach[i] is 0 for a text block; for an image block it is one more than the index of the last block of the image span that holds block i. Block 0 is text; the last block belongs to an image span.
All inputs are finite; a program needn't handle non-finite values.
Results may differ from a plain program's by a relative error of at most 0.017.
Values may be sent and summed in bfloat16 or wider, within the bound.
No kernel may reach another device: no remote copies, remote signals or barrier semaphores. Data moves between devices by JAX's collectives and lax.ppermute only.
A program may use at most 64 MiB of HBM per device.

v0:
```python
import math

import jax
import jax.numpy as jnp
from jax import lax
from jax.sharding import PartitionSpec as P

HEAD_TOTAL = 64
HD = 128
KVH = 8
LB = 256
BLK = 128


PRECISE = lax.Precision.HIGHEST
EPSILON = 1e-05
FAR_BELOW = -1e30


def carried_in(value, axis, combine, identity, reverse):
    peers, here = (lax.axis_size(axis), lax.axis_index(axis))
    everything = jax.tree.map(
        lambda part, kind: lax.all_gather(part.astype(kind), axis),
        value,
        (jnp.bfloat16, jnp.bfloat16),
    )
    start = jax.tree.map(
        lambda part, zero: jnp.broadcast_to(jnp.asarray(zero, part.dtype), part.shape),
        value,
        identity,
    )

    def hop(k, before):
        at = peers - 1 - k if reverse else k
        reached = at > here if reverse else at < here
        new = combine(
            before, jax.tree.map(lambda part, own: part[at].astype(own.dtype), everything, value)
        )
        return jax.tree.map(lambda a, b: jnp.where(reached, a, b), new, before)

    return lax.fori_loop(0, peers, hop, start)


def decay_table(running):
    span_len = running.shape[-1]
    ordering = jnp.arange(span_len, dtype=jnp.int32)
    causal_pairs = ordering[:, None] >= ordering[None, :]
    return jnp.exp(
        jnp.where(causal_pairs, running[..., :, None] - running[..., None, :], FAR_BELOW)
    )


def join_forward(earlier, later_part):
    return (
        earlier[0] + later_part[0],
        jnp.exp(later_part[0])[:, None, None] * earlier[1] + later_part[1],
    )


def join_backward(earlier, later_part):
    return (
        earlier[0] + later_part[0],
        later_part[1] + jnp.exp(later_part[0])[:, None, None] * earlier[1],
    )


def light_layer(lin_q, lin_k, lin_v, log_decay, lin_gain, lin_grad):
    row_count, head_count, head_dim = lin_q.shape
    block_count = row_count // LB
    scaling = 1.0 / head_dim

    def blocked(array):
        return array.reshape(block_count, LB, head_count, head_dim)

    queries, keyset, valueset = (blocked(lin_q), blocked(lin_k), blocked(lin_v))
    running_all = jnp.cumsum(
        log_decay.reshape(head_count, block_count, LB).transpose(1, 0, 2), axis=2
    )
    block_totals = running_all[:, :, -1]
    head_fades = jnp.exp(running_all).transpose(0, 2, 1)[..., None]
    tail_fades = jnp.exp(block_totals[:, :, None] - running_all).transpose(0, 2, 1)[..., None]
    own_terms = jnp.einsum(
        "bshd,bshe->bhde",
        keyset.astype(jnp.float32) * tail_fades,
        valueset.astype(jnp.float32),
        precision=PRECISE,
    )
    zero_state = jnp.zeros((head_count, head_dim, head_dim), jnp.float32)
    zero_total = jnp.zeros((head_count,), jnp.float32)

    def fold_forward(carried_state, inputs):
        block_total, own_term = inputs
        return (jnp.exp(block_total)[:, None, None] * carried_state + own_term, None)

    own_state, _ = lax.scan(fold_forward, zero_state, (block_totals, own_terms))
    own_total = jnp.sum(block_totals, axis=0)
    incoming = carried_in(
        (own_total, own_state), "ctx", join_forward, (zero_total, zero_state), False
    )[1]

    def forward_step(carried_state, inputs):
        query_part, key_part, value_part, running, block_total, head_fade, own_term = inputs
        decays = decay_table(running)
        scores = jnp.einsum(
            "thd,shd->hts", query_part, key_part, preferred_element_type=jnp.float32
        )
        weights = (scores * decays * scaling).astype(jnp.bfloat16)
        within = jnp.einsum("hts,shd->thd", weights, value_part, preferred_element_type=jnp.float32)
        from_state = jnp.einsum(
            "thd,hde->the", query_part.astype(jnp.float32), carried_state, precision=PRECISE
        )
        next_state = jnp.exp(block_total)[:, None, None] * carried_state + own_term
        return (next_state, (within + scaling * head_fade * from_state, carried_state))

    _, (attended, entering) = lax.scan(
        forward_step,
        incoming,
        (queries, keyset, valueset, running_all, block_totals, head_fades, own_terms),
    )
    flattened = attended.reshape(row_count, head_count, head_dim)
    upstream = lin_grad.astype(jnp.float32) * lin_gain
    squares, cross_sum = lax.psum(
        (jnp.sum(flattened * flattened, axis=(1, 2)), jnp.sum(upstream * flattened, axis=(1, 2))),
        "head",
    )
    inverse = lax.rsqrt(squares / (HEAD_TOTAL * HD) + EPSILON)[:, None, None]
    lin_out = (flattened * inverse * lin_gain).astype(jnp.bfloat16)
    att_grad = (
        inverse * upstream - flattened * inverse**3 * (cross_sum / (HEAD_TOTAL * HD))[:, None, None]
    ).astype(jnp.bfloat16)
    grad_blocks = blocked(att_grad)
    back_terms = jnp.einsum(
        "bthd,bthe->bhde",
        queries.astype(jnp.float32) * head_fades,
        grad_blocks.astype(jnp.float32),
        precision=PRECISE,
    )

    def fold_backward(carried_state, inputs):
        block_total, back_term = inputs
        return (back_term + jnp.exp(block_total)[:, None, None] * carried_state, None)

    own_back, _ = lax.scan(fold_backward, zero_state, (block_totals, back_terms), reverse=True)
    outgoing = carried_in(
        (own_total, own_back), "ctx", join_backward, (zero_total, zero_state), True
    )[1]

    def backward_step(later_state, inputs):
        (
            query_part,
            key_part,
            value_part,
            grad_part,
            running,
            block_total,
            head_fade,
            tail_fade,
            carried_state,
            back_term,
        ) = inputs
        decays = decay_table(running)
        scores = jnp.einsum(
            "thd,shd->hts", query_part, key_part, preferred_element_type=jnp.float32
        )
        weights = (scores * decays * scaling).astype(jnp.bfloat16)
        grad_probs = jnp.einsum(
            "the,she->hts", grad_part, value_part, preferred_element_type=jnp.float32
        )
        grad_weights = (grad_probs * decays * scaling).astype(jnp.bfloat16)
        query_grad = jnp.einsum(
            "hts,shd->thd", grad_weights, key_part, preferred_element_type=jnp.float32
        ) + scaling * head_fade * jnp.einsum(
            "the,hde->thd", grad_part.astype(jnp.float32), carried_state, precision=PRECISE
        )
        key_grad = jnp.einsum(
            "hts,thd->shd", grad_weights, query_part, preferred_element_type=jnp.float32
        ) + scaling * tail_fade * jnp.einsum(
            "she,hde->shd", value_part.astype(jnp.float32), later_state, precision=PRECISE
        )
        value_grad = jnp.einsum(
            "hts,the->she", weights, grad_part, preferred_element_type=jnp.float32
        ) + scaling * tail_fade * jnp.einsum(
            "shd,hde->she", key_part.astype(jnp.float32), later_state, precision=PRECISE
        )
        earlier_state = back_term + jnp.exp(block_total)[:, None, None] * later_state
        return (
            earlier_state,
            (
                query_grad.astype(jnp.bfloat16),
                key_grad.astype(jnp.bfloat16),
                value_grad.astype(jnp.bfloat16),
            ),
        )

    _, (query_grads, key_grads, value_grads) = lax.scan(
        backward_step,
        outgoing,
        (
            queries,
            keyset,
            valueset,
            grad_blocks,
            running_all,
            block_totals,
            head_fades,
            tail_fades,
            entering,
            back_terms,
        ),
        reverse=True,
    )
    shape_own = (row_count, head_count, head_dim)
    return (
        lin_out,
        query_grads.reshape(shape_own),
        key_grads.reshape(shape_own),
        value_grads.reshape(shape_own),
    )


def reach_of(span_reach, query_pos):
    block_count = span_reach.shape[0]
    matches = (query_pos // BLK)[:, None] == jnp.arange(block_count, dtype=jnp.int32)[None, :]
    return jnp.sum(jnp.where(matches, span_reach[None, :], 0), axis=1)


def sight(query_pos, query_reach, key_pos):
    return (key_pos[None, :] <= query_pos[:, None]) | (
        key_pos[None, :] // BLK < query_reach[:, None]
    )


def pair_terms(query_part, grad_part, key_part, value_part, visible, log_mass, row_dot, scaling):
    scores = (
        jnp.einsum("thd,sd->hts", query_part, key_part, preferred_element_type=jnp.float32)
        * scaling
    )
    exact_probs = jnp.where(visible[None], jnp.exp(scores - log_mass[:, :, None]), 0.0)
    grad_probs = jnp.einsum(
        "the,se->hts", grad_part, value_part, preferred_element_type=jnp.float32
    )
    score_grads = (exact_probs * (grad_probs - row_dot[:, :, None]) * scaling).astype(jnp.bfloat16)
    return (exact_probs.astype(jnp.bfloat16), score_grads)


def soft_layer(soft_q, soft_k, soft_v, soft_grad, span_reach):
    row_count, head_count, head_dim = soft_q.shape
    kv_count = soft_k.shape[1]
    scaling = 1.0 / math.sqrt(head_dim)
    kv_index = lax.axis_index("head") * head_count // (HEAD_TOTAL // KVH)
    own_k = lax.dynamic_index_in_dim(soft_k, kv_index, 1, keepdims=False)
    own_v = lax.dynamic_index_in_dim(soft_v, kv_index, 1, keepdims=False)
    key_rows, value_rows = (
        lax.all_gather(own_k, "ctx", axis=0, tiled=True),
        lax.all_gather(own_v, "ctx", axis=0, tiled=True),
    )
    total_rows = key_rows.shape[0]
    block_width = math.gcd(total_rows, 512)
    block_count = total_rows // block_width
    query_pos = lax.axis_index("ctx") * row_count + jnp.arange(row_count, dtype=jnp.int32)
    query_reach = reach_of(span_reach, query_pos)
    key_blocks = key_rows.reshape(block_count, block_width, head_dim)
    value_blocks = value_rows.reshape(block_count, block_width, head_dim)
    block_starts = jnp.arange(block_count, dtype=jnp.int32) * block_width
    block_offsets = jnp.arange(block_width, dtype=jnp.int32)

    def forward_block(carried, inputs):
        key_part, value_part, first_row = inputs
        visible = sight(query_pos, query_reach, first_row + block_offsets)

        def forward_compute(state):
            row_max, row_mass, weighted = state
            scores = (
                jnp.einsum("thd,sd->hts", soft_q, key_part, preferred_element_type=jnp.float32)
                * scaling
            )
            new_max = jnp.maximum(
                row_max, jnp.max(jnp.where(visible[None], scores, FAR_BELOW), axis=2)
            )
            fading = jnp.exp(row_max - new_max)
            unscaled = jnp.where(visible[None], jnp.exp(scores - new_max[:, :, None]), 0.0)
            new_mass = row_mass * fading + jnp.sum(unscaled, axis=2)
            added = jnp.einsum(
                "hts,sd->thd",
                unscaled.astype(jnp.bfloat16),
                value_part,
                preferred_element_type=jnp.float32,
            )
            return (new_max, new_mass, weighted * fading.T[:, :, None] + added)

        return (lax.cond(jnp.any(visible), forward_compute, lambda state: state, carried), None)

    initial = (
        jnp.full((head_count, row_count), FAR_BELOW, jnp.float32),
        jnp.zeros((head_count, row_count), jnp.float32),
        jnp.zeros((row_count, head_count, head_dim), jnp.float32),
    )
    (row_max, row_mass, weighted), _ = lax.scan(
        forward_block, initial, (key_blocks, value_blocks, block_starts)
    )
    soft_out = (weighted / row_mass.T[:, :, None]).astype(jnp.bfloat16)
    log_mass = row_max + jnp.log(row_mass)
    out_wide = lax.optimization_barrier(soft_out).astype(jnp.float32)
    row_dot = jnp.sum(soft_grad.astype(jnp.float32) * out_wide, axis=2).T
    zero_grad = jnp.zeros((row_count, head_count, head_dim), jnp.float32)

    def merged_block(query_grad, inputs):
        key_part, value_part, first_row = inputs
        visible = sight(query_pos, query_reach, first_row + block_offsets)

        def merged_compute(grad_sum):
            rounded_probs, score_grads = pair_terms(
                soft_q, soft_grad, key_part, value_part, visible, log_mass, row_dot, scaling
            )
            key_term = jnp.einsum(
                "hts,thd->sd", score_grads, soft_q, preferred_element_type=jnp.float32
            )
            value_term = jnp.einsum(
                "hts,the->se", rounded_probs, soft_grad, preferred_element_type=jnp.float32
            )
            grad_sum = grad_sum + jnp.einsum(
                "hts,sd->thd", score_grads, key_part, preferred_element_type=jnp.float32
            )
            return (grad_sum, jnp.concatenate([key_term, value_term], axis=1))

        def nothing(grad_sum):
            return (grad_sum, jnp.zeros((block_width, 2 * head_dim), jnp.float32))

        return lax.cond(jnp.any(visible), merged_compute, nothing, query_grad)

    query_grad, terms = lax.scan(merged_block, zero_grad, (key_blocks, value_blocks, block_starts))
    summed = lax.psum_scatter(
        terms.reshape(total_rows, 2 * head_dim).astype(jnp.bfloat16),
        "ctx",
        scatter_dimension=0,
        tiled=True,
    ).astype(jnp.float32)
    slot = (jnp.arange(kv_count, dtype=jnp.int32) == kv_index).astype(jnp.float32)
    spread = summed[:, None, :] * slot[None, :, None]
    both = lax.psum(spread.astype(jnp.bfloat16), "head").astype(jnp.float32)
    key_grad = both[:, :, :head_dim]
    value_grad = both[:, :, head_dim:]
    return (
        soft_out,
        query_grad.astype(jnp.bfloat16),
        key_grad.astype(jnp.bfloat16),
        value_grad.astype(jnp.bfloat16),
    )


def per_device(
    lin_q,
    lin_k,
    lin_v,
    log_decay,
    lin_gain,
    lin_grad,
    soft_q,
    soft_k,
    soft_v,
    soft_grad,
    span_reach,
):
    lin_out, lin_dq, lin_dk, lin_dv = light_layer(
        lin_q, lin_k, lin_v, log_decay, lin_gain, lin_grad
    )
    soft_out, soft_dq, soft_dk, soft_dv = soft_layer(soft_q, soft_k, soft_v, soft_grad, span_reach)
    return (lin_out, lin_dq, lin_dk, lin_dv, soft_out, soft_dq, soft_dk, soft_dv)


def solution(mesh):
    placed = (
        P("ctx", "head", None),
        P("ctx", "head", None),
        P("ctx", "head", None),
        P("head", "ctx"),
        P("head", None),
        P("ctx", "head", None),
        P("ctx", "head", None),
        P("ctx", None, None),
        P("ctx", None, None),
        P("ctx", "head", None),
        P(),
    )
    return jax.shard_map(
        per_device,
        mesh=mesh,
        in_specs=placed,
        out_specs=(
            P("ctx", "head", None),
            P("ctx", "head", None),
            P("ctx", "head", None),
            P("ctx", "head", None),
            P("ctx", "head", None),
            P("ctx", "head", None),
            P("ctx", None, None),
            P("ctx", None, None),
        ),
        check_vma=False,
    )
```

profile of v0, /device:TPU:1, one launch (start us, length us, event | category | flops | bytes accessed | tf_op | source)
XLA Modules:
  0.0 527.8 jit_solution(7095765163107311839)
XLA Ops:
  9.1 1.2 constant_dynamic-slice_fusion
  11.7 1.2 reduce-window.6
  14.4 1.3 fusion.76
  17.3 17.7 %all-gather = bf16[16,4,1]{1,2,0:T(2,128)(2,1)S(1)} all-gather(bf16[1,4,1]{1,2,0:T(2,128)(2,1)S(1)} %slice.31), channel_id=2, replica_groups=mesh['ctx'=16,'head'=16] {'ctx'}, dimensions={0}, use_global_device_ids=true | all-gather | bytes 136 | tf_op jit(solution)/shard_map/all_gather | solution.py:23
  37.2 1.1 convolution_bitcast_fusion.11
  38.5 1.1 convert_multiply_fusion
  39.7 21.5 %all-gather.14.cloned.1.call-done = bf16[4096,1,128]{2,0,1:T(8,128)(2,1)} async-done(((bf16[256,1,128]{2,0,1:T(8,128)(2,1)}), bf16[4096,1,128]{2,0,1:T(8,128)(2,1)}) %all-gather.14.cloned.1.call-update) | async-done | bytes 1048592 | tf_op jit(solution)/shard_map/all_gather | solution.py:254
  61.2 50.1 %all-gather.16.cloned.1.call-done = bf16[4096,1,128]{2,0,1:T(8,128)(2,1)} async-done(((bf16[256,1,128]{2,0,1:T(8,128)(2,1)}), bf16[4096,1,128]{2,0,1:T(8,128)(2,1)}) %all-gather.16.cloned.1.call-update) | async-done | bytes 1048592 | tf_op jit(solution)/shard_map/all_gather | solution.py:255
  111.3 31.3 %while.86 = (s32[]{:T(128)}, f32[4,256]{1,0:T(4,128)S(1)}, f32[4,256]{1,0:T(4,128)S(1)}, f32[256,4,128]{2,0,1:T(8,128)S(1)}, s32[8]{0:T(128)}, /*index=5*/s32[25...) while((s32[]{:T(128)}, f32[4,256]{1,0:T(4,128)S(1)}, ...), condition=%wide.region_17.18_spmd.clone, body=%wide.region_11.17_spmd.clone.sunk | while | flops 275000576 | bytes 8466687 | solution.py:298
  111.3 1.3 dynamic_slice.180
  114.8 3.6 conditional.6
  114.8 1.4 fusion.8
  116.2 1.7 fusion.13
  118.4 1.3 dynamic_slice.180
  121.9 1.3 dynamic_slice.180
  125.3 1.3 dynamic_slice.180
  128.8 1.3 dynamic_slice.180
  132.2 1.3 dynamic_slice.180
  135.7 1.3 dynamic_slice.180
  139.2 1.3 dynamic_slice.180
  144.0 40.0 %while.87 = (s32[]{:T(128)}, f32[256,4,128]{2,0,1:T(8,128)S(1)}, bf16[8,512,256]{2,1,0:T(8,128)(2,1)}, s32[8]{0:T(128)}, s32[256]{0:T(256)S(1)}, /*index=5*/bf16...) while((s32[]{:T(128)}, f32[256,4,128]{2,0,1:T(8,128)S(1)}, ...), condition=%wide.region_23.24_spmd.clone, body=%wide.region_19.23_spmd.clone.sunk | while | flops 676471040 | bytes 14046447 | solution.py:331
  144.0 1.3 dynamic_slice.181
  147.4 5.3 %conditional.7 = (f32[256,4,128]{2,0,1:T(8,128)S(1)}, bf16[1,512,256]{1,2,0:T(8,128)(2,1)S(1)}) conditional(s32[]{:T(128)} %convert_element_type.256, f32[256,4,128]{2,0,1:T(8,128)S(1)} %get-tuple-element.1483, (pred[256,512]{0,1:T(8,128)(4,1)S(1)}, bf16[8,512,128]{2,1,0:T(8,128)(2,1)}, s32[]{:T(128)}, bf16[256,4,128]{0,2,1:T(8,128)(2,1)S(1)}, ...), branch_computations={%region_21.21_spmd, %region_22.22_spmd} | conditional | flops 675938304 | bytes 12854800 | solution.py:329
  147.4 1.5 fusion.33
  148.9 1.3 fusion.31
  151.3 1.4 fusion.34
  153.6 1.3 dynamic_slice.181
  157.9 1.3 dynamic_slice.181
  162.3 1.3 dynamic_slice.181
  166.6 1.3 dynamic_slice.181
  170.9 1.3 dynamic_slice.181
  175.3 1.3 dynamic_slice.181
  179.6 1.3 dynamic_slice.181
  184.1 27.2 %while.88 = (s32[]{:T(128)}, f32[4,128,128]{2,1,0:T(8,128)S(1)}, s32[]{:T(128)}, bf16[16,4]{1,0:T(8,128)(2,1)}, bf16[16,4,128,128]{3,2,1,0:T(8,128)(2,1)}, /*index=5*/s32[]{:T(128)}, s32[]{:T(128)}) while((s32[]{:T(128)}, f32[4,128,128]{2,1,0:T(8,128)S(1)}, s32[]{:T(128)}, bf16[16,4]{1,0:T(8,128)(2,1)}, ...), condition=%wide.region_3.4_spmd.clone, body=%wide.region_2.3_spmd.clone.sunk | while | flops 327688 | bytes 655505 | solution.py:41
  190.0 1.0 fusion.119
  191.7 1.0 fusion.119
  193.4 1.0 fusion.119
  211.8 25.5 %all-reduce = (f32[256]{0:T(256)S(1)}, f32[256]{0:T(256)S(1)}) all-reduce(f32[256]{0:T(256)S(1)} %get-tuple-element.1064, f32[256]{0:T(256)S(1)} %get-tuple-element.1063), channel_id=1, replica_groups=mesh['ctx'=16,'head'=16] {'head'}, use_global_device_ids=true, to_apply=%region_5.6 | all-reduce | flops 512 | bytes 4096 | tf_op jit(solution)/shard_map/psum | solution.py:122
  237.3 86.9 %reduce-scatter.2.cloned.1.call-done = bf16[256,256]{1,0:T(8,128)(2,1)} async-done(((bf16[4096,256]{1,0:T(8,128)(2,1)}), bf16[256,256]{1,0:T(8,128)(2,1)}) %reduce-scatter.2.cloned.1.call-update) | async-done | bytes 131088 | tf_op jit(solution)/shard_map/reduce_scatter | solution.py:332
  325.2 1.2 multiply_convert_fusion
  327.5 2.3 fusion.77
  330.0 1.1 copy.275
  333.1 1.8 copy.214
  335.3 1.4 convolution_bitcast_fusion.7
  336.6 102.1 %all-reduce.3.cloned.1.call-done = bf16[256,8,256]{2,1,0:T(8,128)(2,1)} async-done(((bf16[256,8,256]{2,1,0:T(8,128)(2,1)}), bf16[256,8,256]{2,1,0:T(8,128)(2,1)}) %all-reduce.3.cloned.1.call-update) | async-done | bytes 1048592 | tf_op jit(solution)/shard_map/psum | solution.py:340
  438.8 2.2 fusion.93
  441.0 50.2 %all-gather.12.cloned.1.call-done = bf16[64,128,128]{2,1,0:T(8,128)(2,1)} async-done(((bf16[4,128,128]{2,1,0:T(8,128)(2,1)}), bf16[64,128,128]{2,1,0:T(8,128)(2,1)}) %all-gather.12.cloned.1.call-update) | async-done | bytes 2097168 | tf_op jit(solution)/shard_map/all_gather | solution.py:23
  491.2 27.2 %while.89 = (s32[]{:T(128)}, f32[4,128,128]{2,1,0:T(8,128)S(1)}, s32[]{:T(128)}, bf16[16,4,128,128]{3,2,1,0:T(8,128)(2,1)}, bf16[16,4]{1,0:T(8,128)(2,1)}, /*index=5*/s32[]{:T(128)}, s32[]{:T(128)}, s32[]{:T(128)}, s32[]{:T(128)}) while((s32[]{:T(128)}, f32[4,128,128]{2,1,0:T(8,128)S(1)}, s32[]{:T(128)}, ...), condition=%wide.region_9.10_spmd.clone, body=%wide.region_8.9_spmd.clone.sunk | while | flops 327692 | bytes 655567 | solution.py:41
  (267 shorter events, 101.3 us)
Async XLA Ops:
  7.2 1.0 copy-start
  7.2 6.8 %copy-start.2 = (bf16[256,4,128]{2,1,0:T(4,128)(2,1)S(1)}, bf16[256,4,128]{2,1,0:T(4,128)(2,1)}, u32[]{:S(2)}) copy-start(bf16[256,4,128]{2,1,0:T(4,128)(2,1)} %param.24) | copy-start | bytes 786436
  7.2 7.2 %copy-start.3 = (bf16[256,4,128]{2,1,0:T(4,128)(2,1)S(1)}, bf16[256,4,128]{2,1,0:T(4,128)(2,1)}, u32[]{:S(2)}) copy-start(bf16[256,4,128]{2,1,0:T(4,128)(2,1)} %param.25) | copy-start | bytes 786436
  7.2 9.1 %copy-start.9 = (bf16[256,4,128]{2,1,0:T(4,128)(2,1)S(1)}, bf16[256,4,128]{2,1,0:T(4,128)(2,1)}, u32[]{:S(2)}) copy-start(bf16[256,4,128]{2,1,0:T(4,128)(2,1)} %param.29) | copy-start | bytes 786436
  7.2 54.0 %all-gather.14.cloned.1.call-start = ((), (), s32[]{:S(2)}) async-start(), calls=%async_computation.5 | async-start | bytes 1114112 | tf_op jit(solution)/shard_map/all_gather | solution.py:254
  9.0 102.2 %all-gather.16.cloned.1.call-start = ((), (), s32[]{:S(2)}) async-start(), calls=%async_computation.6 | async-start | bytes 1114112 | tf_op jit(solution)/shard_map/all_gather | solution.py:255
  10.9 173.1 %all-gather.10.cloned.1.call-start = ((), (), s32[]{:S(2)}) async-start(), calls=%async_computation.3 | async-start | bytes 2228224 | tf_op jit(solution)/shard_map/all_gather | solution.py:23
  12.9 4.3 copy-start.10
  13.3 3.8 copy-start.18
  14.0 21.9 %copy-start.1 = (bf16[256,4,128]{2,1,0:T(4,128)(2,1)S(1)}, bf16[256,4,128]{2,1,0:T(4,128)(2,1)}, u32[]{:S(2)}) copy-start(bf16[256,4,128]{2,1,0:T(4,128)(2,1)} %param.23) | copy-start | bytes 786436
  15.7 308.6 %reduce-scatter.2.cloned.1.call-start = ((), (), s32[]{:S(2)}) async-start(), calls=%async_computation.1 | async-start | bytes 2228224 | tf_op jit(solution)/shard_map/reduce_scatter | solution.py:332
  17.1 19.3 %copy-start.13 = (pred[256,256]{1,0:T(8,128)(4,1)}, pred[256,256]{1,0:T(8,128)(4,1)S(1)}, u32[]{:S(2)}) copy-start(pred[256,256]{1,0:T(8,128)(4,1)S(1)} %iota_compare_fusion) | copy-start | bytes 196612
  17.3 21.0 %copy-start.12 = (bf16[256,4,128]{2,1,0:T(4,128)(2,1)S(1)}, bf16[256,4,128]{2,1,0:T(4,128)(2,1)}, u32[]{:S(2)}) copy-start(bf16[256,4,128]{2,1,0:T(4,128)(2,1)} %param.28) | copy-start | bytes 786436
  36.0 2.5 copy-start.16
  36.0 3.6 copy-start.21
  36.4 0.8 copy-start.5
  143.2 0.7 copy-start.8
  184.0 27.3 %copy-start.4 = (f32[256,4,128]{0,2,1:T(8,128)S(1)}, f32[256,4,128]{0,2,1:T(8,128)}, u32[]{:S(2)}) copy-start(f32[256,4,128]{0,2,1:T(8,128)} %convolution_bitcast_fusion.11) | copy-start | bytes 1572868
  184.0 27.3 %copy-start.15 = (f32[4,128]{1,0:T(4,128)S(1)}, f32[4,128]{1,0:T(4,128)}, u32[]{:S(2)}) copy-start(f32[4,128]{1,0:T(4,128)} %param.27) | copy-start | bytes 6148
  184.0 254.8 %all-reduce.3.cloned.1.call-start = ((), (), s32[]{:S(2)}) async-start(), calls=%async_computation.2 | async-start | bytes 2097152 | tf_op jit(solution)/shard_map/psum | solution.py:340
  184.1 141.1 %copy-start.20 = (f32[8]{0:T(128)S(1)}, f32[8]{0:T(128)}, u32[]{:S(2)}) copy-start(f32[8]{0:T(128)} %compare_convert_fusion) | copy-start | bytes 100
  211.8 115.7 %copy-start.19 = (f32[4]{0:T(128)S(1)}, f32[4]{0:T(128)}, u32[]{:S(2)}) copy-start(f32[4]{0:T(128)} %copy-done.18) | copy-start | bytes 52
  325.2 4.7 copy-start.11
  326.4 4.7 copy-start.14
  326.4 4.7 copy-start.17
  326.4 164.8 %all-gather.12.cloned.1.call-start = ((), (), s32[]{:S(2)}) async-start(), calls=%async_computation.4 | async-start | bytes 2228224 | tf_op jit(solution)/shard_map/all_gather | solution.py:23
  331.5 1.6 copy-start.7
  331.5 3.4 copy-start.6
Sparse Core Ops, SparseCore 0:
  11.1 50.1 all-gather.13
  64.2 47.0 all-gather.15
  114.3 49.9 all-gather.9
  184.1 140.1 reduce-scatter.1
  326.5 112.1 all-reduce.2
  441.6 49.4 all-gather.11
where the time goes:
time: 531 us; the launch traced here: 528 us
  waiting for transfers between devices  311 us (59%)
  other arithmetic  86.7 us (16%)
  blocking collectives  43.1 us (8%)
  local copies, waits for them, and re-layouts  42.5 us (8%)
  matrix products  17.5 us (3%)
  between operations  14.6 us (3%)
  loops' own time  12.1 us (2%)
    psum x1, waiting for transfers between devices, soft_layer(): both = lax.psum(spread.astype(jnp.bfloat16), 'head').astype(jnp.float32)  102 us
    reduce_scatter x1, waiting for transfers between devices, soft_layer(): lax.psum_scatter(terms.reshape(total_rows, 2 * head_dim).astype(jnp.bfloa...  86.9 us
    all_gather x2, waiting for transfers between devices, carried_in(): lax.all_gather(part.astype(kind), axis)  50.2 us
    all_gather x1, waiting for transfers between devices, soft_layer(): lax.all_gather(own_v, 'ctx', axis=0, tiled=True)  50.1 us
    select_n x32, other arithmetic, hop(): return jax.tree.map(lambda a, b: jnp.where(reached, a, b), new, before)  32.4 us
    psum x1, blocking collectives, light_layer(): lax.psum((jnp.sum(flattened * flattened, axis=(1, 2)), jnp.sum(upstream *...  25.5 us
    all_gather x1, waiting for transfers between devices, soft_layer(): lax.all_gather(own_k, 'ctx', axis=0, tiled=True)  21.5 us
    dynamic_slice x16, local copies, waits for them, and re-layouts, soft_layer(): lax.scan(forward_block, initial, (key_blocks, value_blocks, block_starts))  20.1 us
  transfers between devices with their start and end apart: 6, of which 5 were waited for; matrix products, arithmetic and copies ran while one was open for 21% of the time, Pallas kernels for 0%

commit v1 on v0

v1 whole, which is shorter than its diff:
```python
import functools
import math

import jax
import jax.numpy as jnp
from jax import lax
from jax.experimental import pallas as pl
from jax.experimental.pallas import tpu as pltpu
from jax.sharding import PartitionSpec as P

HEAD_TOTAL = 64
HD = 128
KVH = 8
LB = 256
BLK = 128
CTX = 16
HEADS = 16
OWN = 4
ROWS = LB * OWN
HALF = LB // 2
SLICE = OWN * HD // CTX
EPSILON = 1e-05
FAR_BELOW = -1e30
SCALE_LIN = 1.0 / HD
SCALE_SOFT = 1.0 / math.sqrt(HD)
LOG2E = 1.4426950408889634
KEYS = 256
GROUPS = 2 * CTX * HALF // KEYS
PIECES = KEYS // HALF

f32 = jnp.float32
bf16 = jnp.bfloat16
PRECISE = lax.Precision.HIGHEST


def dot(a, b, dims, precision=None):
    return lax.dot_general(a, b, (dims, ((), ())), precision=precision, preferred_element_type=f32)


NN = ((1,), (0,))
NT = ((1,), (1,))
TN = ((0,), (0,))


def split_heads(source, scratch):
    scratch[...] = source[...].astype(f32)
    return [scratch[pl.ds(h, LB, stride=OWN), :] for h in range(OWN)]


def join_heads(parts, scratch, target):
    for h in range(OWN):
        scratch[pl.ds(h, LB, stride=OWN), :] = parts[h]
    target[...] = scratch[...].astype(bf16)


def run_sums(log_decay):
    row = lax.broadcasted_iota(jnp.int32, (LB, LB), 0)
    col = lax.broadcasted_iota(jnp.int32, (LB, LB), 1)
    upto = (row <= col).astype(f32)
    as_rows = dot(log_decay, upto, NN, PRECISE)
    as_cols = dot((row >= col).astype(f32), log_decay, NT, PRECISE)
    return as_rows, as_cols, row, col


def local_kernel(q_ref, k_ref, v_ref, decay_ref, kv_ref, pay_ref, within_ref, heads_ref, scratch):
    queries = [x.astype(bf16) for x in split_heads(q_ref, scratch)]
    keys_wide = split_heads(k_ref, scratch)
    values = [x.astype(bf16) for x in split_heads(v_ref, scratch)]
    as_rows, as_cols, row, col = run_sums(decay_ref[...])
    for j in range(CTX):
        pay_ref[j, 0:LB, :] = kv_ref[...]
    for h in range(OWN):
        run_row, run_col = as_rows[h : h + 1, :], as_cols[:, h : h + 1]
        total = run_row[:, LB - 1 : LB]
        keys = keys_wide[h].astype(bf16)
        heads_ref[0, h] = queries[h]
        heads_ref[1, h] = keys
        heads_ref[2, h] = values[h]
        tailed = (keys_wide[h] * jnp.exp(total - run_col)).astype(bf16)
        own = dot(tailed, values[h], TN).astype(bf16)
        high = total.astype(bf16)
        low = (total - high.astype(f32)).astype(bf16)
        marks = jnp.concatenate(
            [
                jnp.broadcast_to(high.astype(f32), (8, HD)),
                jnp.broadcast_to(low.astype(f32), (8, HD)),
            ],
            axis=0,
        ).astype(bf16)
        for i in range(OWN):
            pay_ref[h * OWN + i, LB : LB + SLICE, :] = own[i * SLICE : (i + 1) * SLICE]
            pay_ref[h * OWN + i, LB + SLICE :, :] = marks
        decays = jnp.exp(jnp.where(row >= col, run_col - run_row, FAR_BELOW))
        weights = (dot(queries[h], keys, NT) * decays * SCALE_LIN).astype(bf16)
        within_ref[h] = dot(weights, values[h], NN)


def prefix_kernel(got_ref, out_ref):
    state = jnp.zeros((SLICE, HD), f32)
    for j in range(CTX):
        out_ref[j] = state.astype(bf16)
        marks = got_ref[j, LB + SLICE :, :].astype(f32)
        fade = jnp.exp(marks[0:1, :] + marks[8:9, :])
        state = fade * state + got_ref[j, LB : LB + SLICE, :].astype(f32)


def attend_kernel(within_ref, heads_ref, state_ref, decay_ref, grad_ref, gain_ref, att_ref, up_ref, sums_ref, scratch):
    _, as_cols, _, _ = run_sums(decay_ref[...])
    grads = split_heads(grad_ref, scratch)
    squares = jnp.zeros((LB, HD), f32)
    crossed = jnp.zeros((LB, HD), f32)
    for h in range(OWN):
        state = state_ref[h * HD : (h + 1) * HD, :]
        fade = SCALE_LIN * jnp.exp(as_cols[:, h : h + 1])
        attended = within_ref[h] + fade * dot(heads_ref[0, h], state, NN)
        upstream = grads[h] * gain_ref[h : h + 1, :]
        att_ref[h] = attended
        up_ref[h] = upstream
        squares = squares + attended * attended
        crossed = crossed + upstream * attended
    ones = jnp.ones((8, HD), f32)
    square_row = dot(ones, squares, NT, PRECISE)
    cross_row = dot(ones, crossed, NT, PRECISE)
    first = lax.broadcasted_iota(jnp.int32, (8, LB), 0) < 4
    both = jnp.where(first, square_row, cross_row)
    for j in range(HEADS):
        sums_ref[j] = both


def grad_kernel(att_ref, up_ref, got_ref, heads_ref, decay_ref, gain_ref, out_ref, ag_ref, back_ref, scratch):
    _, as_cols, row, col = run_sums(decay_ref[...])
    total = got_ref[0]
    for j in range(1, HEADS):
        total = total + got_ref[j]
    cols = dot((row == col).astype(f32), total, NT, PRECISE)
    inverse = lax.rsqrt(cols[:, 0:1] / (HEAD_TOTAL * HD) + EPSILON)
    pull = inverse * inverse * inverse * (cols[:, 4:5] / (HEAD_TOTAL * HD))
    outs = []
    for h in range(OWN):
        attended = att_ref[h]
        outs.append(attended * inverse * gain_ref[h : h + 1, :])
        att_grad = (inverse * up_ref[h] - attended * pull).astype(bf16)
        ag_ref[h] = att_grad
        faded = (heads_ref[0, h].astype(f32) * jnp.exp(as_cols[:, h : h + 1])).astype(bf16)
        back = dot(faded, att_grad, TN).astype(bf16)
        back_ref[h * HD : (h + 1) * HD, :] = back
    join_heads(outs, scratch, out_ref)


def inner_kernel(heads_ref, ag_ref, state_ref, decay_ref, dq_ref, dk_ref, dv_ref, scratch):
    as_rows, as_cols, row, col = run_sums(decay_ref[...])
    query_grads = []
    for h in range(OWN):
        run_row, run_col = as_rows[h : h + 1, :], as_cols[:, h : h + 1]
        query, key, value, grad = heads_ref[0, h], heads_ref[1, h], heads_ref[2, h], ag_ref[h]
        decays = SCALE_LIN * jnp.exp(jnp.where(row >= col, run_col - run_row, FAR_BELOW))
        turned = SCALE_LIN * jnp.exp(jnp.where(col >= row, run_row - run_col, FAR_BELOW))
        grad_weights = (dot(grad, value, NT) * decays).astype(bf16)
        grad_turned = (dot(value, grad, NT) * turned).astype(bf16)
        weights_turned = (dot(key, query, NT) * turned).astype(bf16)
        state = state_ref[h * HD : (h + 1) * HD, :]
        fade = SCALE_LIN * jnp.exp(run_col)
        query_grads.append(dot(grad_weights, key, NN) + fade * dot(grad, state, NT))
        dk_ref[h] = dot(grad_turned, query, NN)
        dv_ref[h] = dot(weights_turned, grad, NN)
    join_heads(query_grads, scratch, dq_ref)


def finish_kernel(dk_ref, dv_ref, heads_ref, later_ref, decay_ref, dk_out, dv_out, scratch):
    as_rows, as_cols, _, _ = run_sums(decay_ref[...])
    key_grads, value_grads = [], []
    for h in range(OWN):
        later = later_ref[h * HD : (h + 1) * HD, :]
        tail = SCALE_LIN * jnp.exp(as_rows[h : h + 1, LB - 1 : LB] - as_cols[:, h : h + 1])
        key_grads.append(dk_ref[h] + tail * dot(heads_ref[2, h], later, NT))
        value_grads.append(dv_ref[h] + tail * dot(heads_ref[1, h], later, NN))
    join_heads(key_grads, scratch, dk_out)
    join_heads(value_grads, scratch, dv_out)


def soft_kernel(
    info_ref, q_ref, do_ref, mine_ref, other_ref, out_ref, dq_ref, dmine_ref, dother_ref, s_ref, p_ref
):
    base, side, reach0, reach1 = info_ref[0], info_ref[1], info_ref[2], info_ref[3]
    lowest = jnp.minimum(jnp.maximum(base + 1, reach0), jnp.maximum(base + 1 + BLK, reach1))
    highest = jnp.maximum(jnp.maximum(base + BLK, reach0), jnp.maximum(base + 2 * BLK, reach1))
    place = lax.broadcasted_iota(jnp.int32, (1, ROWS), 1) // OWN
    limit = jnp.maximum(base + place + 1, jnp.where(place < BLK, reach0, reach1))
    per_source = GROUPS // 2
    span = PIECES * LB
    used = (highest + span - 1) // span

    def keys_of(ref, g, part):
        block = ref[pl.ds(g * PIECES, PIECES), part * HALF : (part + 1) * HALF, :]
        return block.reshape(KEYS, HD)

    def both(step, carry):
        def body(g, carry):
            carry = step(mine_ref, dmine_ref, g, g, side, carry)
            return step(other_ref, dother_ref, g, per_source + g, 1 - side, carry)

        return lax.fori_loop(0, used, body, carry)

    queries = q_ref[...]

    def find_max(ref, _, g, at, half, top):
        scores = dot(keys_of(ref, g, 0), queries, NT)
        first = g * span + half * HALF

        def masked():
            index = lax.broadcasted_iota(jnp.int32, (KEYS, 1), 0)
            where = first + (index // HALF) * LB + index % HALF
            return jnp.where(where < limit, scores, FAR_BELOW)

        scores = lax.cond((g + 1) * span <= lowest, lambda: scores, masked)
        s_ref[at] = scores
        return jnp.maximum(top, jnp.max(scores.reshape(KEYS // 8, 8, ROWS), axis=0))

    top = both(find_max, jnp.full((8, ROWS), FAR_BELOW, f32))
    top = jnp.max(top, axis=0, keepdims=True)
    factor = SCALE_SOFT * LOG2E
    shift = top * factor

    def weigh(ref, _, g, at, half, carry):
        mass, out = carry
        probs = jnp.exp2(s_ref[at] * factor - shift)
        mass = mass + jnp.sum(probs.reshape(KEYS // 8, 8, ROWS), axis=0)
        probs = probs.astype(bf16)
        p_ref[at] = probs
        return mass, out + dot(keys_of(ref, g, 1), probs, TN)

    mass, out = both(weigh, (jnp.zeros((8, ROWS), f32), jnp.zeros((HD, ROWS), f32)))
    inverse = 1.0 / jnp.sum(mass, axis=0, keepdims=True)
    out = (out * inverse).astype(bf16)
    out_ref[...] = out.T
    grads = do_ref[...].astype(f32).T
    adjust = inverse * SCALE_SOFT
    row_dot = jnp.sum(grads * out.astype(f32), axis=0, keepdims=True) * adjust
    grads = (grads * adjust).astype(bf16)
    grad_rows = grads.T

    def pull(ref, target, g, at, half, dq):
        probs = p_ref[at]
        moved = dot(keys_of(ref, g, 1), grads, NN)
        pulls = (probs.astype(f32) * (moved - row_dot)).astype(bf16)
        dk = dot(pulls, queries, NN)
        dv = dot(probs, grad_rows, NN) * (1.0 / SCALE_SOFT)
        target[pl.ds(g * PIECES, PIECES), 0:HALF, :] = dk.astype(bf16).reshape(PIECES, HALF, HD)
        target[pl.ds(g * PIECES, PIECES), HALF:LB, :] = dv.astype(bf16).reshape(PIECES, HALF, HD)
        return dq + dot(keys_of(ref, g, 0), pulls, TN)

    dq = both(pull, jnp.zeros((HD, ROWS), f32))
    dq_ref[...] = dq.astype(bf16).T

    def clear(g, carry):
        zero = jnp.zeros((PIECES, LB, HD), bf16)
        dmine_ref[pl.ds(g * PIECES, PIECES)] = zero
        dother_ref[pl.ds(g * PIECES, PIECES)] = zero
        return carry

    lax.fori_loop(used, per_source, clear, 0)


def merge_kernel(mine_ref, got_ref, back_ref, pay_ref):
    for j in range(CTX):
        pay_ref[j, 0:LB, :] = (mine_ref[j].astype(f32) + got_ref[j].astype(f32)).astype(bf16)
        pay_ref[j, LB:, :] = back_ref[j]


def suffix_kernel(got_ref, fades_ref, block_ref, out_ref):
    block = got_ref[0, 0:LB, :].astype(f32)
    for j in range(1, CTX):
        block = block + got_ref[j, 0:LB, :].astype(f32)
    block_ref[...] = block.astype(bf16)
    state = jnp.zeros((SLICE, HD), f32)
    for j in reversed(range(CTX)):
        out_ref[j] = state.astype(bf16)
        marks = fades_ref[j].astype(f32)
        fade = jnp.exp(marks[0:1, :] + marks[8:9, :])
        state = fade * state + got_ref[j, LB:, :].astype(f32)


def spread_kernel(mine_ref, other_ref, info_ref, dk_ref, dv_ref, scratch):
    side = info_ref[1]
    for part, target in ((0, dk_ref), (1, dv_ref)):
        for z in range(KVH):
            rows = slice(part * HALF, (part + 1) * HALF)
            scratch[pl.ds(side * (HALF * KVH) + z, HALF, stride=KVH), :] = mine_ref[z, rows, :].astype(f32)
            scratch[pl.ds((1 - side) * (HALF * KVH) + z, HALF, stride=KVH), :] = other_ref[z, rows, :].astype(f32)
        target[...] = scratch[...].astype(bf16)


def call(kernel, outs, scratch=(), smem=(), count=0, flops=0, limit=32):
    spaces = [pl.BlockSpec(memory_space=pltpu.SMEM if n in smem else pltpu.VMEM) for n in range(count)]
    return pl.pallas_call(
        kernel,
        out_shape=[jax.ShapeDtypeStruct(shape, kind) for shape, kind in outs],
        in_specs=spaces,
        out_specs=[pl.BlockSpec(memory_space=pltpu.VMEM) for _ in outs],
        scratch_shapes=[pltpu.VMEM(shape, kind) for shape, kind in scratch],
        compiler_params=pltpu.CompilerParams(vmem_limit_bytes=limit * 1024 * 1024),
        cost_estimate=pl.CostEstimate(flops=flops, bytes_accessed=1 << 20, transcendentals=0),
    )


WIDE = ((ROWS, HD), f32)
FLAT = ((ROWS, HD), bf16)
BY_HEAD = ((OWN, LB, HD), f32)
OTHER_CORE = [(i, i ^ 1) for i in range(HEADS)]
SAME_CORE = [[2 * z + c for z in range(KVH)] for c in range(2)]


def per_device(lin_q, lin_k, lin_v, log_decay, lin_gain, lin_grad, soft_q, soft_k, soft_v, soft_grad, span_reach):
    here, head = lax.axis_index("ctx"), lax.axis_index("head")
    kv, side = head // 2, head % 2
    flat = lambda x: x.reshape(ROWS, HD)
    lin_q, lin_k, lin_v, lin_grad, soft_q, soft_grad = map(
        flat, (lin_q, lin_k, lin_v, lin_grad, soft_q, soft_grad)
    )
    reaches = lax.dynamic_slice(span_reach, (2 * here,), (2,)) * BLK
    info = jnp.concatenate([jnp.stack([here * LB, side]).astype(jnp.int32), reaches])
    kv_half = jnp.concatenate(
        [
            lax.dynamic_slice(x, (side * HALF, kv, 0), (HALF, 1, HD)).reshape(HALF, HD)
            for x in (soft_k, soft_v)
        ]
    )
    decay = jnp.concatenate([log_decay, jnp.zeros((8 - OWN, LB), f32)])

    pay, within, heads = call(
        local_kernel,
        [((CTX, LB + SLICE + 16, HD), bf16), BY_HEAD, ((3, OWN, LB, HD), bf16)],
        [WIDE],
        count=5,
        flops=10**9,
    )(lin_q, lin_k, lin_v, decay, kv_half)
    got = lax.all_to_all(pay, "ctx", 0, 0)
    mine = got[:, :LB]
    fades = got[:, LB + SLICE :]
    other = lax.ppermute(mine, "head", OTHER_CORE)
    (prefixes,) = call(prefix_kernel, [((CTX, SLICE, HD), bf16)], count=1, flops=10**8)(got)
    state = lax.all_to_all(prefixes, "ctx", 0, 0).reshape(OWN * HD, HD)

    soft_out, soft_dq, dmine, dother = call(
        soft_kernel,
        [FLAT, FLAT, ((CTX, LB, HD), bf16), ((CTX, LB, HD), bf16)],
        [((GROUPS, KEYS, ROWS), f32), ((GROUPS, KEYS, ROWS), bf16)],
        smem=(0,),
        count=5,
        flops=10**10,
        limit=56,
    )(info, soft_q, soft_grad, mine, other)
    dgot = lax.ppermute(dother, "head", OTHER_CORE)

    attended, upstream, sums = call(
        attend_kernel,
        [BY_HEAD, BY_HEAD, ((HEADS, 8, LB), f32)],
        [WIDE],
        count=6,
        flops=10**9,
    )(within, heads, state, decay, lin_grad, lin_gain)
    sums = lax.all_to_all(sums, "head", 0, 0)
    lin_out, att_grad, back = call(
        grad_kernel,
        [FLAT, ((OWN, LB, HD), bf16), ((OWN * HD, HD), bf16)],
        [WIDE],
        count=6,
        flops=10**9,
    )(attended, upstream, sums, heads, decay, lin_gain)
    (pay_back,) = call(merge_kernel, [((CTX, LB + SLICE, HD), bf16)], count=3, flops=10**8)(
        dmine, dgot, back.reshape(CTX, SLICE, HD)
    )
    got_back = lax.all_to_all(pay_back, "ctx", 0, 0)
    lin_dq, dk_own, dv_own = call(
        inner_kernel, [FLAT, BY_HEAD, BY_HEAD], [WIDE], count=4, flops=10**9
    )(heads, att_grad, state, decay)
    block, suffixes = call(
        suffix_kernel, [((LB, HD), bf16), ((CTX, SLICE, HD), bf16)], count=2, flops=10**8
    )(got_back, fades)
    later = lax.all_to_all(suffixes, "ctx", 0, 0).reshape(OWN * HD, HD)
    spread = lax.all_to_all(
        jnp.broadcast_to(block[None], (KVH, LB, HD)), "head", 0, 0, axis_index_groups=SAME_CORE
    )
    spread_other = lax.ppermute(spread, "head", OTHER_CORE)
    lin_dk, lin_dv = call(finish_kernel, [FLAT, FLAT], [WIDE], count=5, flops=10**9)(
        dk_own, dv_own, heads, later, decay
    )
    soft_dk, soft_dv = call(
        spread_kernel,
        [((LB * KVH, HD), bf16), ((LB * KVH, HD), bf16)],
        [((LB * KVH, HD), f32)],
        smem=(2,),
        count=3,
        flops=10**8,
    )(spread, spread_other, info)
    deep = lambda x: x.reshape(LB, OWN, HD)
    return (
        deep(lin_out),
        deep(lin_dq),
        deep(lin_dk),
        deep(lin_dv),
        deep(soft_out),
        deep(soft_dq),
        soft_dk.reshape(LB, KVH, HD),
        soft_dv.reshape(LB, KVH, HD),
    )


def solution(mesh):
    long, short = P("ctx", "head", None), P("ctx", None, None)
    return jax.shard_map(
        per_device,
        mesh=mesh,
        in_specs=(long, long, long, P("head", "ctx"), P("head", None), long, long, short, short, long, P()),
        out_specs=(long, long, long, long, long, long, short, short),
        check_vma=False,
    )
```

time: 531 us -> 160 us (0.30)
  waiting for transfers between devices: 311 us -> 25.1 us
  other arithmetic: 86.7 us -> 0.67 us
  blocking collectives: 43.1 us -> 92.8 us
  local copies, waits for them, and re-layouts: 42.5 us -> 8.64 us
  Pallas kernels: 0 us -> 19 us
  matrix products: 17.5 us -> 0 us
  between operations: 14.6 us -> 0.79 us
  loops' own time: 12.1 us -> 0 us
  starting transfers between devices: 0.43 us -> 12.5 us
    all_gather x4 -> x0, waiting for transfers between devices: 122 us -> none  [the longest x2 50.2 us: carried_in(): lax.all_gather(part.astype(kind), axis)]
    psum x1 -> x0, waiting for transfers between devices: 102 us -> none  [soft_layer(): both = lax.psum(spread.astype(jnp.bfloat16), 'head').astype(jnp.float32)]
    all_to_all x0 -> x4, blocking collectives: none -> 92.8 us  [the longest x1 30.1 us: per_device(): state = lax.all_to_all(prefixes, 'ctx', 0, 0).reshape(OWN * HD, HD)]
    reduce_scatter x1 -> x0, waiting for transfers between devices: 86.9 us -> none  [soft_layer(): lax.psum_scatter(terms.reshape(total_rows, 2 * head_dim).astype(jnp.bfloa...]
    select_n x49 -> x0, other arithmetic: 42.9 us -> none  [the longest x32 32.4 us: hop(): return jax.tree.map(lambda a, b: jnp.where(reached, a, b), new, before)]
    psum x1 -> x0, blocking collectives: 25.5 us -> none  [light_layer(): lax.psum((jnp.sum(flattened * flattened, axis=(1, 2)), jnp.sum(upstream *...]
    all_to_all x0 -> x2, waiting for transfers between devices: none -> 23.1 us  [the longest x1 19.6 us: per_device(): got_back = lax.all_to_all(pay_back, 'ctx', 0, 0)]
    exp x32 -> x0, other arithmetic: 21.3 us -> none  [the longest x16 10.7 us: join_forward(): jnp.exp(later_part[0])[:, None, None] * earlier[1] + later_part[1]]
  transfers between devices with their start and end apart: 6 -> 5, of which waited for: 5 -> 3; matrix products, arithmetic and copies ran while one was open for 21% -> 0% of each run, Pallas kernels for 0% -> 4%
where the time goes in v1:
time: 160 us
  blocking collectives  92.8 us (58%)
  waiting for transfers between devices  25.1 us (16%)
  Pallas kernels  19 us (12%)
  starting transfers between devices  12.5 us (8%)
  local copies, waits for them, and re-layouts  8.64 us (5%)
    all_to_all x1, blocking collectives, per_device(): state = lax.all_to_all(prefixes, 'ctx', 0, 0).reshape(OWN * HD, HD)  30.1 us
    all_to_all x1, blocking collectives, per_device(): got = lax.all_to_all(pay, 'ctx', 0, 0)  25.2 us
    all_to_all x1, waiting for transfers between devices, per_device(): got_back = lax.all_to_all(pay_back, 'ctx', 0, 0)  19.6 us
    all_to_all x1, blocking collectives, per_device(): sums = lax.all_to_all(sums, 'head', 0, 0)  19 us
    all_to_all x1, blocking collectives, per_device(): lax.all_to_all(jnp.broadcast_to(block[None], (KVH, LB, HD)), 'head', 0, 0...  18.5 us
    pallas_call x1, Pallas kernels, per_device(): call(soft_kernel, [FLAT, FLAT, ((CTX, LB, HD), bf16), ((CTX, LB, HD), bf1...  7.32 us
    unnamed x24, local copies, waits for them, and re-layouts  5.57 us
    all_to_all x1, starting transfers between devices, per_device(): later = lax.all_to_all(suffixes, 'ctx', 0, 0).reshape(OWN * HD, HD)  3.93 us
  transfers between devices with their start and end apart: 5, of which 3 were waited for; matrix products, arithmetic and copies ran while one was open for 0% of the time, Pallas kernels for 4%

profile of v1, /device:TPU:1, one launch (start us, length us, event | category | flops | bytes accessed | tf_op | source)
XLA Modules:
  0.0 159.5 jit_solution(14744407132575029699)
XLA Ops:
  0.7 1.2 constant_dynamic-slice_fusion
  1.9 0.7 concatenate.9.decay_ref
  2.6 0.0 copy-start.3
  2.6 0.9 copy-done.3
  3.5 0.0 copy-start.4
  3.5 0.9 copy-done.4
  4.5 0.0 copy-start.5
  4.5 0.9 copy-done.5
  5.4 1.8 %shard_map.170 = (bf16[16,304,128]{2,1,0:T(8,128)(2,1)S(1)}, f32[4,256,128]{2,1,0:T(8,128)S(1)}, bf16[3,4,256,128]{3,2,1,0:T(8,128)(2,1)S(1)}) custom-call(bf16[1024,128]{1,0:T(8,128)(2,1)S(1)} %bitcast.29, bf16[1024,128]{1,0:T(8,128)(2,1)S(1)} %bitcast.30, bf16[1024,128]{1,0:T(8,128)(2,1)S(1)} %bitcast.31, f32[8,256]{1,0:T(8,128)S(1)} %concatenate.9.decay_ref, ...), custom_call_target="tpu_custom_call" | custom-call | flops 1000000000 | bytes 1048576 | tf_op jit(solution)/shard_map/pallas_call | solution.py:330
  7.2 25.2 %all_to_all.30.got_ref = bf16[16,304,128]{2,1,0:T(8,128)(2,1)S(1)} all-to-all(bf16[16,304,128]{2,1,0:T(8,128)(2,1)S(1)} %get-tuple-element.32), channel_id=1, replica_groups=mesh['ctx'=16,'head'=16] {'ctx'}, dimensions={0} | all-to-all | bytes 2490368 | tf_op jit(solution)/shard_map/all_to_all | solution.py:337
  32.5 0.0 copy-start.10
  32.5 1.1 slice.8.mine_ref
  33.6 2.1 %collective-permute-start = (bf16[16,256,128]{2,1,0:T(8,128)(2,1)}, bf16[16,256,128]{2,1,0:T(8,128)(2,1)}, u32[]{:S(2)}, u32[]{:S(2)}) collective-permute-start(bf16[16,256,128]{2,1,0:T(8,128)(2,1)} %slice.8.mine_ref), channel_id=1, source_target_pairs={{0,1},{1,0},{2,3},{3,2},{4,5},{5,4},{6,7},{7,6},{8,9},{9,8},{10,11... | collective-permute-start | bytes 3145736 | tf_op jit(solution)/shard_map/ppermute | solution.py:340
  35.8 0.0 copy-done.10
  35.8 0.1 dynamic-slice_multiply_fusion
  35.8 0.6 pad_add_fusion.info_ref
  36.4 2.0 %collective-permute-done.other_ref = bf16[16,256,128]{2,1,0:T(8,128)(2,1)} collective-permute-done((bf16[16,256,128]{2,1,0:T(8,128)(2,1)}, bf16[16,256,128]{2,1,0:T(8,128)(2,1)}, u32[]{:S(2)}, u32[]{:S(2)}) %collective-permute-start) | collective-permute-done | bytes 1048608 | tf_op jit(solution)/shard_map/ppermute | solution.py:340
  38.4 7.3 %shard_map.175 = (bf16[1024,128]{1,0:T(8,128)(2,1)}, bf16[1024,128]{1,0:T(8,128)(2,1)}, bf16[16,256,128]{2,1,0:T(8,128)(2,1)}, bf16[16,256,128]{2,1,0:T(8,128)(2,1)}) custom-call(s32[4]{0:T(128)} %pad_add_fusion.info_ref, bf16[1024,128]{1,0:T(8,128)(2,1)} %bitcast.37, bf16[1024,128]{1,0:T(8,128)(2,1)} %bitcast.38, bf16[16,256,128]{2,1,0:T(8,128)(2,1)} %slice.8.mine_ref, ...), custom_call_target="tpu_custom_call" | custom-call | flops 10000000000 | bytes 1048576 | tf_op jit(solution)/shard_map/pallas_call | solution.py:344
  45.7 0.0 copy-start.6
  45.7 0.0 copy-start.7
  45.7 0.4 collective-permute-start.1
  46.1 30.1 %all_to_all.31 = bf16[16,32,128]{2,1,0:T(8,128)(2,1)S(1)} all-to-all(bf16[16,32,128]{2,1,0:T(8,128)(2,1)S(1)} %shard_map.171), channel_id=1, replica_groups=mesh['ctx'=16,'head'=16] {'ctx'}, dimensions={0} | all-to-all | bytes 262144 | tf_op jit(solution)/shard_map/all_to_all | solution.py:342
  76.2 0.0 copy-done.6
  76.2 0.0 copy-done.7
  76.2 1.2 shard_map.172
  77.5 19.0 %all_to_all.32.got_ref = f32[16,8,256]{2,1,0:T(8,128)S(1)} all-to-all(f32[16,8,256]{2,1,0:T(8,128)S(1)} %get-tuple-element.35), channel_id=1, replica_groups=mesh['ctx'=16,'head'=16] {'head'}, dimensions={0} | all-to-all | bytes 262144 | tf_op jit(solution)/shard_map/all_to_all | solution.py:362
  96.4 1.8 %shard_map.173 = (bf16[1024,128]{1,0:T(8,128)(2,1)}, bf16[4,256,128]{2,1,0:T(8,128)(2,1)S(1)}, bf16[512,128]{1,0:T(8,128)(2,1)S(1)}) custom-call(f32[4,256,128]{2,1,0:T(8,128)S(1)} %get-tuple-element.33.att_ref, f32[4,256,128]{2,1,0:T(8,128)S(1)} %get-tuple-element.34.up_ref, f32[16,8,256]{2,1,0:T(8,128)S(1)} %all_to_all.32.got_ref, ...), custom_call_target="tpu_custom_call" | custom-call | flops 1000000000 | bytes 1048576 | tf_op jit(solution)/shard_map/pallas_call | solution.py:363
  98.2 0.7 copy-done.8
  98.9 0.0 collective-permute-done.1.got_ref
  98.9 0.0 copy-done.1
  98.9 0.2 shard_map.176
  99.1 0.0 copy-start
  99.2 1.0 copy-done
  100.2 3.7 %all-to-all-start.3 = ((bf16[16,288,128]{2,1,0:T(8,128)(2,1)}), bf16[16,288,128]{2,1,0:T(8,128)(2,1)S(1)}, u32[]{:S(2)}, u32[]{:S(2)}) async-start(bf16[16,288,128]{2,1,0:T(8,128)(2,1)} %copy-done), calls=%async_computation.3 | async-start | bytes 2359296 | tf_op jit(solution)/shard_map/all_to_all | solution.py:373
  103.9 19.6 %all-to-all-done.3.got_ref = bf16[16,288,128]{2,1,0:T(8,128)(2,1)S(1)} async-done(((bf16[16,288,128]{2,1,0:T(8,128)(2,1)}), bf16[16,288,128]{2,1,0:T(8,128)(2,1)S(1)}, u32[]{:S(2)}, u32[]{:S(2)}) %all-to-all-start.3) | async-done | bytes 1179680 | tf_op jit(solution)/shard_map/all_to_all | solution.py:373
  123.5 0.7 shard_map.177
  124.2 0.1 broadcast_in_dim.2
  124.3 18.5 %all_to_all.33.mine_ref = bf16[8,256,128]{2,1,0:T(8,128)(2,1)S(1)} all-to-all(bf16[8,256,128]{2,1,0:T(8,128)(2,1)S(1)} %broadcast_in_dim.2), channel_id=1, replica_groups={{0,2,4,6,8,10,12,14},{1,3,5,7,9,11,13,15},{16,18,20,22,24,26,28,30},{17..., dimensions={0} | all-to-all | bytes 1048576 | tf_op jit(solution)/shard_map/all_to_all | solution.py:381
  142.8 2.3 %collective-permute-start.2 = (bf16[8,256,128]{2,1,0:T(8,128)(2,1)S(1)}, bf16[8,256,128]{2,1,0:T(8,128)(2,1)S(1)}, u32[]{:S(2)}, u32[]{:S(2)}) collective-permute-start(bf16[8,256,128]{2,1,0:T(8,128)(2,1)S(1)} %all_to_all.33.mine_ref), channel_id=1, source_target_pairs={{0,1},{1,0},{2,3},{3,2},{4,5},{5,4},{6,7},{7,6},{8,9},{9,8},{10,11... | collective-permute-start | bytes 1572872 | tf_op jit(solution)/shard_map/ppermute | solution.py:384
  145.1 3.9 %all-to-all-start.4 = ((bf16[16,32,128]{2,1,0:T(8,128)(2,1)}), bf16[16,32,128]{2,1,0:T(8,128)(2,1)S(1)}, u32[]{:S(2)}, u32[]{:S(2)}) async-start(bf16[16,32,128]{2,1,0:T(8,128)(2,1)} %get-tuple-element.44), calls=%async_computation.4 | async-start | bytes 262144 | tf_op jit(solution)/shard_map/all_to_all | solution.py:380
  149.1 0.0 copy-start.9
  149.1 0.9 copy-done.9
  150.0 2.2 %shard_map.174 = (bf16[1024,128]{1,0:T(8,128)(2,1)}, f32[4,256,128]{2,1,0:T(8,128)S(1)}, f32[4,256,128]{2,1,0:T(8,128)S(1)}) custom-call(bf16[3,4,256,128]{3,2,1,0:T(8,128)(2,1)S(1)} %get-tuple-element.31.heads_ref, bf16[4,256,128]{2,1,0:T(8,128)(2,1)S(1)} %copy-done.9, bf16[512,128]{1,0:T(8,128)(2,1)S(1)} %bitcast.26, f32[8,256]{1,0:T(8,128)S(1)} %concatenate.9.decay_ref), custom_call_target="tpu_custom_call" | custom-call | flops 1000000000 | bytes 1048576 | tf_op jit(solution)/shard_map/pallas_call | solution.py:374
  152.2 3.6 %all-to-all-done.4 = bf16[16,32,128]{2,1,0:T(8,128)(2,1)S(1)} async-done(((bf16[16,32,128]{2,1,0:T(8,128)(2,1)}), bf16[16,32,128]{2,1,0:T(8,128)(2,1)S(1)}, u32[]{:S(2)}, u32[]{:S(2)}) %all-to-all-start.4) | async-done | bytes 131104 | tf_op jit(solution)/shard_map/all_to_all | solution.py:380
  155.8 1.7 %shard_map.178 = (bf16[1024,128]{1,0:T(8,128)(2,1)}, bf16[1024,128]{1,0:T(8,128)(2,1)}) custom-call(f32[4,256,128]{2,1,0:T(8,128)S(1)} %get-tuple-element.39.dk_ref, f32[4,256,128]{2,1,0:T(8,128)S(1)} %get-tuple-element.40.dv_ref, bf16[3,4,256,128]{3,2,1,0:T(8,128)(2,1)S(1)} %get-tuple-element.31.heads_ref, bf16[512,128]{1,0:T(8,128)(2,1)S(1)} %bitcast.27, ...), custom_call_target="tpu_custom_call" | custom-call | flops 1000000000 | bytes 1048576 | tf_op jit(solution)/shard_map/pallas_call | solution.py:385
  157.5 0.0 collective-permute-done.2.other_ref
  157.5 0.0 copy-done.2
  157.5 2.0 %shard_map.179 = (bf16[2048,128]{1,0:T(8,128)(2,1)}, bf16[2048,128]{1,0:T(8,128)(2,1)}) custom-call(bf16[8,256,128]{2,1,0:T(8,128)(2,1)S(1)} %all_to_all.33.mine_ref, bf16[8,256,128]{2,1,0:T(8,128)(2,1)S(1)} %collective-permute-done.2.other_ref, s32[4]{0:T(128)S(1)} %copy-done.2), custom_call_target="tpu_custom_call" | custom-call | flops 100000000 | bytes 1048576 | tf_op jit(solution)/shard_map/pallas_call | solution.py:388
  (8 shorter events, 0.1 us)
Async XLA Ops:
  2.6 0.9 copy-start.3
  3.5 0.9 copy-start.4
  4.5 0.9 copy-start.5
  32.5 3.3 %copy-start.10 = (s32[32]{0:T(128)S(1)}, s32[32]{0:T(128)}, u32[]{:S(2)}) copy-start(s32[32]{0:T(128)} %param.21) | copy-start | bytes 388
  33.6 4.8 %collective-permute-start = (bf16[16,256,128]{2,1,0:T(8,128)(2,1)}, bf16[16,256,128]{2,1,0:T(8,128)(2,1)}, u32[]{:S(2)}, u32[]{:S(2)}) collective-permute-start(bf16[16,256,128]{2,1,0:T(8,128)(2,1)} %slice.8.mine_ref), channel_id=1, source_target_pairs={{0,1},{1,0},{2,3},{3,2},{4,5},{5,4},{6,7},{7,6},{8,9},{9,8},{10,11... | collective-permute-start | bytes 3145736 | tf_op jit(solution)/shard_map/ppermute | solution.py:340
  45.7 30.5 %copy-start.6 = (bf16[256,4,128]{2,1,0:T(4,128)(2,1)S(1)}, bf16[256,4,128]{2,1,0:T(4,128)(2,1)}, u32[]{:S(2)}) copy-start(bf16[256,4,128]{2,1,0:T(4,128)(2,1)} %param.16) | copy-start | bytes 786436
  45.7 30.5 %copy-start.7 = (f32[4,128]{1,0:T(4,128)S(1)}, f32[4,128]{1,0:T(4,128)}, u32[]{:S(2)}) copy-start(f32[4,128]{1,0:T(4,128)} %gain_ref.3) | copy-start | bytes 6148
  45.7 53.2 %collective-permute-start.1 = (bf16[16,256,128]{2,1,0:T(8,128)(2,1)}, bf16[16,256,128]{2,1,0:T(8,128)(2,1)S(1)}, u32[]{:S(2)}, u32[]{:S(2)}) collective-permute-start(bf16[16,256,128]{2,1,0:T(8,128)(2,1)} %get-tuple-element.42), channel_id=1, source_target_pairs={{0,1},{1,0},{2,3},{3,2},{4,5},{5,4},{6,7},{7,6},{8,9},{9,8},{10,11... | collective-permute-start | bytes 3145736 | tf_op jit(solution)/shard_map/ppermute | solution.py:353
  96.4 2.5 %copy-start.1 = (bf16[16,256,128]{2,1,0:T(8,128)(2,1)S(1)}, bf16[16,256,128]{2,1,0:T(8,128)(2,1)}, u32[]{:S(2)}) copy-start(bf16[16,256,128]{2,1,0:T(8,128)(2,1)} %get-tuple-element.41.mine_ref) | copy-start | bytes 3145732
  98.2 0.7 copy-start.8
  99.1 1.1 copy-start
  100.2 23.3 %all-to-all-start.3 = ((bf16[16,288,128]{2,1,0:T(8,128)(2,1)}), bf16[16,288,128]{2,1,0:T(8,128)(2,1)S(1)}, u32[]{:S(2)}, u32[]{:S(2)}) async-start(bf16[16,288,128]{2,1,0:T(8,128)(2,1)} %copy-done), calls=%async_computation.3 | async-start | bytes 2359296 | tf_op jit(solution)/shard_map/all_to_all | solution.py:373
  142.8 14.7 %collective-permute-start.2 = (bf16[8,256,128]{2,1,0:T(8,128)(2,1)S(1)}, bf16[8,256,128]{2,1,0:T(8,128)(2,1)S(1)}, u32[]{:S(2)}, u32[]{:S(2)}) collective-permute-start(bf16[8,256,128]{2,1,0:T(8,128)(2,1)S(1)} %all_to_all.33.mine_ref), channel_id=1, source_target_pairs={{0,1},{1,0},{2,3},{3,2},{4,5},{5,4},{6,7},{7,6},{8,9},{9,8},{10,11... | collective-permute-start | bytes 1572872 | tf_op jit(solution)/shard_map/ppermute | solution.py:384
  145.1 10.7 %all-to-all-start.4 = ((bf16[16,32,128]{2,1,0:T(8,128)(2,1)}), bf16[16,32,128]{2,1,0:T(8,128)(2,1)S(1)}, u32[]{:S(2)}, u32[]{:S(2)}) async-start(bf16[16,32,128]{2,1,0:T(8,128)(2,1)} %get-tuple-element.44), calls=%async_computation.4 | async-start | bytes 262144 | tf_op jit(solution)/shard_map/all_to_all | solution.py:380
  149.1 1.0 copy-start.9
  155.8 1.7 %copy-start.2 = (s32[4]{0:T(128)S(1)}, s32[4]{0:T(128)}, u32[]{:S(2)}) copy-start(s32[4]{0:T(128)} %pad_add_fusion.info_ref) | copy-start | bytes 52

commit v2 on v1

v2 whole, which is shorter than its diff:
```python
import functools
import math

import jax
import jax.numpy as jnp
from jax import lax
from jax.experimental import pallas as pl
from jax.experimental.pallas import tpu as pltpu
from jax.sharding import PartitionSpec as P

HEAD_TOTAL = 64
HD = 128
KVH = 8
LB = 256
BLK = 128
CTX = 16
HEADS = 16
OWN = 4
ROWS = LB * OWN
HALF = LB // 2
SLICE = OWN * HD // CTX
EPSILON = 1e-05
FAR_BELOW = -1e30
SCALE_LIN = 1.0 / HD
SCALE_SOFT = 1.0 / math.sqrt(HD)
LOG2E = 1.4426950408889634
KEYS = 512
PIECES = KEYS // HALF
PER_SOURCE = CTX // PIECES
GROUPS = 2 * PER_SOURCE
SPAN = PIECES * LB

f32 = jnp.float32
bf16 = jnp.bfloat16
PRECISE = lax.Precision.HIGHEST


def dot(a, b, dims, precision=None):
    return lax.dot_general(a, b, (dims, ((), ())), precision=precision, preferred_element_type=f32)


NN = ((1,), (0,))
NT = ((1,), (1,))
TN = ((0,), (0,))


def split_heads(source, scratch):
    scratch[...] = source[...].astype(f32)
    return [scratch[pl.ds(h, LB, stride=OWN), :] for h in range(OWN)]


def join_heads(parts, scratch, target):
    for h in range(OWN):
        scratch[pl.ds(h, LB, stride=OWN), :] = parts[h]
    target[...] = scratch[...].astype(bf16)


def run_sums(log_decay):
    row = lax.broadcasted_iota(jnp.int32, (LB, LB), 0)
    col = lax.broadcasted_iota(jnp.int32, (LB, LB), 1)
    upto = (row <= col).astype(f32)
    as_rows = dot(log_decay, upto, NN, PRECISE)
    as_cols = dot((row >= col).astype(f32), log_decay, NT, PRECISE)
    return as_rows, as_cols, row, col


def local_kernel(
    q_hbm, k_hbm, v_hbm, decay_hbm, sk_hbm, sv_hbm, pay_hbm, within_hbm, heads_hbm,
    scratch, raw, halves, decay_ref, kv_ref, own_ref, within_ref, heads_ref, sems, out_sems,
):
    side = lax.axis_index("head") % 2
    kv = lax.axis_index("head") // 2
    half = pl.ds(pl.multiple_of(side * (HALF * KVH), HALF * KVH), HALF * KVH)
    copies = [
        pltpu.make_async_copy(sk_hbm.at[half], halves.at[0], sems.at[0]),
        pltpu.make_async_copy(sv_hbm.at[half], halves.at[1], sems.at[1]),
        pltpu.make_async_copy(k_hbm, raw.at[1], sems.at[2]),
        pltpu.make_async_copy(v_hbm, raw.at[2], sems.at[3]),
        pltpu.make_async_copy(q_hbm, raw.at[0], sems.at[4]),
        pltpu.make_async_copy(decay_hbm, decay_ref, sems.at[5]),
    ]
    for copy in copies:
        copy.start()
    for n in range(2):
        copies[n].wait()
        scratch[...] = halves[n].astype(f32)
        kv_ref[n * HALF : (n + 1) * HALF, :] = scratch[pl.ds(kv, HALF, stride=KVH), :].astype(bf16)
    sent = [
        pltpu.make_async_copy(kv_ref, pay_hbm.at[j, pl.ds(0, LB)], out_sems.at[j]) for j in range(CTX)
    ]
    for copy in sent:
        copy.start()
    copies[5].wait()
    as_rows, as_cols, row, col = run_sums(decay_ref[...])
    copies[2].wait()
    keys_wide = split_heads(raw.at[1], scratch)
    copies[3].wait()
    values = [x.astype(bf16) for x in split_heads(raw.at[2], scratch)]
    for h in range(OWN):
        run_col = as_cols[:, h : h + 1]
        total = as_rows[h : h + 1, LB - 1 : LB]
        heads_ref[1, h] = keys_wide[h].astype(bf16)
        heads_ref[2, h] = values[h]
        tailed = (keys_wide[h] * jnp.exp(total - run_col)).astype(bf16)
        own = dot(tailed, values[h], TN).astype(bf16)
        high = total.astype(bf16).astype(f32)
        marks = jnp.concatenate(
            [jnp.broadcast_to(high, (8, HD)), jnp.broadcast_to(total - high, (8, HD))], axis=0
        ).astype(bf16)
        for i in range(OWN):
            j = h * OWN + i
            own_ref[j, 0:SLICE, :] = own[i * SLICE : (i + 1) * SLICE]
            own_ref[j, SLICE:, :] = marks
    states = pltpu.make_async_copy(own_ref, pay_hbm.at[:, pl.ds(LB, SLICE + 16)], out_sems.at[CTX])
    states.start()
    copies[4].wait()
    queries = [x.astype(bf16) for x in split_heads(raw.at[0], scratch)]
    for h in range(OWN):
        heads_ref[0, h] = queries[h]
    kept = pltpu.make_async_copy(heads_ref, heads_hbm, out_sems.at[CTX + 1])
    kept.start()
    for h in range(OWN):
        decays = jnp.exp(jnp.where(row >= col, as_cols[:, h : h + 1] - as_rows[h : h + 1, :], FAR_BELOW))
        weights = (dot(queries[h], heads_ref[1, h], NT) * decays * SCALE_LIN).astype(bf16)
        within_ref[h] = dot(weights, values[h], NN)
    inner = pltpu.make_async_copy(within_ref, within_hbm, out_sems.at[CTX + 2])
    inner.start()
    for copy in sent + [states, kept, inner]:
        copy.wait()


def prefix_kernel(got_ref, out_ref):
    state = jnp.zeros((SLICE, HD), f32)
    for j in range(CTX):
        out_ref[j] = state.astype(bf16)
        marks = got_ref[j, LB + SLICE :, :].astype(f32)
        fade = jnp.exp(marks[0:1, :] + marks[8:9, :])
        state = fade * state + got_ref[j, LB : LB + SLICE, :].astype(f32)


def attend_kernel(within_ref, heads_ref, state_ref, decay_ref, grad_ref, gain_ref, att_ref, up_ref, sums_ref, scratch):
    _, as_cols, _, _ = run_sums(decay_ref[...])
    grads = split_heads(grad_ref, scratch)
    squares = jnp.zeros((LB, HD), f32)
    crossed = jnp.zeros((LB, HD), f32)
    for h in range(OWN):
        state = state_ref[h * HD : (h + 1) * HD, :]
        fade = SCALE_LIN * jnp.exp(as_cols[:, h : h + 1])
        attended = within_ref[h] + fade * dot(heads_ref[0, h], state, NN)
        upstream = grads[h] * gain_ref[h : h + 1, :]
        att_ref[h] = attended
        up_ref[h] = upstream
        squares = squares + attended * attended
        crossed = crossed + upstream * attended
    ones = jnp.ones((8, HD), f32)
    square_row = dot(ones, squares, NT, PRECISE)
    cross_row = dot(ones, crossed, NT, PRECISE)
    both = [x[0:1, n * HALF : (n + 1) * HALF] for x in (square_row, cross_row) for n in range(2)]
    for j in range(HEADS):
        for n in range(4):
            sums_ref[j, n : n + 1, :] = both[n]


def grad_kernel(att_ref, up_ref, got_ref, heads_ref, decay_ref, gain_ref, out_ref, ag_ref, back_ref, scratch):
    _, as_cols, row, col = run_sums(decay_ref[...])
    total = got_ref[0]
    for j in range(1, HEADS):
        total = total + got_ref[j]
    wide = jnp.concatenate(
        [jnp.concatenate([total[n : n + 1], total[n + 1 : n + 2]], axis=1) for n in (0, 2)]
        + [jnp.zeros((6, LB), f32)],
        axis=0,
    )
    cols = dot((row == col).astype(f32), wide, NT, PRECISE)
    inverse = lax.rsqrt(cols[:, 0:1] / (HEAD_TOTAL * HD) + EPSILON)
    pull = inverse * inverse * inverse * (cols[:, 1:2] / (HEAD_TOTAL * HD))
    outs = []
    for h in range(OWN):
        attended = att_ref[h]
        outs.append(attended * inverse * gain_ref[h : h + 1, :])
        att_grad = (inverse * up_ref[h] - attended * pull).astype(bf16)
        ag_ref[h] = att_grad
        faded = (heads_ref[0, h].astype(f32) * jnp.exp(as_cols[:, h : h + 1])).astype(bf16)
        back = dot(faded, att_grad, TN).astype(bf16)
        back_ref[h * HD : (h + 1) * HD, :] = back
    join_heads(outs, scratch, out_ref)


def inner_kernel(
    heads_ref, ag_ref, state_ref, later_ref, decay_ref, dq_ref, dk_ref, dv_ref, scratch
):
    as_rows, as_cols, row, col = run_sums(decay_ref[...])
    query_grads, key_grads, value_grads = [], [], []
    for h in range(OWN):
        run_row, run_col = as_rows[h : h + 1, :], as_cols[:, h : h + 1]
        query, key, value, grad = heads_ref[0, h], heads_ref[1, h], heads_ref[2, h], ag_ref[h]
        decays = SCALE_LIN * jnp.exp(jnp.where(row >= col, run_col - run_row, FAR_BELOW))
        turned = SCALE_LIN * jnp.exp(jnp.where(col >= row, run_row - run_col, FAR_BELOW))
        grad_weights = (dot(grad, value, NT) * decays).astype(bf16)
        grad_turned = (dot(value, grad, NT) * turned).astype(bf16)
        weights_turned = (dot(key, query, NT) * turned).astype(bf16)
        state = state_ref[h * HD : (h + 1) * HD, :]
        later = later_ref[h * HD : (h + 1) * HD, :]
        fade = SCALE_LIN * jnp.exp(run_col)
        tail = SCALE_LIN * jnp.exp(run_row[:, LB - 1 : LB] - run_col)
        query_grads.append(dot(grad_weights, key, NN) + fade * dot(grad, state, NT))
        key_grads.append(dot(grad_turned, query, NN) + tail * dot(value, later, NT))
        value_grads.append(dot(weights_turned, grad, NN) + tail * dot(key, later, NN))
    join_heads(query_grads, scratch, dq_ref)
    join_heads(key_grads, scratch, dk_ref)
    join_heads(value_grads, scratch, dv_ref)


def soft_limits(reach_ref):
    here = lax.axis_index("ctx")
    base = here * LB
    reach0, reach1 = reach_ref[2 * here] * BLK, reach_ref[2 * here + 1] * BLK
    place = lax.broadcasted_iota(jnp.int32, (1, ROWS), 1) // OWN
    limit = jnp.maximum(base + place + 1, jnp.where(place < BLK, reach0, reach1))
    lowest = jnp.minimum(jnp.maximum(base + 1, reach0), jnp.maximum(base + 1 + BLK, reach1))
    highest = jnp.maximum(jnp.maximum(base + BLK, reach0), jnp.maximum(base + 2 * BLK, reach1))
    return limit, lowest // SPAN, (highest + SPAN - 1) // SPAN


def keys_of(ref, g, part):
    return ref[pl.ds(g * PIECES, PIECES), part * HALF : (part + 1) * HALF, :].reshape(KEYS, HD)


def soft_kernel(
    reach_ref, q_ref, do_ref, mine_ref, other_ref, out_ref, dq_ref, dmine_ref, dother_ref,
    s_ref, p_ref, top_ref, mass_ref, sum_ref, turned_ref, rows_ref,
):
    side = lax.axis_index("head") % 2
    limit, full, used = soft_limits(reach_ref)
    top_ref[...] = jnp.full((8, ROWS), FAR_BELOW, f32)
    mass_ref[...] = jnp.zeros((8, ROWS), f32)
    sum_ref[...] = jnp.zeros((HD, ROWS), f32)

    def find_max(low, high, masked):
        @pl.loop(low, high)
        def _(g):
            for at, ref, half in ((g, mine_ref, side), (PER_SOURCE + g, other_ref, 1 - side)):
                scores = dot(keys_of(ref, g, 0), q_ref[...], NT)
                if masked:
                    index = lax.broadcasted_iota(jnp.int32, (KEYS, 1), 0)
                    where = g * SPAN + half * HALF + (index // HALF) * LB + index % HALF
                    scores = jnp.where(where < limit, scores, FAR_BELOW)
                s_ref[at] = scores
                top_ref[...] = jnp.maximum(
                    top_ref[...], jnp.max(scores.reshape(KEYS // 8, 8, ROWS), axis=0)
                )

    find_max(0, full, False)
    find_max(full, used, True)
    factor = SCALE_SOFT * LOG2E
    shift = jnp.max(top_ref[...], axis=0, keepdims=True) * factor

    @pl.loop(0, used)
    def _(g):
        for at, ref in ((g, mine_ref), (PER_SOURCE + g, other_ref)):
            probs = jnp.exp2(s_ref[at] * factor - shift)
            mass_ref[...] = mass_ref[...] + jnp.sum(probs.reshape(KEYS // 8, 8, ROWS), axis=0)
            probs = probs.astype(bf16)
            p_ref[at] = probs
            sum_ref[...] = sum_ref[...] + dot(keys_of(ref, g, 1), probs, TN)

    inverse = 1.0 / jnp.sum(mass_ref[...], axis=0, keepdims=True)
    out = (sum_ref[...] * inverse).astype(bf16)
    out_ref[...] = out.T
    grads = do_ref[...].astype(f32).T
    adjust = inverse * SCALE_SOFT
    row_dot = jnp.sum(grads * out.astype(f32), axis=0, keepdims=True) * adjust
    turned = (grads * adjust).astype(bf16)
    turned_ref[...] = turned
    rows_ref[...] = turned.T
    sum_ref[...] = jnp.zeros((HD, ROWS), f32)

    @pl.loop(0, used)
    def _(g):
        for at, ref, target in ((g, mine_ref, dmine_ref), (PER_SOURCE + g, other_ref, dother_ref)):
            probs = p_ref[at]
            moved = dot(keys_of(ref, g, 1), turned_ref[...], NN)
            pulls = (probs.astype(f32) * (moved - row_dot)).astype(bf16)
            dk = dot(pulls, q_ref[...], NN)
            dv = dot(probs, rows_ref[...], NN) * (1.0 / SCALE_SOFT)
            target[pl.ds(g * PIECES, PIECES), 0:HALF, :] = dk.astype(bf16).reshape(PIECES, HALF, HD)
            target[pl.ds(g * PIECES, PIECES), HALF:LB, :] = dv.astype(bf16).reshape(PIECES, HALF, HD)
            sum_ref[...] = sum_ref[...] + dot(keys_of(ref, g, 0), pulls, TN)

    dq_ref[...] = sum_ref[...].astype(bf16).T

    @pl.loop(used, PER_SOURCE)
    def _(g):
        zero = jnp.zeros((PIECES, LB, HD), bf16)
        dmine_ref[pl.ds(g * PIECES, PIECES)] = zero
        dother_ref[pl.ds(g * PIECES, PIECES)] = zero


def merge_kernel(mine_ref, got_ref, back_ref, pay_ref):
    for j in range(CTX):
        pay_ref[j, 0:LB, :] = (mine_ref[j].astype(f32) + got_ref[j].astype(f32)).astype(bf16)
        pay_ref[j, LB:, :] = back_ref[j]


def reduce_kernel(got_ref, block_ref, later_ref):
    block = got_ref[0, 0:LB, :].astype(f32)
    for j in range(1, CTX):
        block = block + got_ref[j, 0:LB, :].astype(f32)
    block = block.astype(bf16)
    for z in range(KVH):
        block_ref[z] = block
    for j in range(CTX):
        later_ref[j * SLICE : (j + 1) * SLICE, :] = got_ref[j, LB:, :]


def suffix_kernel(got_ref, first_ref, out_ref):
    state = jnp.zeros((SLICE, HD), f32)
    for j in reversed(range(CTX)):
        out_ref[j] = state.astype(bf16)
        marks = first_ref[j, LB + SLICE :, :].astype(f32)
        fade = jnp.exp(marks[0:1, :] + marks[8:9, :])
        state = fade * state + got_ref[j].astype(f32)


def spread_kernel(mine_ref, other_ref, dk_ref, dv_ref, scratch):
    side = lax.axis_index("head") % 2
    for part, target in ((0, dk_ref), (1, dv_ref)):
        for z in range(KVH):
            rows = slice(part * HALF, (part + 1) * HALF)
            scratch[pl.ds(side * (HALF * KVH) + z, HALF, stride=KVH), :] = mine_ref[z, rows, :].astype(f32)
            scratch[pl.ds((1 - side) * (HALF * KVH) + z, HALF, stride=KVH), :] = other_ref[z, rows, :].astype(f32)
        target[...] = scratch[...].astype(bf16)


def call(kernel, outs, scratch=(), smem=(), hbm=(), hbm_out=(), count=0, flops=0, limit=8):
    spaces = [
        pl.BlockSpec(memory_space=pltpu.SMEM if n in smem else pl.ANY if n in hbm else pltpu.VMEM)
        for n in range(count)
    ]
    return pl.pallas_call(
        kernel,
        out_shape=[jax.ShapeDtypeStruct(shape, kind) for shape, kind in outs],
        in_specs=spaces,
        out_specs=[
            pl.BlockSpec(memory_space=pl.ANY if n in hbm_out else pltpu.VMEM) for n in range(len(outs))
        ],
        scratch_shapes=[x if not isinstance(x, tuple) else pltpu.VMEM(*x) for x in scratch],
        compiler_params=pltpu.CompilerParams(vmem_limit_bytes=limit * 1024 * 1024),
        cost_estimate=pl.CostEstimate(flops=flops, bytes_accessed=1 << 20, transcendentals=0),
    )


def after(value, *earlier):
    return lax.optimization_barrier((value,) + earlier)[0]


WIDE = ((ROWS, HD), f32)
FLAT = ((ROWS, HD), bf16)
BY_HEAD = ((OWN, LB, HD), f32)
PROBS = ((GROUPS, KEYS, ROWS), bf16)
KEY_PARTS = ((CTX, LB, HD), bf16)
OTHER_CORE = [(i, i ^ 1) for i in range(HEADS)]
SAME_CORE = [[2 * z + c for z in range(KVH)] for c in range(2)]


def per_device(lin_q, lin_k, lin_v, decay, lin_gain, lin_grad, soft_q, soft_k, soft_v, soft_grad, reach):
    flat = lambda x: x.reshape(-1, HD)
    lin_q, lin_k, lin_v, lin_grad, soft_q, soft_grad, soft_k, soft_v = map(
        flat, (lin_q, lin_k, lin_v, lin_grad, soft_q, soft_grad, soft_k, soft_v)
    )
    pay, within, heads = call(
        local_kernel,
        [((CTX, LB + SLICE + 16, HD), bf16), BY_HEAD, ((3, OWN, LB, HD), bf16)],
        [
            WIDE,
            ((3, ROWS, HD), bf16),
            ((2, HALF * KVH, HD), bf16),
            ((OWN, LB), f32),
            ((LB, HD), bf16),
            ((CTX, SLICE + 16, HD), bf16),
            BY_HEAD,
            ((3, OWN, LB, HD), bf16),
            pltpu.SemaphoreType.DMA((6,)),
            pltpu.SemaphoreType.DMA((CTX + 3,)),
        ],
        hbm=(0, 1, 2, 3, 4, 5),
        hbm_out=(0, 1, 2),
        count=6,
        flops=10**9,
        limit=60,
    )(lin_q, lin_k, lin_v, decay, soft_k, soft_v)
    mine = lax.all_to_all(pay, "ctx", 0, 0)
    other = lax.ppermute(mine, "head", OTHER_CORE)
    (prefixes,) = call(prefix_kernel, [((CTX, SLICE, HD), bf16)], count=1, flops=10**8)(mine)
    state = lax.all_to_all(prefixes, "ctx", 0, 0).reshape(OWN * HD, HD)
    attended, upstream, sums = call(
        attend_kernel,
        [BY_HEAD, BY_HEAD, ((HEADS, 4, HALF), f32)],
        [WIDE],
        count=6,
        flops=10**9,
    )(within, heads, state, decay, lin_grad, lin_gain)
    total = lax.all_to_all(sums, "head", 0, 0)
    lin_out, att_grad, back = call(
        grad_kernel,
        [FLAT, ((OWN, LB, HD), bf16), ((OWN * HD, HD), bf16)],
        [WIDE],
        count=6,
        flops=10**9,
    )(attended, upstream, total, heads, decay, lin_gain)
    backs = lax.all_to_all(back.reshape(CTX, SLICE, HD), "ctx", 0, 0)
    (suffixes,) = call(suffix_kernel, [((CTX, SLICE, HD), bf16)], count=2, flops=10**8)(backs, mine)
    soft_out, soft_dq, dmine, dother = call(
        soft_kernel,
        [FLAT, FLAT, KEY_PARTS, KEY_PARTS],
        [
            ((GROUPS, KEYS, ROWS), f32),
            PROBS,
            ((8, ROWS), f32),
            ((8, ROWS), f32),
            ((HD, ROWS), f32),
            ((HD, ROWS), bf16),
            FLAT,
        ],
        smem=(0,),
        count=5,
        flops=10**10,
        limit=36,
    )(reach, after(soft_q, suffixes), soft_grad, mine, other)
    dgot = lax.ppermute(dother, "head", OTHER_CORE)
    (pay_back,) = call(merge_kernel, [((CTX, LB + SLICE, HD), bf16)], count=3, flops=10**8)(
        dmine, dgot, suffixes
    )
    got_back = lax.all_to_all(pay_back, "ctx", 0, 0)
    blocks, later = call(
        reduce_kernel, [((KVH, LB, HD), bf16), ((OWN * HD, HD), bf16)], count=1, flops=10**8
    )(got_back)
    spread = lax.all_to_all(blocks, "head", 0, 0, axis_index_groups=SAME_CORE)
    lin_dq, lin_dk, lin_dv = call(inner_kernel, [FLAT, FLAT, FLAT], [WIDE], count=5, flops=4 * 10**9)(
        heads, att_grad, state, later, decay
    )
    spread = after(spread, lin_dk)
    spread_other = lax.ppermute(spread, "head", OTHER_CORE)
    soft_dk, soft_dv = call(
        spread_kernel,
        [((LB * KVH, HD), bf16), ((LB * KVH, HD), bf16)],
        [((LB * KVH, HD), f32)],
        count=2,
        flops=10**8,
    )(spread, spread_other)
    deep = lambda x: x.reshape(LB, OWN, HD)
    return (
        deep(lin_out),
        deep(lin_dq),
        deep(lin_dk),
        deep(lin_dv),
        deep(soft_out),
        deep(soft_dq),
        soft_dk.reshape(LB, KVH, HD),
        soft_dv.reshape(LB, KVH, HD),
    )


def solution(mesh):
    long, short = P("ctx", "head", None), P("ctx", None, None)
    return jax.shard_map(
        per_device,
        mesh=mesh,
        in_specs=(long, long, long, P("head", "ctx"), P("head", None), long, long, short, short, long, P()),
        out_specs=(long, long, long, long, long, long, short, short),
        check_vma=False,
    )
```

time: 160 us -> 141 us (0.88)
  local copies, waits for them, and re-layouts: 8.64 us -> 0.03 us
  waiting for transfers between devices: 25.1 us -> 17.1 us
  starting transfers between devices: 12.5 us -> 10.1 us
  blocking collectives: 92.8 us -> 94.5 us
    all_to_all x3 -> x4, blocking collectives: 62.7 us -> 84.5 us  [the longest x1 31.9 us: per_device(): got_back = lax.all_to_all(pay_back, 'ctx', 0, 0)]
    all_to_all x1, blocking collectives: 30.1 us -> 10 us  [per_device(): state = lax.all_to_all(prefixes, 'ctx', 0, 0).reshape(OWN * HD, HD)]
    all_to_all x2 -> x1, waiting for transfers between devices: 23.1 us -> 13.2 us  [per_device(): spread = lax.all_to_all(blocks, 'head', 0, 0, axis_index_groups=SAME_CORE)]
    unnamed x24 -> x16, local copies, waits for them, and re-layouts: 5.57 us -> 0.03 us
    all_to_all x2 -> x1, starting transfers between devices: 7.63 us -> 3.67 us  [per_device(): spread = lax.all_to_all(blocks, 'head', 0, 0, axis_index_groups=SAME_CORE)]
    pallas_call x6, Pallas kernels: 13.2 us -> 10.8 us  [the longest x1 5.96 us: per_device(): call(soft_kernel, [FLAT, FLAT, KEY_PARTS, KEY_PARTS], [((GROUPS, KEYS, RO...]
    ppermute x1, waiting for transfers between devices: 0.01 us -> 2.29 us  [per_device(): dgot = lax.ppermute(dother, 'head', OTHER_CORE)]
    pallas_call x1, Pallas kernels: 1.81 us -> 4.02 us  [per_device(): call(local_kernel, [((CTX, LB + SLICE + 16, HD), bf16), BY_HEAD, ((3, OWN...]
  transfers between devices with their start and end apart: 5 -> 4, of which waited for: 3 -> 3; matrix products, arithmetic and copies ran while one was open for 0% -> 0% of each run, Pallas kernels for 4% -> 4%
where the time goes in v2:
time: 141 us
  blocking collectives  94.5 us (67%)
  Pallas kernels  18.3 us (13%)
  waiting for transfers between devices  17.1 us (12%)
  starting transfers between devices  10.1 us (7%)
    all_to_all x1, blocking collectives, per_device(): got_back = lax.all_to_all(pay_back, 'ctx', 0, 0)  31.9 us
    all_to_all x1, blocking collectives, per_device(): mine = lax.all_to_all(pay, 'ctx', 0, 0)  25.5 us
    all_to_all x1, blocking collectives, per_device(): total = lax.all_to_all(sums, 'head', 0, 0)  17.2 us
    all_to_all x1, waiting for transfers between devices, per_device(): spread = lax.all_to_all(blocks, 'head', 0, 0, axis_index_groups=SAME_CORE)  13.2 us
    all_to_all x1, blocking collectives, per_device(): state = lax.all_to_all(prefixes, 'ctx', 0, 0).reshape(OWN * HD, HD)  10 us
    all_to_all x1, blocking collectives, per_device(): backs = lax.all_to_all(back.reshape(CTX, SLICE, HD), 'ctx', 0, 0)  9.93 us
    pallas_call x1, Pallas kernels, per_device(): call(soft_kernel, [FLAT, FLAT, KEY_PARTS, KEY_PARTS], [((GROUPS, KEYS, RO...  5.96 us
    pallas_call x1, Pallas kernels, per_device(): call(local_kernel, [((CTX, LB + SLICE + 16, HD), bf16), BY_HEAD, ((3, OWN...  4.02 us
  transfers between devices with their start and end apart: 4, of which 3 were waited for; matrix products, arithmetic and copies ran while one was open for 0% of the time, Pallas kernels for 4%

profile of v2, /device:TPU:1, one launch (start us, length us, event | category | flops | bytes accessed | tf_op | source)
XLA Modules:
  0.0 140.8 jit_solution(15498662914833547361)
XLA Ops:
  0.6 4.0 %shard_map.170 = (bf16[16,304,128]{2,1,0:T(8,128)(2,1)}, f32[4,256,128]{2,1,0:T(8,128)}, bf16[3,4,256,128]{3,2,1,0:T(8,128)(2,1)}) custom-call(bf16[1024,128]{1,0:T(8,128)(2,1)} %bitcast.28, bf16[1024,128]{1,0:T(8,128)(2,1)} %bitcast.29, bf16[1024,128]{1,0:T(8,128)(2,1)} %bitcast.30, f32[4,256]{1,0:T(4,128)} %decay_ref.5, bf16[2048,128]{1,0:T(8,128)(2,1)} %bitcast.24, ...), custom_call_target="tpu_custom_call" | custom-call | flops 1000000000 | bytes 1048576 | tf_op jit(solution)/shard_map/pallas_call | solution.py:371
  4.7 25.5 %all_to_all.30.got_ref.first_ref.mine_ref = bf16[16,304,128]{2,1,0:T(8,128)(2,1)S(1)} all-to-all(bf16[16,304,128]{2,1,0:T(8,128)(2,1)} %get-tuple-element.32), channel_id=1, replica_groups=mesh['ctx'=16,'head'=16] {'ctx'}, dimensions={0} | all-to-all | bytes 2490368 | tf_op jit(solution)/shard_map/all_to_all | solution.py:392
  30.1 0.0 copy-start
  30.1 0.0 copy-start.3
  30.1 0.0 copy-start.4
  30.1 0.0 copy-start.6
  30.1 0.0 copy-start.7
  30.1 2.2 %collective-permute-start = (bf16[16,304,128]{2,1,0:T(8,128)(2,1)S(1)}, bf16[16,304,128]{2,1,0:T(8,128)(2,1)S(1)}, u32[]{:S(2)}, u32[]{:S(2)}) collective-permute-start(bf16[16,304,128]{2,1,0:T(8,128)(2,1)S(1)} %all_to_all.30.got_ref.first_ref.mine_ref), channel_id=1, source_target_pairs={{0,1},{1,0},{2,3},{3,2},{4,5},{5,4},{6,7},{7,6},{8,9},{9,8},{10,11... | collective-permute-start | bytes 3735560 | tf_op jit(solution)/shard_map/ppermute | solution.py:393
  32.4 10.0 %all_to_all.31 = bf16[16,32,128]{2,1,0:T(8,128)(2,1)S(1)} all-to-all(bf16[16,32,128]{2,1,0:T(8,128)(2,1)S(1)} %shard_map.171), channel_id=1, replica_groups=mesh['ctx'=16,'head'=16] {'ctx'}, dimensions={0} | all-to-all | bytes 262144 | tf_op jit(solution)/shard_map/all_to_all | solution.py:395
  42.4 0.0 copy-done
  42.4 0.0 copy-done.3
  42.4 0.0 copy-done.4
  42.4 0.0 copy-done.6
  42.5 0.0 copy-done.7
  42.5 1.2 shard_map.172
  43.7 17.2 %all_to_all.32.got_ref = f32[16,4,128]{2,1,0:T(4,128)S(1)} all-to-all(f32[16,4,128]{2,1,0:T(4,128)S(1)} %get-tuple-element.35), channel_id=1, replica_groups=mesh['ctx'=16,'head'=16] {'head'}, dimensions={0} | all-to-all | bytes 65536 | tf_op jit(solution)/shard_map/all_to_all | solution.py:403
  60.9 1.8 %shard_map.173 = (bf16[1024,128]{1,0:T(8,128)(2,1)}, bf16[4,256,128]{2,1,0:T(8,128)(2,1)S(1)}, bf16[512,128]{1,0:T(8,128)(2,1)S(1)}) custom-call(f32[4,256,128]{2,1,0:T(8,128)S(1)} %get-tuple-element.33.att_ref, f32[4,256,128]{2,1,0:T(8,128)S(1)} %get-tuple-element.34.up_ref, f32[16,4,128]{2,1,0:T(4,128)S(1)} %all_to_all.32.got_ref, ...), custom_call_target="tpu_custom_call" | custom-call | flops 1000000000 | bytes 1048576 | tf_op jit(solution)/shard_map/pallas_call | solution.py:404
  62.7 0.0 copy-start.1
  62.7 0.0 copy-start.2
  62.7 0.0 copy-start.5
  62.7 9.9 %all_to_all.33.got_ref = bf16[16,32,128]{2,1,0:T(8,128)(2,1)S(1)} all-to-all(bf16[16,32,128]{2,1,0:T(8,128)(2,1)S(1)} %bitcast.20), channel_id=1, replica_groups=mesh['ctx'=16,'head'=16] {'ctx'}, dimensions={0} | all-to-all | bytes 262144 | tf_op jit(solution)/shard_map/all_to_all | solution.py:411
  72.7 0.0 collective-permute-done.other_ref
  72.7 0.0 copy-done.1
  72.7 0.0 copy-done.2
  72.7 0.0 copy-done.5
  72.7 6.0 %shard_map.175 = (bf16[1024,128]{1,0:T(8,128)(2,1)}, bf16[1024,128]{1,0:T(8,128)(2,1)}, bf16[16,256,128]{2,1,0:T(8,128)(2,1)S(1)}, bf16[16,256,128]{2,1,0:T(8,128)(2,1)S(1)}) custom-call(s32[32]{0:T(128)S(1)} %copy-done.5, bf16[1024,128]{1,0:T(8,128)(2,1)S(1)} %bitcast.22, bf16[1024,128]{1,0:T(8,128)(2,1)S(1)} %bitcast.23, ...), custom_call_target="tpu_custom_call" | custom-call | flops 10000000000 | bytes 1048576 | tf_op jit(solution)/shard_map/pallas_call | solution.py:413
  78.7 1.8 %collective-permute-start.1 = (bf16[16,256,128]{2,1,0:T(8,128)(2,1)S(1)}, bf16[16,256,128]{2,1,0:T(8,128)(2,1)S(1)}, u32[]{:S(2)}, u32[]{:S(2)}) collective-permute-start(bf16[16,256,128]{2,1,0:T(8,128)(2,1)S(1)} %get-tuple-element.41), channel_id=1, source_target_pairs={{0,1},{1,0},{2,3},{3,2},{4,5},{5,4},{6,7},{7,6},{8,9},{9,8},{10,11... | collective-permute-start | bytes 3145736 | tf_op jit(solution)/shard_map/ppermute | solution.py:430
  80.5 2.3 %collective-permute-done.1.got_ref = bf16[16,256,128]{2,1,0:T(8,128)(2,1)S(1)} collective-permute-done((bf16[16,256,128]{2,1,0:T(8,128)(2,1)S(1)}, bf16[16,256,128]{2,1,0:T(8,128)(2,1)S(1)}, u32[]{:S(2)}, u32[]{:S(2)}) %collective-permute-start.1) | collective-permute-done | bytes 1048608 | tf_op jit(solution)/shard_map/ppermute | solution.py:430
  82.8 0.2 shard_map.176
  83.0 31.9 %all_to_all.34.got_ref = bf16[16,288,128]{2,1,0:T(8,128)(2,1)S(1)} all-to-all(bf16[16,288,128]{2,1,0:T(8,128)(2,1)S(1)} %shard_map.176), channel_id=1, replica_groups=mesh['ctx'=16,'head'=16] {'ctx'}, dimensions={0} | all-to-all | bytes 2359296 | tf_op jit(solution)/shard_map/all_to_all | solution.py:434
  114.9 0.9 shard_map.177
  115.9 3.7 %all-to-all-start.5 = ((bf16[8,256,128]{2,1,0:T(8,128)(2,1)}), bf16[8,256,128]{2,1,0:T(8,128)(2,1)S(1)}, u32[]{:S(2)}, u32[]{:S(2)}) async-start(bf16[8,256,128]{2,1,0:T(8,128)(2,1)} %get-tuple-element.48), calls=%async_computation.5 | async-start | bytes 1048576 | tf_op jit(solution)/shard_map/all_to_all | solution.py:438
  119.5 2.5 %shard_map.178 = (bf16[1024,128]{1,0:T(8,128)(2,1)}, bf16[1024,128]{1,0:T(8,128)(2,1)}, bf16[1024,128]{1,0:T(8,128)(2,1)}) custom-call(bf16[3,4,256,128]{3,2,1,0:T(8,128)(2,1)S(1)} %copy-done.6, bf16[4,256,128]{2,1,0:T(8,128)(2,1)S(1)} %get-tuple-element.37.ag_ref, bf16[512,128]{1,0:T(8,128)(2,1)S(1)} %bitcast.19, ...), custom_call_target="tpu_custom_call" | custom-call | flops 4000000000 | bytes 1048576 | tf_op jit(solution)/shard_map/pallas_call | solution.py:439
  122.1 13.2 %all-to-all-done.5.mine_ref = bf16[8,256,128]{2,1,0:T(8,128)(2,1)S(1)} async-done(((bf16[8,256,128]{2,1,0:T(8,128)(2,1)}), bf16[8,256,128]{2,1,0:T(8,128)(2,1)S(1)}, u32[]{:S(2)}, u32[]{:S(2)}) %all-to-all-start.5) | async-done | bytes 524320 | tf_op jit(solution)/shard_map/all_to_all | solution.py:438
  135.3 2.4 %collective-permute-start.2 = (bf16[8,256,128]{2,1,0:T(8,128)(2,1)S(1)}, bf16[8,256,128]{2,1,0:T(8,128)(2,1)S(1)}, u32[]{:S(2)}, u32[]{:S(2)}) collective-permute-start(bf16[8,256,128]{2,1,0:T(8,128)(2,1)S(1)} %all-to-all-done.5.mine_ref), channel_id=1, source_target_pairs={{0,1},{1,0},{2,3},{3,2},{4,5},{5,4},{6,7},{7,6},{8,9},{9,8},{10,11... | collective-permute-start | bytes 1572872 | tf_op jit(solution)/shard_map/ppermute | solution.py:443
  137.7 1.5 %collective-permute-done.2.other_ref = bf16[8,256,128]{2,1,0:T(8,128)(2,1)S(1)} collective-permute-done((bf16[8,256,128]{2,1,0:T(8,128)(2,1)S(1)}, bf16[8,256,128]{2,1,0:T(8,128)(2,1)S(1)}, u32[]{:S(2)}, u32[]{:S(2)}) %collective-permute-start.2) | collective-permute-done | bytes 524320 | tf_op jit(solution)/shard_map/ppermute | solution.py:443
  139.3 1.5 %shard_map.179 = (bf16[2048,128]{1,0:T(8,128)(2,1)}, bf16[2048,128]{1,0:T(8,128)(2,1)}) custom-call(bf16[8,256,128]{2,1,0:T(8,128)(2,1)S(1)} %all-to-all-done.5.mine_ref, bf16[8,256,128]{2,1,0:T(8,128)(2,1)S(1)} %collective-permute-done.2.other_ref), custom_call_target="tpu_custom_call" | custom-call | flops 100000000 | bytes 1048576 | tf_op jit(solution)/shard_map/pallas_call | solution.py:444
  (2 shorter events, 0.1 us)
Async XLA Ops:
  30.1 12.3 %copy-start = (bf16[256,4,128]{2,1,0:T(4,128)(2,1)S(1)}, bf16[256,4,128]{2,1,0:T(4,128)(2,1)}, u32[]{:S(2)}) copy-start(bf16[256,4,128]{2,1,0:T(4,128)(2,1)} %param.16) | copy-start | bytes 786436
  30.1 12.3 %copy-start.3 = (f32[4,256]{1,0:T(4,128)S(1)}, f32[4,256]{1,0:T(4,128)}, u32[]{:S(2)}) copy-start(f32[4,256]{1,0:T(4,128)} %decay_ref.5) | copy-start | bytes 12292
  30.1 12.3 %copy-start.4 = (f32[4,128]{1,0:T(4,128)S(1)}, f32[4,128]{1,0:T(4,128)}, u32[]{:S(2)}) copy-start(f32[4,128]{1,0:T(4,128)} %gain_ref.3) | copy-start | bytes 6148
  30.1 12.3 %copy-start.6 = (bf16[3,4,256,128]{3,2,1,0:T(8,128)(2,1)S(1)}, bf16[3,4,256,128]{3,2,1,0:T(8,128)(2,1)}, u32[]{:S(2)}) copy-start(bf16[3,4,256,128]{3,2,1,0:T(8,128)(2,1)} %get-tuple-element.31.heads_ref) | copy-start | bytes 2359300
  30.1 12.3 %copy-start.7 = (f32[4,256,128]{2,1,0:T(8,128)S(1)}, f32[4,256,128]{2,1,0:T(8,128)}, u32[]{:S(2)}) copy-start(f32[4,256,128]{2,1,0:T(8,128)} %get-tuple-element.30.within_ref) | copy-start | bytes 1572868
  30.1 42.5 %collective-permute-start = (bf16[16,304,128]{2,1,0:T(8,128)(2,1)S(1)}, bf16[16,304,128]{2,1,0:T(8,128)(2,1)S(1)}, u32[]{:S(2)}, u32[]{:S(2)}) collective-permute-start(bf16[16,304,128]{2,1,0:T(8,128)(2,1)S(1)} %all_to_all.30.got_ref.first_ref.mine_ref), channel_id=1, source_target_pairs={{0,1},{1,0},{2,3},{3,2},{4,5},{5,4},{6,7},{7,6},{8,9},{9,8},{10,11... | collective-permute-start | bytes 3735560 | tf_op jit(solution)/shard_map/ppermute | solution.py:393
  62.7 10.0 %copy-start.1 = (bf16[256,4,128]{2,1,0:T(4,128)(2,1)S(1)}, bf16[256,4,128]{2,1,0:T(4,128)(2,1)}, u32[]{:S(2)}) copy-start(bf16[256,4,128]{2,1,0:T(4,128)(2,1)} %param.17) | copy-start | bytes 786436
  62.7 10.0 %copy-start.2 = (bf16[256,4,128]{2,1,0:T(4,128)(2,1)S(1)}, bf16[256,4,128]{2,1,0:T(4,128)(2,1)}, u32[]{:S(2)}) copy-start(bf16[256,4,128]{2,1,0:T(4,128)(2,1)} %param.20) | copy-start | bytes 786436
  62.7 10.0 %copy-start.5 = (s32[32]{0:T(128)S(1)}, s32[32]{0:T(128)}, u32[]{:S(2)}) copy-start(s32[32]{0:T(128)} %reach_ref.1) | copy-start | bytes 388
  78.7 4.1 %collective-permute-start.1 = (bf16[16,256,128]{2,1,0:T(8,128)(2,1)S(1)}, bf16[16,256,128]{2,1,0:T(8,128)(2,1)S(1)}, u32[]{:S(2)}, u32[]{:S(2)}) collective-permute-start(bf16[16,256,128]{2,1,0:T(8,128)(2,1)S(1)} %get-tuple-element.41), channel_id=1, source_target_pairs={{0,1},{1,0},{2,3},{3,2},{4,5},{5,4},{6,7},{7,6},{8,9},{9,8},{10,11... | collective-permute-start | bytes 3145736 | tf_op jit(solution)/shard_map/ppermute | solution.py:430
  115.9 19.5 %all-to-all-start.5 = ((bf16[8,256,128]{2,1,0:T(8,128)(2,1)}), bf16[8,256,128]{2,1,0:T(8,128)(2,1)S(1)}, u32[]{:S(2)}, u32[]{:S(2)}) async-start(bf16[8,256,128]{2,1,0:T(8,128)(2,1)} %get-tuple-element.48), calls=%async_computation.5 | async-start | bytes 1048576 | tf_op jit(solution)/shard_map/all_to_all | solution.py:438
  135.3 3.9 %collective-permute-start.2 = (bf16[8,256,128]{2,1,0:T(8,128)(2,1)S(1)}, bf16[8,256,128]{2,1,0:T(8,128)(2,1)S(1)}, u32[]{:S(2)}, u32[]{:S(2)}) collective-permute-start(bf16[8,256,128]{2,1,0:T(8,128)(2,1)S(1)} %all-to-all-done.5.mine_ref), channel_id=1, source_target_pairs={{0,1},{1,0},{2,3},{3,2},{4,5},{5,4},{6,7},{7,6},{8,9},{9,8},{10,11... | collective-permute-start | bytes 1572872 | tf_op jit(solution)/shard_map/ppermute | solution.py:443

commit v3 on v2

--- a/solution.py
+++ b/solution.py
@@ -65,8 +65,8 @@
 
 
 def local_kernel(
-    q_hbm, k_hbm, v_hbm, decay_hbm, sk_hbm, sv_hbm, pay_hbm, within_hbm, heads_hbm,
-    scratch, raw, halves, decay_ref, kv_ref, own_ref, within_ref, heads_ref, sems, out_sems,
+    q_hbm, k_hbm, v_hbm, decay_hbm, sk_hbm, sv_hbm, sq_hbm, sg_hbm, pay_hbm, within_hbm, heads_hbm, trade_hbm,
+    scratch, raw, halves, decay_ref, kv_ref, own_ref, within_ref, heads_ref, trade_ref, sems, out_sems,
 ):
     side = lax.axis_index("head") % 2
     kv = lax.axis_index("head") // 2
@@ -78,6 +78,11 @@
         pltpu.make_async_copy(v_hbm, raw.at[2], sems.at[3]),
         pltpu.make_async_copy(q_hbm, raw.at[0], sems.at[4]),
         pltpu.make_async_copy(decay_hbm, decay_ref, sems.at[5]),
+    ] + [
+        pltpu.make_async_copy(
+            x.at[pl.ds(ROWS // 2, ROWS // 2)], trade_ref.at[pl.ds(n * (ROWS // 2), ROWS // 2)], sems.at[6 + n]
+        )
+        for n, x in enumerate((sq_hbm, sg_hbm))
     ]
     for copy in copies:
         copy.start()
@@ -90,6 +95,10 @@
     ]
     for copy in sent:
         copy.start()
+    for copy in copies[6:]:
+        copy.wait()
+    traded = pltpu.make_async_copy(trade_ref, trade_hbm, out_sems.at[CTX + 3])
+    traded.start()
     copies[5].wait()
     as_rows, as_cols, row, col = run_sums(decay_ref[...])
     copies[2].wait()
@@ -125,7 +134,7 @@
         within_ref[h] = dot(weights, values[h], NN)
     inner = pltpu.make_async_copy(within_ref, within_hbm, out_sems.at[CTX + 2])
     inner.start()
-    for copy in sent + [states, kept, inner]:
+    for copy in sent + [traded, states, kept, inner]:
         copy.wait()
 
 
@@ -187,8 +196,12 @@
 
 
 def inner_kernel(
-    heads_ref, ag_ref, state_ref, later_ref, decay_ref, dq_ref, dk_ref, dv_ref, scratch
+    heads_ref, ag_ref, state_ref, later_ref, decay_ref, out_ref, sdq_ref, traded_ref,
+    dq_ref, dk_ref, dv_ref, soft_out_ref, soft_dq_ref, scratch,
 ):
+    for n, (own, target) in enumerate(((out_ref, soft_out_ref), (sdq_ref, soft_dq_ref))):
+        target[0 : ROWS // 2] = own[...]
+        target[ROWS // 2 :] = traded_ref[n * (ROWS // 2) : (n + 1) * (ROWS // 2)]
     as_rows, as_cols, row, col = run_sums(decay_ref[...])
     query_grads, key_grads, value_grads = [], [], []
     for h in range(OWN):
@@ -211,85 +224,112 @@
     join_heads(value_grads, scratch, dv_ref)
 
 
-def soft_limits(reach_ref):
-    here = lax.axis_index("ctx")
-    base = here * LB
-    reach0, reach1 = reach_ref[2 * here] * BLK, reach_ref[2 * here + 1] * BLK
-    place = lax.broadcasted_iota(jnp.int32, (1, ROWS), 1) // OWN
-    limit = jnp.maximum(base + place + 1, jnp.where(place < BLK, reach0, reach1))
-    lowest = jnp.minimum(jnp.maximum(base + 1, reach0), jnp.maximum(base + 1 + BLK, reach1))
-    highest = jnp.maximum(jnp.maximum(base + BLK, reach0), jnp.maximum(base + 2 * BLK, reach1))
-    return limit, lowest // SPAN, (highest + SPAN - 1) // SPAN
-
-
 def keys_of(ref, g, part):
     return ref[pl.ds(g * PIECES, PIECES), part * HALF : (part + 1) * HALF, :].reshape(KEYS, HD)
 
 
 def soft_kernel(
-    reach_ref, q_ref, do_ref, mine_ref, other_ref, out_ref, dq_ref, dmine_ref, dother_ref,
-    s_ref, p_ref, top_ref, mass_ref, sum_ref, turned_ref, rows_ref,
+    reach_ref, q_ref, do_ref, trade_ref, mine_ref, other_ref, out_ref, dq_ref, back_ref, dmine_ref, dother_ref,
+    rows_ref, s_ref, p_ref, top_ref, mass_ref, sum_ref, turned_ref, grad_ref, row_ref,
 ):
+    here = lax.axis_index("ctx")
     side = lax.axis_index("head") % 2
-    limit, full, used = soft_limits(reach_ref)
+    blocks = (2 * here, 2 * CTX - 1 - 2 * here)
+    bases = [block * BLK for block in blocks]
+    reaches = [reach_ref[block] * BLK for block in blocks]
+    lowest = [jnp.maximum(base + 1, reach) // SPAN for base, reach in zip(bases, reaches)]
+    used = [(jnp.maximum(base + BLK, reach) + SPAN - 1) // SPAN for base, reach in zip(bases, reaches)]
+    common, most = jnp.minimum(used[0], used[1]), jnp.maximum(used[0], used[1])
+    larger = (used[1] > used[0]).astype(jnp.int32)
+    whole = pl.ds(0, ROWS)
+    part = pl.ds(pl.multiple_of(larger * (ROWS // 2), ROWS // 2), ROWS // 2)
+    full_both = jnp.minimum(jnp.minimum(lowest[0], lowest[1]), common)
+    full_part = jnp.clip(jnp.where(larger == 1, lowest[1], lowest[0]), common, most)
+
+    rows_ref[0 : ROWS // 2] = q_ref[0 : ROWS // 2]
+    rows_ref[ROWS // 2 :] = trade_ref[0 : ROWS // 2]
+    lane = lax.broadcasted_iota(jnp.int32, (8, ROWS), 1)
+    second = lane >= ROWS // 2
+    place = jnp.where(second, lane - ROWS // 2, lane) // OWN
+    row_ref[...] = jnp.maximum(
+        jnp.where(second, bases[1], bases[0]) + place + 1, jnp.where(second, reaches[1], reaches[0])
+    ).astype(f32)
     top_ref[...] = jnp.full((8, ROWS), FAR_BELOW, f32)
     mass_ref[...] = jnp.zeros((8, ROWS), f32)
     sum_ref[...] = jnp.zeros((HD, ROWS), f32)
 
-    def find_max(low, high, masked):
-        @pl.loop(low, high)
-        def _(g):
-            for at, ref, half in ((g, mine_ref, side), (PER_SOURCE + g, other_ref, 1 - side)):
-                scores = dot(keys_of(ref, g, 0), q_ref[...], NT)
-                if masked:
-                    index = lax.broadcasted_iota(jnp.int32, (KEYS, 1), 0)
-                    where = g * SPAN + half * HALF + (index // HALF) * LB + index % HALF
-                    scores = jnp.where(where < limit, scores, FAR_BELOW)
-                s_ref[at] = scores
-                top_ref[...] = jnp.maximum(
-                    top_ref[...], jnp.max(scores.reshape(KEYS // 8, 8, ROWS), axis=0)
-                )
-
-    find_max(0, full, False)
-    find_max(full, used, True)
+    def over_keys(step):
+        def run(low, high, cols, width, masked):
+            @pl.loop(low, high)
+            def _(g):
+                step(g, g, mine_ref, dmine_ref, side, cols, width, masked)
+                step(g, PER_SOURCE + g, other_ref, dother_ref, 1 - side, cols, width, masked)
+
+        return run
+
+    def find_max(g, at, ref, _, half, cols, width, masked):
+        scores = dot(keys_of(ref, g, 0), rows_ref[cols, :], NT)
+        if masked:
+            index = lax.broadcasted_iota(jnp.int32, (KEYS, 1), 0)
+            where = g * SPAN + half * HALF + (index // HALF) * LB + index % HALF
+            scores = jnp.where(where.astype(f32) < row_ref[0:1, cols], scores, FAR_BELOW)
+        s_ref[at, :, cols] = scores
+        top_ref[:, cols] = jnp.maximum(top_ref[:, cols], jnp.max(scores.reshape(KEYS // 8, 8, width), axis=0))
+
+    run = over_keys(find_max)
+    run(0, full_both, whole, ROWS, False)
+    run(full_both, common, whole, ROWS, True)
+    run(common, full_part, part, ROWS // 2, False)
+    run(full_part, most, part, ROWS // 2, True)
     factor = SCALE_SOFT * LOG2E
-    shift = jnp.max(top_ref[...], axis=0, keepdims=True) * factor
-
-    @pl.loop(0, used)
-    def _(g):
-        for at, ref in ((g, mine_ref), (PER_SOURCE + g, other_ref)):
-            probs = jnp.exp2(s_ref[at] * factor - shift)
-            mass_ref[...] = mass_ref[...] + jnp.sum(probs.reshape(KEYS // 8, 8, ROWS), axis=0)
-            probs = probs.astype(bf16)
-            p_ref[at] = probs
-            sum_ref[...] = sum_ref[...] + dot(keys_of(ref, g, 1), probs, TN)
+    row_ref[...] = jnp.broadcast_to(jnp.max(top_ref[...], axis=0, keepdims=True) * factor, (8, ROWS))
+
+    def weigh(g, at, ref, _, half, cols, width, masked):
+        probs = jnp.exp2(s_ref[at, :, cols] * factor - row_ref[0:1, cols])
+        mass_ref[:, cols] = mass_ref[:, cols] + jnp.sum(probs.reshape(KEYS // 8, 8, width), axis=0)
+        probs = probs.astype(bf16)
+        p_ref[at, :, cols] = probs
+        sum_ref[:, cols] = sum_ref[:, cols] + dot(keys_of(ref, g, 1), probs, TN)
+
+    run = over_keys(weigh)
+    run(0, common, whole, ROWS, False)
+    run(common, most, part, ROWS // 2, False)
 
     inverse = 1.0 / jnp.sum(mass_ref[...], axis=0, keepdims=True)
     out = (sum_ref[...] * inverse).astype(bf16)
-    out_ref[...] = out.T
-    grads = do_ref[...].astype(f32).T
+    out_rows = out.T
+    out_ref[...] = out_rows[0 : ROWS // 2]
+    back_ref[0 : ROWS // 2] = out_rows[ROWS // 2 :]
+    grads = jnp.concatenate(
+        [do_ref[0 : ROWS // 2].astype(f32).T, trade_ref[ROWS // 2 :].astype(f32).T], axis=1
+    )
     adjust = inverse * SCALE_SOFT
-    row_dot = jnp.sum(grads * out.astype(f32), axis=0, keepdims=True) * adjust
+    row_ref[...] = jnp.broadcast_to(
+        jnp.sum(grads * out.astype(f32), axis=0, keepdims=True) * adjust, (8, ROWS)
+    )
     turned = (grads * adjust).astype(bf16)
     turned_ref[...] = turned
-    rows_ref[...] = turned.T
+    grad_ref[...] = turned.T
     sum_ref[...] = jnp.zeros((HD, ROWS), f32)
 
-    @pl.loop(0, used)
-    def _(g):
-        for at, ref, target in ((g, mine_ref, dmine_ref), (PER_SOURCE + g, other_ref, dother_ref)):
-            probs = p_ref[at]
-            moved = dot(keys_of(ref, g, 1), turned_ref[...], NN)
-            pulls = (probs.astype(f32) * (moved - row_dot)).astype(bf16)
-            dk = dot(pulls, q_ref[...], NN)
-            dv = dot(probs, rows_ref[...], NN) * (1.0 / SCALE_SOFT)
-            target[pl.ds(g * PIECES, PIECES), 0:HALF, :] = dk.astype(bf16).reshape(PIECES, HALF, HD)
-            target[pl.ds(g * PIECES, PIECES), HALF:LB, :] = dv.astype(bf16).reshape(PIECES, HALF, HD)
-            sum_ref[...] = sum_ref[...] + dot(keys_of(ref, g, 0), pulls, TN)
-
-    dq_ref[...] = sum_ref[...].astype(bf16).T
-
-    @pl.loop(used, PER_SOURCE)
+    def pull(g, at, ref, target, half, cols, width, masked):
+        probs = p_ref[at, :, cols]
+        moved = dot(keys_of(ref, g, 1), turned_ref[:, cols], NN)
+        pulls = (probs.astype(f32) * (moved - row_ref[0:1, cols])).astype(bf16)
+        dk = dot(pulls, rows_ref[cols, :], NN)
+        dv = dot(probs, grad_ref[cols, :], NN) * (1.0 / SCALE_SOFT)
+        target[pl.ds(g * PIECES, PIECES), 0:HALF, :] = dk.astype(bf16).reshape(PIECES, HALF, HD)
+        target[pl.ds(g * PIECES, PIECES), HALF:LB, :] = dv.astype(bf16).reshape(PIECES, HALF, HD)
+        sum_ref[:, cols] = sum_ref[:, cols] + dot(keys_of(ref, g, 0), pulls, TN)
+
+    run = over_keys(pull)
+    run(0, common, whole, ROWS, False)
+    run(common, most, part, ROWS // 2, False)
+    dq_rows = sum_ref[...].astype(bf16).T
+    dq_ref[...] = dq_rows[0 : ROWS // 2]
+    back_ref[ROWS // 2 :] = dq_rows[ROWS // 2 :]
+
+    @pl.loop(most, PER_SOURCE)
     def _(g):
         zero = jnp.zeros((PIECES, LB, HD), bf16)
         dmine_ref[pl.ds(g * PIECES, PIECES)] = zero
@@ -357,8 +397,9 @@
 WIDE = ((ROWS, HD), f32)
 FLAT = ((ROWS, HD), bf16)
 BY_HEAD = ((OWN, LB, HD), f32)
-PROBS = ((GROUPS, KEYS, ROWS), bf16)
+HALF_FLAT = ((ROWS // 2, HD), bf16)
 KEY_PARTS = ((CTX, LB, HD), bf16)
+MIRROR = [(i, CTX - 1 - i) for i in range(CTX)]
 OTHER_CORE = [(i, i ^ 1) for i in range(HEADS)]
 SAME_CORE = [[2 * z + c for z in range(KVH)] for c in range(2)]
 
@@ -368,9 +409,9 @@
     lin_q, lin_k, lin_v, lin_grad, soft_q, soft_grad, soft_k, soft_v = map(
         flat, (lin_q, lin_k, lin_v, lin_grad, soft_q, soft_grad, soft_k, soft_v)
     )
-    pay, within, heads = call(
+    pay, within, heads, trade = call(
         local_kernel,
-        [((CTX, LB + SLICE + 16, HD), bf16), BY_HEAD, ((3, OWN, LB, HD), bf16)],
+        [((CTX, LB + SLICE + 16, HD), bf16), BY_HEAD, ((3, OWN, LB, HD), bf16), FLAT],
         [
             WIDE,
             ((3, ROWS, HD), bf16),
@@ -380,17 +421,18 @@
             ((CTX, SLICE + 16, HD), bf16),
             BY_HEAD,
             ((3, OWN, LB, HD), bf16),
-            pltpu.SemaphoreType.DMA((6,)),
-            pltpu.SemaphoreType.DMA((CTX + 3,)),
+            FLAT,
+            pltpu.SemaphoreType.DMA((8,)),
+            pltpu.SemaphoreType.DMA((CTX + 4,)),
         ],
-        hbm=(0, 1, 2, 3, 4, 5),
-        hbm_out=(0, 1, 2),
-        count=6,
+        hbm=(0, 1, 2, 3, 4, 5, 6, 7),
+        hbm_out=(0, 1, 2, 3),
+        count=8,
         flops=10**9,
         limit=60,
-    )(lin_q, lin_k, lin_v, decay, soft_k, soft_v)
+    )(lin_q, lin_k, lin_v, decay, soft_k, soft_v, soft_q, soft_grad)
+    trade = lax.ppermute(trade, "ctx", MIRROR)
     mine = lax.all_to_all(pay, "ctx", 0, 0)
-    other = lax.ppermute(mine, "head", OTHER_CORE)
     (prefixes,) = call(prefix_kernel, [((CTX, SLICE, HD), bf16)], count=1, flops=10**8)(mine)
     state = lax.all_to_all(prefixes, "ctx", 0, 0).reshape(OWN * HD, HD)
     attended, upstream, sums = call(
@@ -400,45 +442,49 @@
         count=6,
         flops=10**9,
     )(within, heads, state, decay, lin_grad, lin_gain)
-    total = lax.all_to_all(sums, "head", 0, 0)
+    total = lax.all_to_all(after(sums, trade), "head", 0, 0)
     lin_out, att_grad, back = call(
         grad_kernel,
         [FLAT, ((OWN, LB, HD), bf16), ((OWN * HD, HD), bf16)],
         [WIDE],
         count=6,
-        flops=10**9,
+        flops=10**10,
     )(attended, upstream, total, heads, decay, lin_gain)
+    other = lax.ppermute(after(mine, back), "head", OTHER_CORE)
     backs = lax.all_to_all(back.reshape(CTX, SLICE, HD), "ctx", 0, 0)
     (suffixes,) = call(suffix_kernel, [((CTX, SLICE, HD), bf16)], count=2, flops=10**8)(backs, mine)
-    soft_out, soft_dq, dmine, dother = call(
+    own_out, own_dq, traded, dmine, dother = call(
         soft_kernel,
-        [FLAT, FLAT, KEY_PARTS, KEY_PARTS],
+        [HALF_FLAT, HALF_FLAT, FLAT, KEY_PARTS, KEY_PARTS],
         [
+            FLAT,
             ((GROUPS, KEYS, ROWS), f32),
-            PROBS,
+            ((GROUPS, KEYS, ROWS), bf16),
             ((8, ROWS), f32),
             ((8, ROWS), f32),
             ((HD, ROWS), f32),
             ((HD, ROWS), bf16),
             FLAT,
+            ((8, ROWS), f32),
         ],
         smem=(0,),
-        count=5,
+        count=6,
         flops=10**10,
         limit=36,
-    )(reach, after(soft_q, suffixes), soft_grad, mine, other)
+    )(reach, after(soft_q, suffixes), soft_grad, trade, mine, other)
     dgot = lax.ppermute(dother, "head", OTHER_CORE)
     (pay_back,) = call(merge_kernel, [((CTX, LB + SLICE, HD), bf16)], count=3, flops=10**8)(
         dmine, dgot, suffixes
     )
+    traded = lax.ppermute(traded, "ctx", MIRROR)
     got_back = lax.all_to_all(pay_back, "ctx", 0, 0)
     blocks, later = call(
         reduce_kernel, [((KVH, LB, HD), bf16), ((OWN * HD, HD), bf16)], count=1, flops=10**8
     )(got_back)
     spread = lax.all_to_all(blocks, "head", 0, 0, axis_index_groups=SAME_CORE)
-    lin_dq, lin_dk, lin_dv = call(inner_kernel, [FLAT, FLAT, FLAT], [WIDE], count=5, flops=4 * 10**9)(
-        heads, att_grad, state, later, decay
-    )
+    lin_dq, lin_dk, lin_dv, soft_out, soft_dq = call(
+        inner_kernel, [FLAT] * 5, [WIDE], count=8, flops=4 * 10**9
+    )(heads, att_grad, state, later, decay, own_out, own_dq, traded)
     spread = after(spread, lin_dk)
     spread_other = lax.ppermute(spread, "head", OTHER_CORE)
     soft_dk, soft_dv = call(

time: 141 us -> 138 us (0.979)
  blocking collectives: 94.5 us -> 61.3 us
  starting transfers between devices: 10.1 us -> 22 us
  waiting for transfers between devices: 17.1 us -> 28.4 us
  Pallas kernels: 18.3 us -> 24.2 us
    all_to_all x2 -> x1, blocking collectives: 42.7 us -> 20.4 us  [per_device(): total = lax.all_to_all(after(sums, trade), 'head', 0, 0)]
    all_to_all x0 -> x1, waiting for transfers between devices: none -> 12.7 us  [per_device(): mine = lax.all_to_all(pay, 'ctx', 0, 0)]
    all_to_all x1, blocking collectives: 31.9 us -> 20.5 us  [per_device(): got_back = lax.all_to_all(pay_back, 'ctx', 0, 0)]
    all_to_all x1, waiting for transfers between devices: 13.2 us -> 3.75 us  [per_device(): spread = lax.all_to_all(blocks, 'head', 0, 0, axis_index_groups=SAME_CORE)]
    ppermute x1 -> x3, waiting for transfers between devices: 0.01 us -> 8.11 us  [the longest x1 8.07 us: per_device(): traded = lax.ppermute(traded, 'ctx', MIRROR)]
    all_to_all x0 -> x1, starting transfers between devices: none -> 7.73 us  [per_device(): mine = lax.all_to_all(pay, 'ctx', 0, 0)]
    pallas_call x2, Pallas kernels: 8.5 us -> 14.2 us  [the longest x1 11.5 us: per_device(): call(soft_kernel, [HALF_FLAT, HALF_FLAT, FLAT, KEY_PARTS, KEY_PARTS], [FL...]
    ppermute x1 -> x3, starting transfers between devices: 2.23 us -> 6.57 us  [the longest x1 4.77 us: per_device(): trade = lax.ppermute(trade, 'ctx', MIRROR)]
  transfers between devices with their start and end apart: 4 -> 7, of which waited for: 3 -> 5; matrix products, arithmetic and copies ran while one was open for 0% -> 0% of each run, Pallas kernels for 4% -> 3%
where the time goes in v3:
time: 138 us; the launch traced here: 137 us
  blocking collectives  61.3 us (44%)
  waiting for transfers between devices  28.4 us (21%)
  Pallas kernels  24.2 us (18%)
  starting transfers between devices  22 us (16%)
    all_to_all x1, blocking collectives, per_device(): got_back = lax.all_to_all(pay_back, 'ctx', 0, 0)  20.5 us
    all_to_all x1, blocking collectives, per_device(): total = lax.all_to_all(after(sums, trade), 'head', 0, 0)  20.4 us
    all_to_all x1, waiting for transfers between devices, per_device(): mine = lax.all_to_all(pay, 'ctx', 0, 0)  12.7 us
    pallas_call x1, Pallas kernels, per_device(): call(soft_kernel, [HALF_FLAT, HALF_FLAT, FLAT, KEY_PARTS, KEY_PARTS], [FL...  11.5 us
    all_to_all x1, blocking collectives, per_device(): state = lax.all_to_all(prefixes, 'ctx', 0, 0).reshape(OWN * HD, HD)  10.6 us
    all_to_all x1, blocking collectives, per_device(): backs = lax.all_to_all(back.reshape(CTX, SLICE, HD), 'ctx', 0, 0)  9.82 us
    ppermute x1, waiting for transfers between devices, per_device(): traded = lax.ppermute(traded, 'ctx', MIRROR)  8.07 us
    all_to_all x1, starting transfers between devices, per_device(): mine = lax.all_to_all(pay, 'ctx', 0, 0)  7.73 us
  transfers between devices with their start and end apart: 7, of which 5 were waited for; matrix products, arithmetic and copies ran while one was open for 0% of the time, Pallas kernels for 3%

profile of v3, /device:TPU:1, one launch (start us, length us, event | category | flops | bytes accessed | tf_op | source)
XLA Modules:
  0.0 136.8 jit_solution(13636368346958621947)
XLA Ops:
  0.6 4.3 %shard_map.170 = (bf16[16,304,128]{2,1,0:T(8,128)(2,1)}, f32[4,256,128]{2,1,0:T(8,128)}, bf16[3,4,256,128]{3,2,1,0:T(8,128)(2,1)}, bf16[1024,128]{1,0:T(8,128)(2,1)}) custom-call(bf16[1024,128]{1,0:T(8,128)(2,1)} %bitcast.30, bf16[1024,128]{1,0:T(8,128)(2,1)} %bitcast.31, bf16[1024,128]{1,0:T(8,128)(2,1)} %bitcast.32, f32[4,256]{1,0:T(4,128)} %decay_ref.5, ...), custom_call_target="tpu_custom_call" | custom-call | flops 1000000000 | bytes 1048576 | tf_op jit(solution)/shard_map/pallas_call | solution.py:412
  4.9 0.0 copy-start.8
  5.0 7.7 %all-to-all-start = ((bf16[16,304,128]{2,1,0:T(8,128)(2,1)}), bf16[16,304,128]{2,1,0:T(8,128)(2,1)S(1)}, u32[]{:S(2)}, u32[]{:S(2)}) async-start(bf16[16,304,128]{2,1,0:T(8,128)(2,1)} %get-tuple-element.38), calls=%async_computation | async-start | bytes 2490368 | tf_op jit(solution)/shard_map/all_to_all | solution.py:435
  12.7 0.0 copy-start
  12.7 0.0 copy-start.3
  12.7 0.0 copy-start.4
  12.7 0.0 copy-start.6
  12.7 0.0 copy-start.7
  12.7 0.0 copy-done.8
  12.8 4.8 %collective-permute-start = (bf16[1024,128]{1,0:T(8,128)(2,1)S(1)}, bf16[1024,128]{1,0:T(8,128)(2,1)S(1)}, u32[]{:S(2)}, u32[]{:S(2)}) collective-permute-start(bf16[1024,128]{1,0:T(8,128)(2,1)S(1)} %copy-done.8), channel_id=1, source_target_pairs={{0,240},{16,224},{32,208},{48,192},{64,176},{80,160},{96,144},{112... | collective-permute-start | bytes 786440 | tf_op jit(solution)/shard_map/ppermute | solution.py:434
  17.5 12.7 %all-to-all-done.got_ref.first_ref.mine_ref = bf16[16,304,128]{2,1,0:T(8,128)(2,1)S(1)} async-done(((bf16[16,304,128]{2,1,0:T(8,128)(2,1)}), bf16[16,304,128]{2,1,0:T(8,128)(2,1)S(1)}, u32[]{:S(2)}, u32[]{:S(2)}) %all-to-all-start) | async-done | bytes 1245216 | tf_op jit(solution)/shard_map/all_to_all | solution.py:435
  30.3 10.6 %all_to_all.30 = bf16[16,32,128]{2,1,0:T(8,128)(2,1)S(1)} all-to-all(bf16[16,32,128]{2,1,0:T(8,128)(2,1)S(1)} %shard_map.171), channel_id=1, replica_groups=mesh['ctx'=16,'head'=16] {'ctx'}, dimensions={0} | all-to-all | bytes 262144 | tf_op jit(solution)/shard_map/all_to_all | solution.py:437
  40.9 0.0 copy-done
  40.9 0.0 copy-done.3
  40.9 0.0 copy-done.4
  41.0 0.0 copy-done.6
  41.0 0.0 copy-done.7
  41.0 1.2 shard_map.172
  42.2 0.0 collective-permute-done.trade_ref
  42.3 20.4 %all_to_all.31.got_ref = f32[16,4,128]{2,1,0:T(4,128)S(1)} all-to-all(f32[16,4,128]{2,1,0:T(4,128)S(1)} %get-tuple-element.43), channel_id=1, replica_groups=mesh['ctx'=16,'head'=16] {'head'}, dimensions={0} | all-to-all | bytes 65536 | tf_op jit(solution)/shard_map/all_to_all | solution.py:445
  62.6 1.7 %shard_map.173 = (bf16[1024,128]{1,0:T(8,128)(2,1)}, bf16[4,256,128]{2,1,0:T(8,128)(2,1)S(1)}, bf16[512,128]{1,0:T(8,128)(2,1)S(1)}) custom-call(f32[4,256,128]{2,1,0:T(8,128)S(1)} %get-tuple-element.39.att_ref, f32[4,256,128]{2,1,0:T(8,128)S(1)} %get-tuple-element.40.up_ref, f32[16,4,128]{2,1,0:T(4,128)S(1)} %all_to_all.31.got_ref, ...), custom_call_target="tpu_custom_call" | custom-call | flops 10000000000 | bytes 1048576 | tf_op jit(solution)/shard_map/pallas_call | solution.py:446
  64.4 0.0 copy-start.1
  64.4 0.0 copy-start.2
  64.4 0.0 copy-start.5
  64.4 0.4 collective-permute-start.1
  64.8 9.8 %all_to_all.32.got_ref = bf16[16,32,128]{2,1,0:T(8,128)(2,1)S(1)} all-to-all(bf16[16,32,128]{2,1,0:T(8,128)(2,1)S(1)} %bitcast.20), channel_id=1, replica_groups=mesh['ctx'=16,'head'=16] {'ctx'}, dimensions={0} | all-to-all | bytes 262144 | tf_op jit(solution)/shard_map/all_to_all | solution.py:454
  74.6 0.0 collective-permute-done.1.other_ref
  74.6 0.0 copy-done.1
  74.7 0.0 copy-done.2
  74.7 0.0 copy-done.5
  74.7 11.5 %shard_map.175 = (bf16[512,128]{1,0:T(8,128)(2,1)S(1)}, bf16[512,128]{1,0:T(8,128)(2,1)S(1)}, bf16[1024,128]{1,0:T(8,128)(2,1)S(1)}, bf16[16,256,128]{2,1,0:T(8,128)(2,1)S(1)}, bf16[16,256,128]{2,1,0:T(8,128)(2,1)S(1)}) custom-call(s32[32]{0:T(128)S(1)} %copy-done.5, bf16[1024,128]{1,0:T(8,128)(2,1)S(1)} %bitcast.23, bf16[1024,128]{1,0:T(8,128)(2,1)S(1)} %bitcast.25, ...), custom_call_target="tpu_custom_call" | custom-call | flops 10000000000 | bytes 1048576 | tf_op jit(solution)/shard_map/pallas_call | solution.py:456
  86.2 1.7 %collective-permute-start.2 = (bf16[16,256,128]{2,1,0:T(8,128)(2,1)S(1)}, bf16[16,256,128]{2,1,0:T(8,128)(2,1)S(1)}, u32[]{:S(2)}, u32[]{:S(2)}) collective-permute-start(bf16[16,256,128]{2,1,0:T(8,128)(2,1)S(1)} %get-tuple-element.50), channel_id=1, source_target_pairs={{0,1},{1,0},{2,3},{3,2},{4,5},{5,4},{6,7},{7,6},{8,9},{9,8},{10,11... | collective-permute-start | bytes 3145736 | tf_op jit(solution)/shard_map/ppermute | solution.py:475
  87.9 2.3 %collective-permute-done.2.got_ref = bf16[16,256,128]{2,1,0:T(8,128)(2,1)S(1)} collective-permute-done((bf16[16,256,128]{2,1,0:T(8,128)(2,1)S(1)}, bf16[16,256,128]{2,1,0:T(8,128)(2,1)S(1)}, u32[]{:S(2)}, u32[]{:S(2)}) %collective-permute-start.2) | collective-permute-done | bytes 1048608 | tf_op jit(solution)/shard_map/ppermute | solution.py:475
  90.2 0.2 shard_map.176
  90.5 20.5 %all_to_all.33.got_ref = bf16[16,288,128]{2,1,0:T(8,128)(2,1)S(1)} all-to-all(bf16[16,288,128]{2,1,0:T(8,128)(2,1)S(1)} %shard_map.176), channel_id=1, replica_groups=mesh['ctx'=16,'head'=16] {'ctx'}, dimensions={0} | all-to-all | bytes 2359296 | tf_op jit(solution)/shard_map/all_to_all | solution.py:480
  111.0 0.9 shard_map.177
  111.9 3.5 %all-to-all-start.5 = ((bf16[8,256,128]{2,1,0:T(8,128)(2,1)}), bf16[8,256,128]{2,1,0:T(8,128)(2,1)S(1)}, u32[]{:S(2)}, u32[]{:S(2)}) async-start(bf16[8,256,128]{2,1,0:T(8,128)(2,1)} %get-tuple-element.60), calls=%async_computation.5 | async-start | bytes 1048576 | tf_op jit(solution)/shard_map/all_to_all | solution.py:484
  115.4 1.4 %collective-permute-start.3 = (bf16[1024,128]{1,0:T(8,128)(2,1)S(1)}, bf16[1024,128]{1,0:T(8,128)(2,1)S(1)}, u32[]{:S(2)}, u32[]{:S(2)}) collective-permute-start(bf16[1024,128]{1,0:T(8,128)(2,1)S(1)} %get-tuple-element.54), channel_id=1, source_target_pairs={{0,240},{16,224},{32,208},{48,192},{64,176},{80,160},{96,144},{112... | collective-permute-start | bytes 786440 | tf_op jit(solution)/shard_map/ppermute | solution.py:479
  116.8 8.1 %collective-permute-done.3.traded_ref = bf16[1024,128]{1,0:T(8,128)(2,1)S(1)} collective-permute-done((bf16[1024,128]{1,0:T(8,128)(2,1)S(1)}, bf16[1024,128]{1,0:T(8,128)(2,1)S(1)}, u32[]{:S(2)}, u32[]{:S(2)}) %collective-permute-start.3) | collective-permute-done | bytes 262176 | tf_op jit(solution)/shard_map/ppermute | solution.py:479
  124.9 2.6 %shard_map.178 = (bf16[1024,128]{1,0:T(8,128)(2,1)}, bf16[1024,128]{1,0:T(8,128)(2,1)}, bf16[1024,128]{1,0:T(8,128)(2,1)}, bf16[1024,128]{1,0:T(8,128)(2,1)}, bf16[1024,128]{1,0:T(8,128)(2,1)}) custom-call(bf16[3,4,256,128]{3,2,1,0:T(8,128)(2,1)S(1)} %copy-done.6, bf16[4,256,128]{2,1,0:T(8,128)(2,1)S(1)} %get-tuple-element.45.ag_ref, ...), custom_call_target="tpu_custom_call" | custom-call | flops 4000000000 | bytes 1048576 | tf_op jit(solution)/shard_map/pallas_call | solution.py:485
  127.5 3.8 %all-to-all-done.5.mine_ref = bf16[8,256,128]{2,1,0:T(8,128)(2,1)S(1)} async-done(((bf16[8,256,128]{2,1,0:T(8,128)(2,1)}), bf16[8,256,128]{2,1,0:T(8,128)(2,1)S(1)}, u32[]{:S(2)}, u32[]{:S(2)}) %all-to-all-start.5) | async-done | bytes 524320 | tf_op jit(solution)/shard_map/all_to_all | solution.py:484
  131.3 2.5 %collective-permute-start.4 = (bf16[8,256,128]{2,1,0:T(8,128)(2,1)S(1)}, bf16[8,256,128]{2,1,0:T(8,128)(2,1)S(1)}, u32[]{:S(2)}, u32[]{:S(2)}) collective-permute-start(bf16[8,256,128]{2,1,0:T(8,128)(2,1)S(1)} %all-to-all-done.5.mine_ref), channel_id=1, source_target_pairs={{0,1},{1,0},{2,3},{3,2},{4,5},{5,4},{6,7},{7,6},{8,9},{9,8},{10,11... | collective-permute-start | bytes 1572872 | tf_op jit(solution)/shard_map/ppermute | solution.py:489
  133.8 1.5 %collective-permute-done.4.other_ref = bf16[8,256,128]{2,1,0:T(8,128)(2,1)S(1)} collective-permute-done((bf16[8,256,128]{2,1,0:T(8,128)(2,1)S(1)}, bf16[8,256,128]{2,1,0:T(8,128)(2,1)S(1)}, u32[]{:S(2)}, u32[]{:S(2)}) %collective-permute-start.4) | collective-permute-done | bytes 524320 | tf_op jit(solution)/shard_map/ppermute | solution.py:489
  135.3 1.5 %shard_map.179 = (bf16[2048,128]{1,0:T(8,128)(2,1)}, bf16[2048,128]{1,0:T(8,128)(2,1)}) custom-call(bf16[8,256,128]{2,1,0:T(8,128)(2,1)S(1)} %all-to-all-done.5.mine_ref, bf16[8,256,128]{2,1,0:T(8,128)(2,1)S(1)} %collective-permute-done.4.other_ref), custom_call_target="tpu_custom_call" | custom-call | flops 100000000 | bytes 1048576 | tf_op jit(solution)/shard_map/pallas_call | solution.py:490
  (2 shorter events, 0.1 us)
Async XLA Ops:
  4.9 7.8 %copy-start.8 = (bf16[1024,128]{1,0:T(8,128)(2,1)S(1)}, bf16[1024,128]{1,0:T(8,128)(2,1)}, u32[]{:S(2)}) copy-start(bf16[1024,128]{1,0:T(8,128)(2,1)} %get-tuple-element.42) | copy-start | bytes 786436
  5.0 25.3 %all-to-all-start = ((bf16[16,304,128]{2,1,0:T(8,128)(2,1)}), bf16[16,304,128]{2,1,0:T(8,128)(2,1)S(1)}, u32[]{:S(2)}, u32[]{:S(2)}) async-start(bf16[16,304,128]{2,1,0:T(8,128)(2,1)} %get-tuple-element.38), calls=%async_computation | async-start | bytes 2490368 | tf_op jit(solution)/shard_map/all_to_all | solution.py:435
  12.7 28.3 %copy-start = (bf16[256,4,128]{2,1,0:T(4,128)(2,1)S(1)}, bf16[256,4,128]{2,1,0:T(4,128)(2,1)}, u32[]{:S(2)}) copy-start(bf16[256,4,128]{2,1,0:T(4,128)(2,1)} %param.16) | copy-start | bytes 786436
  12.7 28.2 %copy-start.3 = (f32[4,256]{1,0:T(4,128)S(1)}, f32[4,256]{1,0:T(4,128)}, u32[]{:S(2)}) copy-start(f32[4,256]{1,0:T(4,128)} %decay_ref.5) | copy-start | bytes 12292
  12.7 28.2 %copy-start.4 = (f32[4,128]{1,0:T(4,128)S(1)}, f32[4,128]{1,0:T(4,128)}, u32[]{:S(2)}) copy-start(f32[4,128]{1,0:T(4,128)} %gain_ref.3) | copy-start | bytes 6148
  12.7 28.2 %copy-start.6 = (bf16[3,4,256,128]{3,2,1,0:T(8,128)(2,1)S(1)}, bf16[3,4,256,128]{3,2,1,0:T(8,128)(2,1)}, u32[]{:S(2)}) copy-start(bf16[3,4,256,128]{3,2,1,0:T(8,128)(2,1)} %get-tuple-element.37.heads_ref) | copy-start | bytes 2359300
  12.7 28.2 %copy-start.7 = (f32[4,256,128]{2,1,0:T(8,128)S(1)}, f32[4,256,128]{2,1,0:T(8,128)}, u32[]{:S(2)}) copy-start(f32[4,256,128]{2,1,0:T(8,128)} %get-tuple-element.36.within_ref) | copy-start | bytes 1572868
  12.8 29.5 %collective-permute-start = (bf16[1024,128]{1,0:T(8,128)(2,1)S(1)}, bf16[1024,128]{1,0:T(8,128)(2,1)S(1)}, u32[]{:S(2)}, u32[]{:S(2)}) collective-permute-start(bf16[1024,128]{1,0:T(8,128)(2,1)S(1)} %copy-done.8), channel_id=1, source_target_pairs={{0,240},{16,224},{32,208},{48,192},{64,176},{80,160},{96,144},{112... | collective-permute-start | bytes 786440 | tf_op jit(solution)/shard_map/ppermute | solution.py:434
  64.4 10.3 %copy-start.1 = (bf16[256,4,128]{2,1,0:T(4,128)(2,1)S(1)}, bf16[256,4,128]{2,1,0:T(4,128)(2,1)}, u32[]{:S(2)}) copy-start(bf16[256,4,128]{2,1,0:T(4,128)(2,1)} %param.17) | copy-start | bytes 786436
  64.4 10.3 %copy-start.2 = (bf16[256,4,128]{2,1,0:T(4,128)(2,1)S(1)}, bf16[256,4,128]{2,1,0:T(4,128)(2,1)}, u32[]{:S(2)}) copy-start(bf16[256,4,128]{2,1,0:T(4,128)(2,1)} %param.20) | copy-start | bytes 786436
  64.4 10.3 %copy-start.5 = (s32[32]{0:T(128)S(1)}, s32[32]{0:T(128)}, u32[]{:S(2)}) copy-start(s32[32]{0:T(128)} %reach_ref.1) | copy-start | bytes 388
  64.4 10.3 %collective-permute-start.1 = (bf16[16,304,128]{2,1,0:T(8,128)(2,1)S(1)}, bf16[16,304,128]{2,1,0:T(8,128)(2,1)S(1)}, u32[]{:S(2)}, u32[]{:S(2)}) collective-permute-start(bf16[16,304,128]{2,1,0:T(8,128)(2,1)S(1)} %all-to-all-done.got_ref.first_ref.mine_ref), channel_id=1, source_target_pairs={{0,1},{1,0},{2,3},{3,2},{4,5},{5,4},{6,7},{7,6},{8,9},{9,8},{10,11... | collective-permute-start | bytes 3735560 | tf_op jit(solution)/shard_map/ppermute | solution.py:453
  86.2 4.0 %collective-permute-start.2 = (bf16[16,256,128]{2,1,0:T(8,128)(2,1)S(1)}, bf16[16,256,128]{2,1,0:T(8,128)(2,1)S(1)}, u32[]{:S(2)}, u32[]{:S(2)}) collective-permute-start(bf16[16,256,128]{2,1,0:T(8,128)(2,1)S(1)} %get-tuple-element.50), channel_id=1, source_target_pairs={{0,1},{1,0},{2,3},{3,2},{4,5},{5,4},{6,7},{7,6},{8,9},{9,8},{10,11... | collective-permute-start | bytes 3145736 | tf_op jit(solution)/shard_map/ppermute | solution.py:475
  111.9 19.4 %all-to-all-start.5 = ((bf16[8,256,128]{2,1,0:T(8,128)(2,1)}), bf16[8,256,128]{2,1,0:T(8,128)(2,1)S(1)}, u32[]{:S(2)}, u32[]{:S(2)}) async-start(bf16[8,256,128]{2,1,0:T(8,128)(2,1)} %get-tuple-element.60), calls=%async_computation.5 | async-start | bytes 1048576 | tf_op jit(solution)/shard_map/all_to_all | solution.py:484
  115.4 9.5 %collective-permute-start.3 = (bf16[1024,128]{1,0:T(8,128)(2,1)S(1)}, bf16[1024,128]{1,0:T(8,128)(2,1)S(1)}, u32[]{:S(2)}, u32[]{:S(2)}) collective-permute-start(bf16[1024,128]{1,0:T(8,128)(2,1)S(1)} %get-tuple-element.54), channel_id=1, source_target_pairs={{0,240},{16,224},{32,208},{48,192},{64,176},{80,160},{96,144},{112... | collective-permute-start | bytes 786440 | tf_op jit(solution)/shard_map/ppermute | solution.py:479
  131.3 4.0 %collective-permute-start.4 = (bf16[8,256,128]{2,1,0:T(8,128)(2,1)S(1)}, bf16[8,256,128]{2,1,0:T(8,128)(2,1)S(1)}, u32[]{:S(2)}, u32[]{:S(2)}) collective-permute-start(bf16[8,256,128]{2,1,0:T(8,128)(2,1)S(1)} %all-to-all-done.5.mine_ref), channel_id=1, source_target_pairs={{0,1},{1,0},{2,3},{3,2},{4,5},{5,4},{6,7},{7,6},{8,9},{9,8},{10,11... | collective-permute-start | bytes 1572872 | tf_op jit(solution)/shard_map/ppermute | solution.py:489

commit v4 on v3

--- a/solution.py
+++ b/solution.py
@@ -442,6 +442,7 @@
         count=6,
         flops=10**9,
     )(within, heads, state, decay, lin_grad, lin_gain)
+    other = lax.ppermute(after(mine, sums, trade), "head", OTHER_CORE)
     total = lax.all_to_all(after(sums, trade), "head", 0, 0)
     lin_out, att_grad, back = call(
         grad_kernel,
@@ -450,9 +451,7 @@
         count=6,
         flops=10**10,
     )(attended, upstream, total, heads, decay, lin_gain)
-    other = lax.ppermute(after(mine, back), "head", OTHER_CORE)
     backs = lax.all_to_all(back.reshape(CTX, SLICE, HD), "ctx", 0, 0)
-    (suffixes,) = call(suffix_kernel, [((CTX, SLICE, HD), bf16)], count=2, flops=10**8)(backs, mine)
     own_out, own_dq, traded, dmine, dother = call(
         soft_kernel,
         [HALF_FLAT, HALF_FLAT, FLAT, KEY_PARTS, KEY_PARTS],
@@ -471,7 +470,8 @@
         count=6,
         flops=10**10,
         limit=36,
-    )(reach, after(soft_q, suffixes), soft_grad, trade, mine, other)
+    )(reach, after(soft_q, back), soft_grad, trade, mine, other)
+    (suffixes,) = call(suffix_kernel, [((CTX, SLICE, HD), bf16)], count=2, flops=10**8)(after(backs, own_out), mine)
     dgot = lax.ppermute(dother, "head", OTHER_CORE)
     (pay_back,) = call(merge_kernel, [((CTX, LB + SLICE, HD), bf16)], count=3, flops=10**8)(
         dmine, dgot, suffixes

time: 138 us -> 134 us (0.971)
  blocking collectives: 61.3 us -> 56.1 us
  starting transfers between devices: 22 us -> 27 us
  waiting for transfers between devices: 28.4 us -> 24.3 us
    all_to_all x1, blocking collectives: 20.4 us -> 15.8 us  [per_device(): total = lax.all_to_all(after(sums, trade), 'head', 0, 0)]
    ppermute x1, starting transfers between devices: 0.4 us -> 4.79 us  [per_device(): other = lax.ppermute(after(mine, sums, trade), 'head', OTHER_CORE)]
    ppermute x1, waiting for transfers between devices: 2.29 us -> 0.01 us  [per_device(): dgot = lax.ppermute(dother, 'head', OTHER_CORE)]
    ppermute x1, waiting for transfers between devices: 8.07 us -> 6.56 us  [per_device(): traded = lax.ppermute(traded, 'ctx', MIRROR)]
  transfers between devices with their start and end apart: 7 -> 7, of which waited for: 5 -> 4; matrix products, arithmetic and copies ran while one was open for 0% -> 0% of each run, Pallas kernels for 3% -> 4%
where the time goes in v4:
time: 134 us; the launch traced here: 132 us
  blocking collectives  56.1 us (42%)
  starting transfers between devices  27 us (20%)
  waiting for transfers between devices  24.3 us (18%)
  Pallas kernels  24 us (18%)
    all_to_all x1, blocking collectives, per_device(): got_back = lax.all_to_all(pay_back, 'ctx', 0, 0)  20 us
    all_to_all x1, blocking collectives, per_device(): total = lax.all_to_all(after(sums, trade), 'head', 0, 0)  15.8 us
    all_to_all x1, waiting for transfers between devices, per_device(): mine = lax.all_to_all(pay, 'ctx', 0, 0)  12.7 us
    pallas_call x1, Pallas kernels, per_device(): call(soft_kernel, [HALF_FLAT, HALF_FLAT, FLAT, KEY_PARTS, KEY_PARTS], [FL...  11.3 us
    all_to_all x1, blocking collectives, per_device(): state = lax.all_to_all(prefixes, 'ctx', 0, 0).reshape(OWN * HD, HD)  10.6 us
    all_to_all x1, blocking collectives, per_device(): backs = lax.all_to_all(back.reshape(CTX, SLICE, HD), 'ctx', 0, 0)  9.68 us
    all_to_all x1, starting transfers between devices, per_device(): mine = lax.all_to_all(pay, 'ctx', 0, 0)  7.6 us
    ppermute x1, waiting for transfers between devices, per_device(): traded = lax.ppermute(traded, 'ctx', MIRROR)  6.56 us
  transfers between devices with their start and end apart: 7, of which 4 were waited for; matrix products, arithmetic and copies ran while one was open for 0% of the time, Pallas kernels for 4%

profile of v4, /device:TPU:1, one launch (start us, length us, event | category | flops | bytes accessed | tf_op | source)
XLA Modules:
  0.0 132.3 jit_solution(16433152929759434355)
XLA Ops:
  0.6 4.3 %shard_map.170 = (bf16[16,304,128]{2,1,0:T(8,128)(2,1)}, f32[4,256,128]{2,1,0:T(8,128)}, bf16[3,4,256,128]{3,2,1,0:T(8,128)(2,1)}, bf16[1024,128]{1,0:T(8,128)(2,1)}) custom-call(bf16[1024,128]{1,0:T(8,128)(2,1)} %bitcast.30, bf16[1024,128]{1,0:T(8,128)(2,1)} %bitcast.31, bf16[1024,128]{1,0:T(8,128)(2,1)} %bitcast.32, f32[4,256]{1,0:T(4,128)} %decay_ref.5, ...), custom_call_target="tpu_custom_call" | custom-call | flops 1000000000 | bytes 1048576 | tf_op jit(solution)/shard_map/pallas_call | solution.py:412
  4.9 7.6 %all-to-all-start = ((bf16[16,304,128]{2,1,0:T(8,128)(2,1)}), bf16[16,304,128]{2,1,0:T(8,128)(2,1)S(1)}, u32[]{:S(2)}, u32[]{:S(2)}) async-start(bf16[16,304,128]{2,1,0:T(8,128)(2,1)} %get-tuple-element.39), calls=%async_computation | async-start | bytes 2490368 | tf_op jit(solution)/shard_map/all_to_all | solution.py:435
  12.5 0.0 copy-start
  12.6 0.0 copy-start.3
  12.6 0.0 copy-start.4
  12.6 0.0 copy-start.6
  12.6 0.0 copy-start.7
  12.6 4.8 %collective-permute-start = (bf16[1024,128]{1,0:T(8,128)(2,1)}, bf16[1024,128]{1,0:T(8,128)(2,1)S(1)}, u32[]{:S(2)}, u32[]{:S(2)}) collective-permute-start(bf16[1024,128]{1,0:T(8,128)(2,1)} %get-tuple-element.43), channel_id=1, source_target_pairs={{0,240},{16,224},{32,208},{48,192},{64,176},{80,160},{96,144},{112... | collective-permute-start | bytes 786440 | tf_op jit(solution)/shard_map/ppermute | solution.py:434
  17.4 12.7 %all-to-all-done.got_ref.mine_ref.first_ref = bf16[16,304,128]{2,1,0:T(8,128)(2,1)S(1)} async-done(((bf16[16,304,128]{2,1,0:T(8,128)(2,1)}), bf16[16,304,128]{2,1,0:T(8,128)(2,1)S(1)}, u32[]{:S(2)}, u32[]{:S(2)}) %all-to-all-start) | async-done | bytes 1245216 | tf_op jit(solution)/shard_map/all_to_all | solution.py:435
  30.2 10.6 %all_to_all.30 = bf16[16,32,128]{2,1,0:T(8,128)(2,1)S(1)} all-to-all(bf16[16,32,128]{2,1,0:T(8,128)(2,1)S(1)} %shard_map.171), channel_id=1, replica_groups=mesh['ctx'=16,'head'=16] {'ctx'}, dimensions={0} | all-to-all | bytes 262144 | tf_op jit(solution)/shard_map/all_to_all | solution.py:437
  40.8 0.0 copy-done
  40.8 0.0 copy-done.3
  40.8 0.0 copy-done.4
  40.8 0.0 copy-done.6
  40.8 0.0 copy-done.7
  40.8 1.2 shard_map.172
  42.1 0.0 collective-permute-done.trade_ref
  42.1 4.8 %collective-permute-start.1 = (bf16[16,304,128]{2,1,0:T(8,128)(2,1)S(1)}, bf16[16,304,128]{2,1,0:T(8,128)(2,1)S(1)}, u32[]{:S(2)}, u32[]{:S(2)}) collective-permute-start(bf16[16,304,128]{2,1,0:T(8,128)(2,1)S(1)} %all-to-all-done.got_ref.mine_ref.first_ref), channel_id=1, source_target_pairs={{0,1},{1,0},{2,3},{3,2},{4,5},{5,4},{6,7},{7,6},{8,9},{9,8},{10,11... | collective-permute-start | bytes 3735560 | tf_op jit(solution)/shard_map/ppermute | solution.py:445
  46.9 15.8 %all_to_all.31.got_ref = f32[16,4,128]{2,1,0:T(4,128)S(1)} all-to-all(f32[16,4,128]{2,1,0:T(4,128)S(1)} %get-tuple-element.44), channel_id=1, replica_groups=mesh['ctx'=16,'head'=16] {'head'}, dimensions={0} | all-to-all | bytes 65536 | tf_op jit(solution)/shard_map/all_to_all | solution.py:446
  62.7 0.0 copy-start.1
  62.7 0.0 copy-start.2
  62.7 0.0 copy-start.5
  62.7 1.7 %shard_map.173 = (bf16[1024,128]{1,0:T(8,128)(2,1)}, bf16[4,256,128]{2,1,0:T(8,128)(2,1)S(1)}, bf16[512,128]{1,0:T(8,128)(2,1)S(1)}) custom-call(f32[4,256,128]{2,1,0:T(8,128)S(1)} %get-tuple-element.40.att_ref, f32[4,256,128]{2,1,0:T(8,128)S(1)} %get-tuple-element.41.up_ref, f32[16,4,128]{2,1,0:T(4,128)S(1)} %all_to_all.31.got_ref, ...), custom_call_target="tpu_custom_call" | custom-call | flops 10000000000 | bytes 1048576 | tf_op jit(solution)/shard_map/pallas_call | solution.py:447
  64.4 0.0 collective-permute-done.1.other_ref
  64.4 0.0 copy-done.1
  64.4 0.0 copy-done.2
  64.4 0.0 copy-done.5
  64.4 11.3 %shard_map.174 = (bf16[512,128]{1,0:T(8,128)(2,1)S(1)}, bf16[512,128]{1,0:T(8,128)(2,1)S(1)}, bf16[1024,128]{1,0:T(8,128)(2,1)S(1)}, bf16[16,256,128]{2,1,0:T(8,128)(2,1)S(1)}, bf16[16,256,128]{2,1,0:T(8,128)(2,1)S(1)}) custom-call(s32[32]{0:T(128)S(1)} %copy-done.5, bf16[1024,128]{1,0:T(8,128)(2,1)S(1)} %bitcast.23, bf16[1024,128]{1,0:T(8,128)(2,1)S(1)} %bitcast.25, ...), custom_call_target="tpu_custom_call" | custom-call | flops 10000000000 | bytes 1048576 | tf_op jit(solution)/shard_map/pallas_call | solution.py:455
  75.7 0.7 collective-permute-start.2
  76.4 9.7 %all_to_all.32.got_ref = bf16[16,32,128]{2,1,0:T(8,128)(2,1)S(1)} all-to-all(bf16[16,32,128]{2,1,0:T(8,128)(2,1)S(1)} %bitcast.20), channel_id=1, replica_groups=mesh['ctx'=16,'head'=16] {'ctx'}, dimensions={0} | all-to-all | bytes 262144 | tf_op jit(solution)/shard_map/all_to_all | solution.py:454
  86.1 0.0 collective-permute-done.2.got_ref
  86.1 0.2 shard_map.176
  86.4 20.0 %all_to_all.33.got_ref = bf16[16,288,128]{2,1,0:T(8,128)(2,1)S(1)} all-to-all(bf16[16,288,128]{2,1,0:T(8,128)(2,1)S(1)} %shard_map.176), channel_id=1, replica_groups=mesh['ctx'=16,'head'=16] {'ctx'}, dimensions={0} | all-to-all | bytes 2359296 | tf_op jit(solution)/shard_map/all_to_all | solution.py:480
  106.4 0.9 shard_map.177
  107.4 3.5 %all-to-all-start.5 = ((bf16[8,256,128]{2,1,0:T(8,128)(2,1)}), bf16[8,256,128]{2,1,0:T(8,128)(2,1)S(1)}, u32[]{:S(2)}, u32[]{:S(2)}) async-start(bf16[8,256,128]{2,1,0:T(8,128)(2,1)} %get-tuple-element.62), calls=%async_computation.5 | async-start | bytes 1048576 | tf_op jit(solution)/shard_map/all_to_all | solution.py:484
  110.9 2.1 %collective-permute-start.3 = (bf16[1024,128]{1,0:T(8,128)(2,1)S(1)}, bf16[1024,128]{1,0:T(8,128)(2,1)S(1)}, u32[]{:S(2)}, u32[]{:S(2)}) collective-permute-start(bf16[1024,128]{1,0:T(8,128)(2,1)S(1)} %get-tuple-element.56), channel_id=1, source_target_pairs={{0,240},{16,224},{32,208},{48,192},{64,176},{80,160},{96,144},{112... | collective-permute-start | bytes 786440 | tf_op jit(solution)/shard_map/ppermute | solution.py:479
  112.9 6.6 %collective-permute-done.3.traded_ref = bf16[1024,128]{1,0:T(8,128)(2,1)S(1)} collective-permute-done((bf16[1024,128]{1,0:T(8,128)(2,1)S(1)}, bf16[1024,128]{1,0:T(8,128)(2,1)S(1)}, u32[]{:S(2)}, u32[]{:S(2)}) %collective-permute-start.3) | collective-permute-done | bytes 262176 | tf_op jit(solution)/shard_map/ppermute | solution.py:479
  119.5 2.6 %shard_map.178 = (bf16[1024,128]{1,0:T(8,128)(2,1)}, bf16[1024,128]{1,0:T(8,128)(2,1)}, bf16[1024,128]{1,0:T(8,128)(2,1)}, bf16[1024,128]{1,0:T(8,128)(2,1)}, bf16[1024,128]{1,0:T(8,128)(2,1)}) custom-call(bf16[3,4,256,128]{3,2,1,0:T(8,128)(2,1)S(1)} %copy-done.6, bf16[4,256,128]{2,1,0:T(8,128)(2,1)S(1)} %get-tuple-element.46.ag_ref, ...), custom_call_target="tpu_custom_call" | custom-call | flops 4000000000 | bytes 1048576 | tf_op jit(solution)/shard_map/pallas_call | solution.py:485
  122.1 3.5 %all-to-all-done.5.mine_ref = bf16[8,256,128]{2,1,0:T(8,128)(2,1)S(1)} async-done(((bf16[8,256,128]{2,1,0:T(8,128)(2,1)}), bf16[8,256,128]{2,1,0:T(8,128)(2,1)S(1)}, u32[]{:S(2)}, u32[]{:S(2)}) %all-to-all-start.5) | async-done | bytes 524320 | tf_op jit(solution)/shard_map/all_to_all | solution.py:484
  125.6 3.6 %collective-permute-start.4 = (bf16[8,256,128]{2,1,0:T(8,128)(2,1)S(1)}, bf16[8,256,128]{2,1,0:T(8,128)(2,1)S(1)}, u32[]{:S(2)}, u32[]{:S(2)}) collective-permute-start(bf16[8,256,128]{2,1,0:T(8,128)(2,1)S(1)} %all-to-all-done.5.mine_ref), channel_id=1, source_target_pairs={{0,1},{1,0},{2,3},{3,2},{4,5},{5,4},{6,7},{7,6},{8,9},{9,8},{10,11... | collective-permute-start | bytes 1572872 | tf_op jit(solution)/shard_map/ppermute | solution.py:489
  129.2 1.5 %collective-permute-done.4.other_ref = bf16[8,256,128]{2,1,0:T(8,128)(2,1)S(1)} collective-permute-done((bf16[8,256,128]{2,1,0:T(8,128)(2,1)S(1)}, bf16[8,256,128]{2,1,0:T(8,128)(2,1)S(1)}, u32[]{:S(2)}, u32[]{:S(2)}) %collective-permute-start.4) | collective-permute-done | bytes 524320 | tf_op jit(solution)/shard_map/ppermute | solution.py:489
  130.8 1.5 %shard_map.179 = (bf16[2048,128]{1,0:T(8,128)(2,1)}, bf16[2048,128]{1,0:T(8,128)(2,1)}) custom-call(bf16[8,256,128]{2,1,0:T(8,128)(2,1)S(1)} %all-to-all-done.5.mine_ref, bf16[8,256,128]{2,1,0:T(8,128)(2,1)S(1)} %collective-permute-done.4.other_ref), custom_call_target="tpu_custom_call" | custom-call | flops 100000000 | bytes 1048576 | tf_op jit(solution)/shard_map/pallas_call | solution.py:490
  (2 shorter events, 0.1 us)
Async XLA Ops:
  4.9 25.2 %all-to-all-start = ((bf16[16,304,128]{2,1,0:T(8,128)(2,1)}), bf16[16,304,128]{2,1,0:T(8,128)(2,1)S(1)}, u32[]{:S(2)}, u32[]{:S(2)}) async-start(bf16[16,304,128]{2,1,0:T(8,128)(2,1)} %get-tuple-element.39), calls=%async_computation | async-start | bytes 2490368 | tf_op jit(solution)/shard_map/all_to_all | solution.py:435
  12.5 28.3 %copy-start = (bf16[256,4,128]{2,1,0:T(4,128)(2,1)S(1)}, bf16[256,4,128]{2,1,0:T(4,128)(2,1)}, u32[]{:S(2)}) copy-start(bf16[256,4,128]{2,1,0:T(4,128)(2,1)} %param.16) | copy-start | bytes 786436
  12.6 28.2 %copy-start.3 = (f32[4,256]{1,0:T(4,128)S(1)}, f32[4,256]{1,0:T(4,128)}, u32[]{:S(2)}) copy-start(f32[4,256]{1,0:T(4,128)} %decay_ref.5) | copy-start | bytes 12292
  12.6 28.2 %copy-start.4 = (f32[4,128]{1,0:T(4,128)S(1)}, f32[4,128]{1,0:T(4,128)}, u32[]{:S(2)}) copy-start(f32[4,128]{1,0:T(4,128)} %gain_ref.3) | copy-start | bytes 6148
  12.6 28.2 %copy-start.6 = (bf16[3,4,256,128]{3,2,1,0:T(8,128)(2,1)S(1)}, bf16[3,4,256,128]{3,2,1,0:T(8,128)(2,1)}, u32[]{:S(2)}) copy-start(bf16[3,4,256,128]{3,2,1,0:T(8,128)(2,1)} %get-tuple-element.38.heads_ref) | copy-start | bytes 2359300
  12.6 28.2 %copy-start.7 = (f32[4,256,128]{2,1,0:T(8,128)S(1)}, f32[4,256,128]{2,1,0:T(8,128)}, u32[]{:S(2)}) copy-start(f32[4,256,128]{2,1,0:T(8,128)} %get-tuple-element.37.within_ref) | copy-start | bytes 1572868
  12.6 29.5 %collective-permute-start = (bf16[1024,128]{1,0:T(8,128)(2,1)}, bf16[1024,128]{1,0:T(8,128)(2,1)S(1)}, u32[]{:S(2)}, u32[]{:S(2)}) collective-permute-start(bf16[1024,128]{1,0:T(8,128)(2,1)} %get-tuple-element.43), channel_id=1, source_target_pairs={{0,240},{16,224},{32,208},{48,192},{64,176},{80,160},{96,144},{112... | collective-permute-start | bytes 786440 | tf_op jit(solution)/shard_map/ppermute | solution.py:434
  42.1 22.3 %collective-permute-start.1 = (bf16[16,304,128]{2,1,0:T(8,128)(2,1)S(1)}, bf16[16,304,128]{2,1,0:T(8,128)(2,1)S(1)}, u32[]{:S(2)}, u32[]{:S(2)}) collective-permute-start(bf16[16,304,128]{2,1,0:T(8,128)(2,1)S(1)} %all-to-all-done.got_ref.mine_ref.first_ref), channel_id=1, source_target_pairs={{0,1},{1,0},{2,3},{3,2},{4,5},{5,4},{6,7},{7,6},{8,9},{9,8},{10,11... | collective-permute-start | bytes 3735560 | tf_op jit(solution)/shard_map/ppermute | solution.py:445
  62.7 1.7 %copy-start.1 = (bf16[256,4,128]{2,1,0:T(4,128)(2,1)S(1)}, bf16[256,4,128]{2,1,0:T(4,128)(2,1)}, u32[]{:S(2)}) copy-start(bf16[256,4,128]{2,1,0:T(4,128)(2,1)} %param.17) | copy-start | bytes 786436
  62.7 1.7 %copy-start.2 = (bf16[256,4,128]{2,1,0:T(4,128)(2,1)S(1)}, bf16[256,4,128]{2,1,0:T(4,128)(2,1)}, u32[]{:S(2)}) copy-start(bf16[256,4,128]{2,1,0:T(4,128)(2,1)} %param.20) | copy-start | bytes 786436
  62.7 1.7 %copy-start.5 = (s32[32]{0:T(128)S(1)}, s32[32]{0:T(128)}, u32[]{:S(2)}) copy-start(s32[32]{0:T(128)} %reach_ref.1) | copy-start | bytes 388
  75.7 10.4 %collective-permute-start.2 = (bf16[16,256,128]{2,1,0:T(8,128)(2,1)S(1)}, bf16[16,256,128]{2,1,0:T(8,128)(2,1)S(1)}, u32[]{:S(2)}, u32[]{:S(2)}) collective-permute-start(bf16[16,256,128]{2,1,0:T(8,128)(2,1)S(1)} %get-tuple-element.51), channel_id=1, source_target_pairs={{0,1},{1,0},{2,3},{3,2},{4,5},{5,4},{6,7},{7,6},{8,9},{9,8},{10,11... | collective-permute-start | bytes 3145736 | tf_op jit(solution)/shard_map/ppermute | solution.py:475
  107.4 18.2 %all-to-all-start.5 = ((bf16[8,256,128]{2,1,0:T(8,128)(2,1)}), bf16[8,256,128]{2,1,0:T(8,128)(2,1)S(1)}, u32[]{:S(2)}, u32[]{:S(2)}) async-start(bf16[8,256,128]{2,1,0:T(8,128)(2,1)} %get-tuple-element.62), calls=%async_computation.5 | async-start | bytes 1048576 | tf_op jit(solution)/shard_map/all_to_all | solution.py:484
  110.9 8.6 %collective-permute-start.3 = (bf16[1024,128]{1,0:T(8,128)(2,1)S(1)}, bf16[1024,128]{1,0:T(8,128)(2,1)S(1)}, u32[]{:S(2)}, u32[]{:S(2)}) collective-permute-start(bf16[1024,128]{1,0:T(8,128)(2,1)S(1)} %get-tuple-element.56), channel_id=1, source_target_pairs={{0,240},{16,224},{32,208},{48,192},{64,176},{80,160},{96,144},{112... | collective-permute-start | bytes 786440 | tf_op jit(solution)/shard_map/ppermute | solution.py:479
  125.6 5.2 %collective-permute-start.4 = (bf16[8,256,128]{2,1,0:T(8,128)(2,1)S(1)}, bf16[8,256,128]{2,1,0:T(8,128)(2,1)S(1)}, u32[]{:S(2)}, u32[]{:S(2)}) collective-permute-start(bf16[8,256,128]{2,1,0:T(8,128)(2,1)S(1)} %all-to-all-done.5.mine_ref), channel_id=1, source_target_pairs={{0,1},{1,0},{2,3},{3,2},{4,5},{5,4},{6,7},{7,6},{8,9},{9,8},{10,11... | collective-permute-start | bytes 1572872 | tf_op jit(solution)/shard_map/ppermute | solution.py:489

commit v5 on v4

--- a/solution.py
+++ b/solution.py
@@ -65,8 +65,8 @@
 
 
 def local_kernel(
-    q_hbm, k_hbm, v_hbm, decay_hbm, sk_hbm, sv_hbm, sq_hbm, sg_hbm, pay_hbm, within_hbm, heads_hbm, trade_hbm,
-    scratch, raw, halves, decay_ref, kv_ref, own_ref, within_ref, heads_ref, trade_ref, sems, out_sems,
+    k_hbm, v_hbm, decay_hbm, sk_hbm, sv_hbm, sq_hbm, sg_hbm, pay_hbm, trade_hbm,
+    scratch, raw, halves, decay_ref, kv_ref, own_ref, trade_ref, sems, out_sems,
 ):
     side = lax.axis_index("head") % 2
     kv = lax.axis_index("head") // 2
@@ -74,13 +74,12 @@
     copies = [
         pltpu.make_async_copy(sk_hbm.at[half], halves.at[0], sems.at[0]),
         pltpu.make_async_copy(sv_hbm.at[half], halves.at[1], sems.at[1]),
-        pltpu.make_async_copy(k_hbm, raw.at[1], sems.at[2]),
-        pltpu.make_async_copy(v_hbm, raw.at[2], sems.at[3]),
-        pltpu.make_async_copy(q_hbm, raw.at[0], sems.at[4]),
-        pltpu.make_async_copy(decay_hbm, decay_ref, sems.at[5]),
+        pltpu.make_async_copy(k_hbm, raw.at[0], sems.at[2]),
+        pltpu.make_async_copy(v_hbm, raw.at[1], sems.at[3]),
+        pltpu.make_async_copy(decay_hbm, decay_ref, sems.at[4]),
     ] + [
         pltpu.make_async_copy(
-            x.at[pl.ds(ROWS // 2, ROWS // 2)], trade_ref.at[pl.ds(n * (ROWS // 2), ROWS // 2)], sems.at[6 + n]
+            x.at[pl.ds(ROWS // 2, ROWS // 2)], trade_ref.at[pl.ds(n * (ROWS // 2), ROWS // 2)], sems.at[5 + n]
         )
         for n, x in enumerate((sq_hbm, sg_hbm))
     ]
@@ -95,21 +94,19 @@
     ]
     for copy in sent:
         copy.start()
-    for copy in copies[6:]:
+    for copy in copies[5:]:
         copy.wait()
-    traded = pltpu.make_async_copy(trade_ref, trade_hbm, out_sems.at[CTX + 3])
+    traded = pltpu.make_async_copy(trade_ref, trade_hbm, out_sems.at[CTX + 1])
     traded.start()
-    copies[5].wait()
+    copies[4].wait()
     as_rows, as_cols, row, col = run_sums(decay_ref[...])
     copies[2].wait()
-    keys_wide = split_heads(raw.at[1], scratch)
+    keys_wide = split_heads(raw.at[0], scratch)
     copies[3].wait()
-    values = [x.astype(bf16) for x in split_heads(raw.at[2], scratch)]
+    values = [x.astype(bf16) for x in split_heads(raw.at[1], scratch)]
     for h in range(OWN):
         run_col = as_cols[:, h : h + 1]
         total = as_rows[h : h + 1, LB - 1 : LB]
-        heads_ref[1, h] = keys_wide[h].astype(bf16)
-        heads_ref[2, h] = values[h]
         tailed = (keys_wide[h] * jnp.exp(total - run_col)).astype(bf16)
         own = dot(tailed, values[h], TN).astype(bf16)
         high = total.astype(bf16).astype(f32)
@@ -122,20 +119,19 @@
             own_ref[j, SLICE:, :] = marks
     states = pltpu.make_async_copy(own_ref, pay_hbm.at[:, pl.ds(LB, SLICE + 16)], out_sems.at[CTX])
     states.start()
-    copies[4].wait()
-    queries = [x.astype(bf16) for x in split_heads(raw.at[0], scratch)]
-    for h in range(OWN):
-        heads_ref[0, h] = queries[h]
-    kept = pltpu.make_async_copy(heads_ref, heads_hbm, out_sems.at[CTX + 1])
-    kept.start()
+    for copy in sent + [traded, states]:
+        copy.wait()
+
+
+def within_kernel(q_ref, k_ref, v_ref, decay_ref, within_ref, heads_ref, scratch):
+    as_rows, as_cols, row, col = run_sums(decay_ref[...])
+    for n, ref in enumerate((q_ref, k_ref, v_ref)):
+        for h, part in enumerate(split_heads(ref, scratch)):
+            heads_ref[n, h] = part.astype(bf16)
     for h in range(OWN):
         decays = jnp.exp(jnp.where(row >= col, as_cols[:, h : h + 1] - as_rows[h : h + 1, :], FAR_BELOW))
-        weights = (dot(queries[h], heads_ref[1, h], NT) * decays * SCALE_LIN).astype(bf16)
-        within_ref[h] = dot(weights, values[h], NN)
-    inner = pltpu.make_async_copy(within_ref, within_hbm, out_sems.at[CTX + 2])
-    inner.start()
-    for copy in sent + [traded, states, kept, inner]:
-        copy.wait()
+        weights = (dot(heads_ref[0, h], heads_ref[1, h], NT) * decays * SCALE_LIN).astype(bf16)
+        within_ref[h] = dot(weights, heads_ref[2, h], NN)
 
 
 def prefix_kernel(got_ref, out_ref):
@@ -342,24 +338,33 @@
         pay_ref[j, LB:, :] = back_ref[j]
 
 
-def reduce_kernel(got_ref, block_ref, later_ref):
+def reduce_kernel(got_ref, first_ref, block_ref, out_ref):
     block = got_ref[0, 0:LB, :].astype(f32)
     for j in range(1, CTX):
         block = block + got_ref[j, 0:LB, :].astype(f32)
-    block = block.astype(bf16)
-    for z in range(KVH):
-        block_ref[z] = block
-    for j in range(CTX):
-        later_ref[j * SLICE : (j + 1) * SLICE, :] = got_ref[j, LB:, :]
-
-
-def suffix_kernel(got_ref, first_ref, out_ref):
+    block_ref[...] = block.astype(bf16)
     state = jnp.zeros((SLICE, HD), f32)
     for j in reversed(range(CTX)):
         out_ref[j] = state.astype(bf16)
         marks = first_ref[j, LB + SLICE :, :].astype(f32)
         fade = jnp.exp(marks[0:1, :] + marks[8:9, :])
-        state = fade * state + got_ref[j].astype(f32)
+        state = fade * state + got_ref[j, LB:, :].astype(f32)
+
+
+def pair_kernel(own_ref, below_ref, above_ref, up_ref, down_ref):
+    up_ref[0:LB] = own_ref[...]
+    up_ref[LB:] = below_ref[...]
+    down_ref[0:LB] = own_ref[...]
+    down_ref[LB:] = above_ref[...]
+
+
+def gather_kernel(own_ref, below_ref, above_ref, far_ref, up_ref, down_ref, out_ref):
+    z = lax.axis_index("head") // 2
+    for shift, ref, at in (
+        (0, own_ref, 0), (-2, below_ref, 0), (2, above_ref, 0), (4, far_ref, 0),
+        (-1, up_ref, 0), (-3, up_ref, 1), (1, down_ref, 0), (3, down_ref, 1),
+    ):
+        out_ref[(z + shift + KVH) % KVH] = ref[at * LB : (at + 1) * LB, :]
 
 
 def spread_kernel(mine_ref, other_ref, dk_ref, dv_ref, scratch):
@@ -401,7 +406,7 @@
 KEY_PARTS = ((CTX, LB, HD), bf16)
 MIRROR = [(i, CTX - 1 - i) for i in range(CTX)]
 OTHER_CORE = [(i, i ^ 1) for i in range(HEADS)]
-SAME_CORE = [[2 * z + c for z in range(KVH)] for c in range(2)]
+ALONG = {k: [(i, (i + 2 * k) % HEADS) for i in range(HEADS)] for k in (-2, -1, 1, 2, 4)}
 
 
 def per_device(lin_q, lin_k, lin_v, decay, lin_gain, lin_grad, soft_q, soft_k, soft_v, soft_grad, reach):
@@ -409,31 +414,34 @@
     lin_q, lin_k, lin_v, lin_grad, soft_q, soft_grad, soft_k, soft_v = map(
         flat, (lin_q, lin_k, lin_v, lin_grad, soft_q, soft_grad, soft_k, soft_v)
     )
-    pay, within, heads, trade = call(
+    pay, trade = call(
         local_kernel,
-        [((CTX, LB + SLICE + 16, HD), bf16), BY_HEAD, ((3, OWN, LB, HD), bf16), FLAT],
+        [((CTX, LB + SLICE + 16, HD), bf16), FLAT],
         [
             WIDE,
-            ((3, ROWS, HD), bf16),
+            ((2, ROWS, HD), bf16),
             ((2, HALF * KVH, HD), bf16),
             ((OWN, LB), f32),
             ((LB, HD), bf16),
             ((CTX, SLICE + 16, HD), bf16),
-            BY_HEAD,
-            ((3, OWN, LB, HD), bf16),
             FLAT,
-            pltpu.SemaphoreType.DMA((8,)),
-            pltpu.SemaphoreType.DMA((CTX + 4,)),
+            pltpu.SemaphoreType.DMA((7,)),
+            pltpu.SemaphoreType.DMA((CTX + 2,)),
         ],
-        hbm=(0, 1, 2, 3, 4, 5, 6, 7),
-        hbm_out=(0, 1, 2, 3),
-        count=8,
+        hbm=(0, 1, 2, 3, 4, 5, 6),
+        hbm_out=(0, 1),
+        count=7,
         flops=10**9,
         limit=60,
-    )(lin_q, lin_k, lin_v, decay, soft_k, soft_v, soft_q, soft_grad)
+    )(lin_k, lin_v, decay, soft_k, soft_v, soft_q, soft_grad)
+    within, heads = call(
+        within_kernel, [BY_HEAD, ((3, OWN, LB, HD), bf16)], [WIDE], count=4, flops=10**9, limit=60
+    )(lin_q, lin_k, lin_v, after(decay, pay))
     trade = lax.ppermute(trade, "ctx", MIRROR)
     mine = lax.all_to_all(pay, "ctx", 0, 0)
-    (prefixes,) = call(prefix_kernel, [((CTX, SLICE, HD), bf16)], count=1, flops=10**8)(mine)
+    (prefixes,) = call(prefix_kernel, [((CTX, SLICE, HD), bf16)], count=1, flops=10**8)(
+        after(mine, within)
+    )
     state = lax.all_to_all(prefixes, "ctx", 0, 0).reshape(OWN * HD, HD)
     attended, upstream, sums = call(
         attend_kernel,
@@ -444,14 +452,6 @@
     )(within, heads, state, decay, lin_grad, lin_gain)
     other = lax.ppermute(after(mine, sums, trade), "head", OTHER_CORE)
     total = lax.all_to_all(after(sums, trade), "head", 0, 0)
-    lin_out, att_grad, back = call(
-        grad_kernel,
-        [FLAT, ((OWN, LB, HD), bf16), ((OWN * HD, HD), bf16)],
-        [WIDE],
-        count=6,
-        flops=10**10,
-    )(attended, upstream, total, heads, decay, lin_gain)
-    backs = lax.all_to_all(back.reshape(CTX, SLICE, HD), "ctx", 0, 0)
     own_out, own_dq, traded, dmine, dother = call(
         soft_kernel,
         [HALF_FLAT, HALF_FLAT, FLAT, KEY_PARTS, KEY_PARTS],
@@ -470,22 +470,34 @@
         count=6,
         flops=10**10,
         limit=36,
-    )(reach, after(soft_q, back), soft_grad, trade, mine, other)
-    (suffixes,) = call(suffix_kernel, [((CTX, SLICE, HD), bf16)], count=2, flops=10**8)(after(backs, own_out), mine)
+    )(reach, after(soft_q, total), soft_grad, trade, mine, other)
     dgot = lax.ppermute(dother, "head", OTHER_CORE)
+    lin_out, att_grad, back = call(
+        grad_kernel,
+        [FLAT, ((OWN, LB, HD), bf16), ((OWN * HD, HD), bf16)],
+        [WIDE],
+        count=6,
+        flops=2 * 10**9,
+    )(attended, upstream, total, heads, decay, after(lin_gain, own_out))
     (pay_back,) = call(merge_kernel, [((CTX, LB + SLICE, HD), bf16)], count=3, flops=10**8)(
-        dmine, dgot, suffixes
-    )
-    traded = lax.ppermute(traded, "ctx", MIRROR)
+        dmine, dgot, back.reshape(CTX, SLICE, HD)
+    )
     got_back = lax.all_to_all(pay_back, "ctx", 0, 0)
-    blocks, later = call(
-        reduce_kernel, [((KVH, LB, HD), bf16), ((OWN * HD, HD), bf16)], count=1, flops=10**8
-    )(got_back)
-    spread = lax.all_to_all(blocks, "head", 0, 0, axis_index_groups=SAME_CORE)
+    block, suffixes = call(
+        reduce_kernel, [((LB, HD), bf16), ((CTX, SLICE, HD), bf16)], count=2, flops=10**8
+    )(got_back, mine)
+    along = lambda x, k: lax.ppermute(x, "head", ALONG[k])
+    below, above, far = along(block, 2), along(block, -2), along(block, 4)
+    traded = lax.ppermute(after(traded, block), "ctx", MIRROR)
+    later = lax.all_to_all(suffixes, "ctx", 0, 0).reshape(OWN * HD, HD)
+    up, down = call(pair_kernel, [((2 * LB, HD), bf16)] * 2, count=3, flops=10**8)(block, below, after(above, later))
+    up, down = along(up, 1), along(down, -1)
     lin_dq, lin_dk, lin_dv, soft_out, soft_dq = call(
         inner_kernel, [FLAT] * 5, [WIDE], count=8, flops=4 * 10**9
     )(heads, att_grad, state, later, decay, own_out, own_dq, traded)
-    spread = after(spread, lin_dk)
+    (spread,) = call(gather_kernel, [((KVH, LB, HD), bf16)], count=6, flops=10**8)(
+        after(block, lin_dk), below, above, far, up, down
+    )
     spread_other = lax.ppermute(spread, "head", OTHER_CORE)
     soft_dk, soft_dv = call(
         spread_kernel,

time: 134 us -> 127 us (0.948); the launches traced: 132 us -> 127 us
  starting transfers between devices: 27 us -> 35.3 us
  waiting for transfers between devices: 24.3 us -> 16.2 us
  blocking collectives: 56.1 us -> 48.7 us
  Pallas kernels: 24 us -> 26.1 us
    all_to_all x1 -> x0, blocking collectives: 9.68 us -> none  [per_device(): backs = lax.all_to_all(back.reshape(CTX, SLICE, HD), 'ctx', 0, 0)]
    ppermute x1 -> x6, starting transfers between devices: 2.07 us -> 7.78 us  [the longest x5 6.47 us: per_device(): along = lambda x, k: lax.ppermute(x, 'head', ALONG[k])]
    ppermute x1 -> x6, waiting for transfers between devices: 6.56 us -> 2.69 us  [the longest x5 2.68 us: per_device(): along = lambda x, k: lax.ppermute(x, 'head', ALONG[k])]
    all_to_all x1, waiting for transfers between devices: 12.7 us -> 9.72 us  [per_device(): mine = lax.all_to_all(pay, 'ctx', 0, 0)]
    all_to_all x1, blocking collectives: 20 us -> 22.4 us  [per_device(): got_back = lax.all_to_all(pay_back, 'ctx', 0, 0)]
    pallas_call x3 -> x5, Pallas kernels: 5.28 us -> 7.36 us  [the longest x1 3.55 us: per_device(): call(local_kernel, [((CTX, LB + SLICE + 16, HD), bf16), FLAT], [WIDE, ((2...]
    all_to_all x1, waiting for transfers between devices: 3.46 us -> 1.65 us  [per_device(): later = lax.all_to_all(suffixes, 'ctx', 0, 0).reshape(OWN * HD, HD)]
    all_to_all x1, starting transfers between devices: 3.49 us -> 4.85 us  [per_device(): later = lax.all_to_all(suffixes, 'ctx', 0, 0).reshape(OWN * HD, HD)]
  transfers between devices with their start and end apart: 7 -> 12, of which waited for: 4 -> 6; matrix products, arithmetic and copies ran while one was open for 0% -> 0% of each run, Pallas kernels for 4% -> 7%
where the time goes in v5:
time: 127 us
  blocking collectives  48.7 us (38%)
  starting transfers between devices  35.3 us (28%)
  Pallas kernels  26.1 us (21%)
  waiting for transfers between devices  16.2 us (13%)
    all_to_all x1, blocking collectives, per_device(): got_back = lax.all_to_all(pay_back, 'ctx', 0, 0)  22.4 us
    all_to_all x1, blocking collectives, per_device(): total = lax.all_to_all(after(sums, trade), 'head', 0, 0)  15.8 us
    pallas_call x1, Pallas kernels, per_device(): call(soft_kernel, [HALF_FLAT, HALF_FLAT, FLAT, KEY_PARTS, KEY_PARTS], [FL...  11.3 us
    all_to_all x1, blocking collectives, per_device(): state = lax.all_to_all(prefixes, 'ctx', 0, 0).reshape(OWN * HD, HD)  10.6 us
    all_to_all x1, waiting for transfers between devices, per_device(): mine = lax.all_to_all(pay, 'ctx', 0, 0)  9.72 us
    all_to_all x1, starting transfers between devices, per_device(): mine = lax.all_to_all(pay, 'ctx', 0, 0)  7.73 us
    ppermute x5, starting transfers between devices, per_device(): along = lambda x, k: lax.ppermute(x, 'head', ALONG[k])  6.47 us
    all_to_all x1, starting transfers between devices, per_device(): later = lax.all_to_all(suffixes, 'ctx', 0, 0).reshape(OWN * HD, HD)  4.85 us
  transfers between devices with their start and end apart: 12, of which 6 were waited for; matrix products, arithmetic and copies ran while one was open for 0% of the time, Pallas kernels for 7%

profile of v5, /device:TPU:1, one launch (start us, length us, event | category | flops | bytes accessed | tf_op | source)
XLA Modules:
  0.0 127.1 jit_solution(9684871976390492023)
XLA Ops:
  0.6 3.5 %shard_map.170 = (bf16[16,304,128]{2,1,0:T(8,128)(2,1)}, bf16[1024,128]{1,0:T(8,128)(2,1)}) custom-call(bf16[1024,128]{1,0:T(8,128)(2,1)} %bitcast.33, bf16[1024,128]{1,0:T(8,128)(2,1)} %bitcast.35, f32[4,256]{1,0:T(4,128)} %decay_ref.6, bf16[2048,128]{1,0:T(8,128)(2,1)} %bitcast.28, bf16[2048,128]{1,0:T(8,128)(2,1)} %bitcast.29, ...), custom_call_target="tpu_custom_call" | custom-call | flops 1000000000 | bytes 1048576 | tf_op jit(solution)/shard_map/pallas_call | solution.py:417
  4.2 0.0 copy-start.8
  4.2 7.7 %all-to-all-start = ((bf16[16,304,128]{2,1,0:T(8,128)(2,1)}), bf16[16,304,128]{2,1,0:T(8,128)(2,1)S(1)}, u32[]{:S(2)}, u32[]{:S(2)}) async-start(bf16[16,304,128]{2,1,0:T(8,128)(2,1)} %get-tuple-element.43), calls=%async_computation | async-start | bytes 2490368 | tf_op jit(solution)/shard_map/all_to_all | solution.py:441
  11.9 0.0 copy-done.8
  11.9 4.8 %collective-permute-start = (bf16[1024,128]{1,0:T(8,128)(2,1)S(1)}, bf16[1024,128]{1,0:T(8,128)(2,1)S(1)}, u32[]{:S(2)}, u32[]{:S(2)}) collective-permute-start(bf16[1024,128]{1,0:T(8,128)(2,1)S(1)} %copy-done.8), channel_id=1, source_target_pairs={{0,240},{16,224},{32,208},{48,192},{64,176},{80,160},{96,144},{112... | collective-permute-start | bytes 786440 | tf_op jit(solution)/shard_map/ppermute | solution.py:440
  16.7 3.0 %shard_map.171 = (f32[4,256,128]{2,1,0:T(8,128)}, bf16[3,4,256,128]{3,2,1,0:T(8,128)(2,1)}) custom-call(bf16[1024,128]{1,0:T(8,128)(2,1)} %bitcast.32, bf16[1024,128]{1,0:T(8,128)(2,1)} %bitcast.34, bf16[1024,128]{1,0:T(8,128)(2,1)} %bitcast.36, f32[4,256]{1,0:T(4,128)} %decay_ref.6), custom_call_target="tpu_custom_call" | custom-call | flops 1000000000 | bytes 1048576 | tf_op jit(solution)/shard_map/pallas_call | solution.py:437
  19.8 0.0 copy-start.6
  19.8 0.0 copy-start.7
  19.8 9.7 %all-to-all-done.got_ref.mine_ref.first_ref = bf16[16,304,128]{2,1,0:T(8,128)(2,1)S(1)} async-done(((bf16[16,304,128]{2,1,0:T(8,128)(2,1)}), bf16[16,304,128]{2,1,0:T(8,128)(2,1)S(1)}, u32[]{:S(2)}, u32[]{:S(2)}) %all-to-all-start) | async-done | bytes 1245216 | tf_op jit(solution)/shard_map/all_to_all | solution.py:441
  29.6 10.6 %all_to_all.25 = bf16[16,32,128]{2,1,0:T(8,128)(2,1)S(1)} all-to-all(bf16[16,32,128]{2,1,0:T(8,128)(2,1)S(1)} %shard_map.172), channel_id=1, replica_groups=mesh['ctx'=16,'head'=16] {'ctx'}, dimensions={0} | all-to-all | bytes 262144 | tf_op jit(solution)/shard_map/all_to_all | solution.py:445
  40.2 0.0 copy-done
  40.2 0.0 copy-done.3
  40.2 0.0 copy-done.4
  40.2 0.0 copy-done.6
  40.2 0.0 copy-done.7
  40.2 0.0 copy-start.1
  40.2 0.0 copy-start.2
  40.2 0.0 copy-start.5
  40.2 1.2 shard_map.173
  41.5 0.0 collective-permute-done.trade_ref
  41.5 4.8 %collective-permute-start.1 = (bf16[16,304,128]{2,1,0:T(8,128)(2,1)S(1)}, bf16[16,304,128]{2,1,0:T(8,128)(2,1)S(1)}, u32[]{:S(2)}, u32[]{:S(2)}) collective-permute-start(bf16[16,304,128]{2,1,0:T(8,128)(2,1)S(1)} %all-to-all-done.got_ref.mine_ref.first_ref), channel_id=1, source_target_pairs={{0,1},{1,0},{2,3},{3,2},{4,5},{5,4},{6,7},{7,6},{8,9},{9,8},{10,11... | collective-permute-start | bytes 3735560 | tf_op jit(solution)/shard_map/ppermute | solution.py:453
  46.3 15.8 %all_to_all.26.got_ref = f32[16,4,128]{2,1,0:T(4,128)S(1)} all-to-all(f32[16,4,128]{2,1,0:T(4,128)S(1)} %get-tuple-element.52), channel_id=1, replica_groups=mesh['ctx'=16,'head'=16] {'head'}, dimensions={0} | all-to-all | bytes 65536 | tf_op jit(solution)/shard_map/all_to_all | solution.py:454
  62.1 0.0 collective-permute-done.1.other_ref
  62.1 11.3 %shard_map.174 = (bf16[512,128]{1,0:T(8,128)(2,1)S(1)}, bf16[512,128]{1,0:T(8,128)(2,1)S(1)}, bf16[1024,128]{1,0:T(8,128)(2,1)S(1)}, bf16[16,256,128]{2,1,0:T(8,128)(2,1)S(1)}, bf16[16,256,128]{2,1,0:T(8,128)(2,1)S(1)}) custom-call(s32[32]{0:T(128)S(1)} %copy-done.5, bf16[1024,128]{1,0:T(8,128)(2,1)S(1)} %bitcast.25, bf16[1024,128]{1,0:T(8,128)(2,1)S(1)} %bitcast.27, ...), custom_call_target="tpu_custom_call" | custom-call | flops 10000000000 | bytes 1048576 | tf_op jit(solution)/shard_map/pallas_call | solution.py:455
  73.4 0.7 collective-permute-start.2
  74.1 1.7 %shard_map.175 = (bf16[1024,128]{1,0:T(8,128)(2,1)}, bf16[4,256,128]{2,1,0:T(8,128)(2,1)S(1)}, bf16[512,128]{1,0:T(8,128)(2,1)S(1)}) custom-call(f32[4,256,128]{2,1,0:T(8,128)S(1)} %get-tuple-element.48.att_ref, f32[4,256,128]{2,1,0:T(8,128)S(1)} %get-tuple-element.49.up_ref, f32[16,4,128]{2,1,0:T(4,128)S(1)} %all_to_all.26.got_ref, ...), custom_call_target="tpu_custom_call" | custom-call | flops 2000000000 | bytes 1048576 | tf_op jit(solution)/shard_map/pallas_call | solution.py:475
  75.8 0.5 collective-permute-done.2.got_ref
  76.4 0.2 shard_map.176
  76.6 22.4 %all_to_all.27.got_ref = bf16[16,288,128]{2,1,0:T(8,128)(2,1)S(1)} all-to-all(bf16[16,288,128]{2,1,0:T(8,128)(2,1)S(1)} %shard_map.176), channel_id=1, replica_groups=mesh['ctx'=16,'head'=16] {'ctx'}, dimensions={0} | all-to-all | bytes 2359296 | tf_op jit(solution)/shard_map/all_to_all | solution.py:485
  99.0 0.7 shard_map.177
  99.7 1.3 %collective-permute-start.3 = (bf16[1024,128]{1,0:T(8,128)(2,1)S(1)}, bf16[1024,128]{1,0:T(8,128)(2,1)S(1)}, u32[]{:S(2)}, u32[]{:S(2)}) collective-permute-start(bf16[1024,128]{1,0:T(8,128)(2,1)S(1)} %get-tuple-element.66), channel_id=1, source_target_pairs={{0,240},{16,224},{32,208},{48,192},{64,176},{80,160},{96,144},{112... | collective-permute-start | bytes 786440 | tf_op jit(solution)/shard_map/ppermute | solution.py:491
  101.0 4.9 %all-to-all-start.4 = ((bf16[16,32,128]{2,1,0:T(8,128)(2,1)}), bf16[16,32,128]{2,1,0:T(8,128)(2,1)S(1)}, u32[]{:S(2)}, u32[]{:S(2)}) async-start(bf16[16,32,128]{2,1,0:T(8,128)(2,1)} %get-tuple-element.62), calls=%async_computation.4 | async-start | bytes 262144 | tf_op jit(solution)/shard_map/all_to_all | solution.py:492
  105.9 0.4 collective-permute-start.5
  106.3 2.0 %collective-permute-start.4 = (bf16[256,128]{1,0:T(8,128)(2,1)S(1)}, bf16[256,128]{1,0:T(8,128)(2,1)S(1)}, u32[]{:S(2)}, u32[]{:S(2)}) collective-permute-start(bf16[256,128]{1,0:T(8,128)(2,1)S(1)} %get-tuple-element.72.own_ref), channel_id=1, source_target_pairs={{0,4},{1,5},{2,6},{3,7},{4,8},{5,9},{6,10},{7,11},{8,12},{9,13},{1... | collective-permute-start | bytes 196616 | tf_op jit(solution)/shard_map/ppermute | solution.py:489
  108.3 1.3 collective-permute-start.6
  109.6 1.3 %collective-permute-done.5.above_ref = bf16[256,128]{1,0:T(8,128)(2,1)S(1)} collective-permute-done((bf16[256,128]{1,0:T(8,128)(2,1)S(1)}, bf16[256,128]{1,0:T(8,128)(2,1)S(1)}, u32[]{:S(2)}, u32[]{:S(2)}) %collective-permute-start.5) | collective-permute-done | bytes 65568 | tf_op jit(solution)/shard_map/ppermute | solution.py:489
  110.9 1.7 %all-to-all-done.4 = bf16[16,32,128]{2,1,0:T(8,128)(2,1)S(1)} async-done(((bf16[16,32,128]{2,1,0:T(8,128)(2,1)}), bf16[16,32,128]{2,1,0:T(8,128)(2,1)S(1)}, u32[]{:S(2)}, u32[]{:S(2)}) %all-to-all-start.4) | async-done | bytes 131104 | tf_op jit(solution)/shard_map/all_to_all | solution.py:492
  112.6 0.0 collective-permute-done.4.below_ref
  112.6 0.9 collective-permute-start.7
  113.6 1.8 %collective-permute-start.8 = (bf16[512,128]{1,0:T(8,128)(2,1)S(1)}, bf16[512,128]{1,0:T(8,128)(2,1)S(1)}, u32[]{:S(2)}, u32[]{:S(2)}) collective-permute-start(bf16[512,128]{1,0:T(8,128)(2,1)S(1)} %get-tuple-element.75), channel_id=1, source_target_pairs={{0,14},{1,15},{2,0},{3,1},{4,2},{5,3},{6,4},{7,5},{8,6},{9,7},{10,... | collective-permute-start | bytes 393224 | tf_op jit(solution)/shard_map/ppermute | solution.py:489
  115.4 0.0 collective-permute-done.3.traded_ref
  115.4 2.6 %shard_map.178 = (bf16[1024,128]{1,0:T(8,128)(2,1)}, bf16[1024,128]{1,0:T(8,128)(2,1)}, bf16[1024,128]{1,0:T(8,128)(2,1)}, bf16[1024,128]{1,0:T(8,128)(2,1)}, bf16[1024,128]{1,0:T(8,128)(2,1)}) custom-call(bf16[3,4,256,128]{3,2,1,0:T(8,128)(2,1)S(1)} %copy-done.6, bf16[4,256,128]{2,1,0:T(8,128)(2,1)S(1)} %get-tuple-element.58.ag_ref, ...), custom_call_target="tpu_custom_call" | custom-call | flops 4000000000 | bytes 1048576 | tf_op jit(solution)/shard_map/pallas_call | solution.py:495
  118.0 0.0 collective-permute-done.6.far_ref
  118.0 1.3 %collective-permute-done.7.up_ref = bf16[512,128]{1,0:T(8,128)(2,1)S(1)} collective-permute-done((bf16[512,128]{1,0:T(8,128)(2,1)S(1)}, bf16[512,128]{1,0:T(8,128)(2,1)S(1)}, u32[]{:S(2)}, u32[]{:S(2)}) %collective-permute-start.7) | collective-permute-done | bytes 131104 | tf_op jit(solution)/shard_map/ppermute | solution.py:489
  119.3 0.0 collective-permute-done.8.down_ref
  119.4 4.7 %collective-permute-start.9 = (bf16[8,256,128]{2,1,0:T(8,128)(2,1)S(1)}, bf16[8,256,128]{2,1,0:T(8,128)(2,1)S(1)}, u32[]{:S(2)}, u32[]{:S(2)}) collective-permute-start(bf16[8,256,128]{2,1,0:T(8,128)(2,1)S(1)} %shard_map.180.mine_ref), channel_id=1, source_target_pairs={{0,1},{1,0},{2,3},{3,2},{4,5},{5,4},{6,7},{7,6},{8,9},{9,8},{10,11... | collective-permute-start | bytes 1572872 | tf_op jit(solution)/shard_map/ppermute | solution.py:501
  124.1 1.5 %collective-permute-done.9.other_ref = bf16[8,256,128]{2,1,0:T(8,128)(2,1)S(1)} collective-permute-done((bf16[8,256,128]{2,1,0:T(8,128)(2,1)S(1)}, bf16[8,256,128]{2,1,0:T(8,128)(2,1)S(1)}, u32[]{:S(2)}, u32[]{:S(2)}) %collective-permute-start.9) | collective-permute-done | bytes 524320 | tf_op jit(solution)/shard_map/ppermute | solution.py:501
  125.6 1.5 %shard_map.181 = (bf16[2048,128]{1,0:T(8,128)(2,1)}, bf16[2048,128]{1,0:T(8,128)(2,1)}) custom-call(bf16[8,256,128]{2,1,0:T(8,128)(2,1)S(1)} %shard_map.180.mine_ref, bf16[8,256,128]{2,1,0:T(8,128)(2,1)S(1)} %collective-permute-done.9.other_ref), custom_call_target="tpu_custom_call" | custom-call | flops 100000000 | bytes 1048576 | tf_op jit(solution)/shard_map/pallas_call | solution.py:502
  (9 shorter events, 0.1 us)
Async XLA Ops:
  4.2 7.7 %copy-start.8 = (bf16[1024,128]{1,0:T(8,128)(2,1)S(1)}, bf16[1024,128]{1,0:T(8,128)(2,1)}, u32[]{:S(2)}) copy-start(bf16[1024,128]{1,0:T(8,128)(2,1)} %get-tuple-element.51) | copy-start | bytes 786436
  4.2 25.3 %all-to-all-start = ((bf16[16,304,128]{2,1,0:T(8,128)(2,1)}), bf16[16,304,128]{2,1,0:T(8,128)(2,1)S(1)}, u32[]{:S(2)}, u32[]{:S(2)}) async-start(bf16[16,304,128]{2,1,0:T(8,128)(2,1)} %get-tuple-element.43), calls=%async_computation | async-start | bytes 2490368 | tf_op jit(solution)/shard_map/all_to_all | solution.py:441
  11.9 29.6 %collective-permute-start = (bf16[1024,128]{1,0:T(8,128)(2,1)S(1)}, bf16[1024,128]{1,0:T(8,128)(2,1)S(1)}, u32[]{:S(2)}, u32[]{:S(2)}) collective-permute-start(bf16[1024,128]{1,0:T(8,128)(2,1)S(1)} %copy-done.8), channel_id=1, source_target_pairs={{0,240},{16,224},{32,208},{48,192},{64,176},{80,160},{96,144},{112... | collective-permute-start | bytes 786440 | tf_op jit(solution)/shard_map/ppermute | solution.py:440
  19.8 20.4 %copy-start = (bf16[256,4,128]{2,1,0:T(4,128)(2,1)S(1)}, bf16[256,4,128]{2,1,0:T(4,128)(2,1)}, u32[]{:S(2)}) copy-start(bf16[256,4,128]{2,1,0:T(4,128)(2,1)} %param.16) | copy-start | bytes 786436
  19.8 20.4 %copy-start.3 = (f32[4,256]{1,0:T(4,128)S(1)}, f32[4,256]{1,0:T(4,128)}, u32[]{:S(2)}) copy-start(f32[4,256]{1,0:T(4,128)} %decay_ref.6) | copy-start | bytes 12292
  19.8 20.4 %copy-start.4 = (f32[4,128]{1,0:T(4,128)S(1)}, f32[4,128]{1,0:T(4,128)}, u32[]{:S(2)}) copy-start(f32[4,128]{1,0:T(4,128)} %gain_ref.2) | copy-start | bytes 6148
  19.8 20.4 %copy-start.6 = (bf16[3,4,256,128]{3,2,1,0:T(8,128)(2,1)S(1)}, bf16[3,4,256,128]{3,2,1,0:T(8,128)(2,1)}, u32[]{:S(2)}) copy-start(bf16[3,4,256,128]{3,2,1,0:T(8,128)(2,1)} %get-tuple-element.46.heads_ref) | copy-start | bytes 2359300
  19.8 20.4 %copy-start.7 = (f32[4,256,128]{2,1,0:T(8,128)S(1)}, f32[4,256,128]{2,1,0:T(8,128)}, u32[]{:S(2)}) copy-start(f32[4,256,128]{2,1,0:T(8,128)} %get-tuple-element.45.within_ref) | copy-start | bytes 1572868
  40.2 21.9 %copy-start.1 = (bf16[256,4,128]{2,1,0:T(4,128)(2,1)S(1)}, bf16[256,4,128]{2,1,0:T(4,128)(2,1)}, u32[]{:S(2)}) copy-start(bf16[256,4,128]{2,1,0:T(4,128)(2,1)} %param.17) | copy-start | bytes 786436
  40.2 21.9 %copy-start.2 = (bf16[256,4,128]{2,1,0:T(4,128)(2,1)S(1)}, bf16[256,4,128]{2,1,0:T(4,128)(2,1)}, u32[]{:S(2)}) copy-start(bf16[256,4,128]{2,1,0:T(4,128)(2,1)} %param.20) | copy-start | bytes 786436
  40.2 21.9 %copy-start.5 = (s32[32]{0:T(128)S(1)}, s32[32]{0:T(128)}, u32[]{:S(2)}) copy-start(s32[32]{0:T(128)} %reach_ref.1) | copy-start | bytes 388
  41.5 20.6 %collective-permute-start.1 = (bf16[16,304,128]{2,1,0:T(8,128)(2,1)S(1)}, bf16[16,304,128]{2,1,0:T(8,128)(2,1)S(1)}, u32[]{:S(2)}, u32[]{:S(2)}) collective-permute-start(bf16[16,304,128]{2,1,0:T(8,128)(2,1)S(1)} %all-to-all-done.got_ref.mine_ref.first_ref), channel_id=1, source_target_pairs={{0,1},{1,0},{2,3},{3,2},{4,5},{5,4},{6,7},{7,6},{8,9},{9,8},{10,11... | collective-permute-start | bytes 3735560 | tf_op jit(solution)/shard_map/ppermute | solution.py:453
  73.4 2.9 %collective-permute-start.2 = (bf16[16,256,128]{2,1,0:T(8,128)(2,1)S(1)}, bf16[16,256,128]{2,1,0:T(8,128)(2,1)S(1)}, u32[]{:S(2)}, u32[]{:S(2)}) collective-permute-start(bf16[16,256,128]{2,1,0:T(8,128)(2,1)S(1)} %get-tuple-element.60), channel_id=1, source_target_pairs={{0,1},{1,0},{2,3},{3,2},{4,5},{5,4},{6,7},{7,6},{8,9},{9,8},{10,11... | collective-permute-start | bytes 3145736 | tf_op jit(solution)/shard_map/ppermute | solution.py:474
  99.7 15.7 %collective-permute-start.3 = (bf16[1024,128]{1,0:T(8,128)(2,1)S(1)}, bf16[1024,128]{1,0:T(8,128)(2,1)S(1)}, u32[]{:S(2)}, u32[]{:S(2)}) collective-permute-start(bf16[1024,128]{1,0:T(8,128)(2,1)S(1)} %get-tuple-element.66), channel_id=1, source_target_pairs={{0,240},{16,224},{32,208},{48,192},{64,176},{80,160},{96,144},{112... | collective-permute-start | bytes 786440 | tf_op jit(solution)/shard_map/ppermute | solution.py:491
  101.0 11.6 %all-to-all-start.4 = ((bf16[16,32,128]{2,1,0:T(8,128)(2,1)}), bf16[16,32,128]{2,1,0:T(8,128)(2,1)S(1)}, u32[]{:S(2)}, u32[]{:S(2)}) async-start(bf16[16,32,128]{2,1,0:T(8,128)(2,1)} %get-tuple-element.62), calls=%async_computation.4 | async-start | bytes 262144 | tf_op jit(solution)/shard_map/all_to_all | solution.py:492
  105.9 5.1 %collective-permute-start.5 = (bf16[256,128]{1,0:T(8,128)(2,1)S(1)}, bf16[256,128]{1,0:T(8,128)(2,1)S(1)}, u32[]{:S(2)}, u32[]{:S(2)}) collective-permute-start(bf16[256,128]{1,0:T(8,128)(2,1)S(1)} %get-tuple-element.72.own_ref), channel_id=1, source_target_pairs={{0,12},{1,13},{2,14},{3,15},{4,0},{5,1},{6,2},{7,3},{8,4},{9,5},{1... | collective-permute-start | bytes 196616 | tf_op jit(solution)/shard_map/ppermute | solution.py:489
  106.3 6.3 %collective-permute-start.4 = (bf16[256,128]{1,0:T(8,128)(2,1)S(1)}, bf16[256,128]{1,0:T(8,128)(2,1)S(1)}, u32[]{:S(2)}, u32[]{:S(2)}) collective-permute-start(bf16[256,128]{1,0:T(8,128)(2,1)S(1)} %get-tuple-element.72.own_ref), channel_id=1, source_target_pairs={{0,4},{1,5},{2,6},{3,7},{4,8},{5,9},{6,10},{7,11},{8,12},{9,13},{1... | collective-permute-start | bytes 196616 | tf_op jit(solution)/shard_map/ppermute | solution.py:489
  108.3 9.7 %collective-permute-start.6 = (bf16[256,128]{1,0:T(8,128)(2,1)S(1)}, bf16[256,128]{1,0:T(8,128)(2,1)S(1)}, u32[]{:S(2)}, u32[]{:S(2)}) collective-permute-start(bf16[256,128]{1,0:T(8,128)(2,1)S(1)} %get-tuple-element.72.own_ref), channel_id=1, source_target_pairs={{0,8},{1,9},{2,10},{3,11},{4,12},{5,13},{6,14},{7,15},{8,0},{9,1},... | collective-permute-start | bytes 196616 | tf_op jit(solution)/shard_map/ppermute | solution.py:489
  112.6 6.7 %collective-permute-start.7 = (bf16[512,128]{1,0:T(8,128)(2,1)S(1)}, bf16[512,128]{1,0:T(8,128)(2,1)S(1)}, u32[]{:S(2)}, u32[]{:S(2)}) collective-permute-start(bf16[512,128]{1,0:T(8,128)(2,1)S(1)} %get-tuple-element.74), channel_id=1, source_target_pairs={{0,2},{1,3},{2,4},{3,5},{4,6},{5,7},{6,8},{7,9},{8,10},{9,11},{10,... | collective-permute-start | bytes 393224 | tf_op jit(solution)/shard_map/ppermute | solution.py:489
  113.6 5.8 %collective-permute-start.8 = (bf16[512,128]{1,0:T(8,128)(2,1)S(1)}, bf16[512,128]{1,0:T(8,128)(2,1)S(1)}, u32[]{:S(2)}, u32[]{:S(2)}) collective-permute-start(bf16[512,128]{1,0:T(8,128)(2,1)S(1)} %get-tuple-element.75), channel_id=1, source_target_pairs={{0,14},{1,15},{2,0},{3,1},{4,2},{5,3},{6,4},{7,5},{8,6},{9,7},{10,... | collective-permute-start | bytes 393224 | tf_op jit(solution)/shard_map/ppermute | solution.py:489
  119.4 6.2 %collective-permute-start.9 = (bf16[8,256,128]{2,1,0:T(8,128)(2,1)S(1)}, bf16[8,256,128]{2,1,0:T(8,128)(2,1)S(1)}, u32[]{:S(2)}, u32[]{:S(2)}) collective-permute-start(bf16[8,256,128]{2,1,0:T(8,128)(2,1)S(1)} %shard_map.180.mine_ref), channel_id=1, source_target_pairs={{0,1},{1,0},{2,3},{3,2},{4,5},{5,4},{6,7},{7,6},{8,9},{9,8},{10,11... | collective-permute-start | bytes 1572872 | tf_op jit(solution)/shard_map/ppermute | solution.py:501

commit v6 on v5

--- a/solution.py
+++ b/solution.py
@@ -192,12 +192,8 @@
 
 
 def inner_kernel(
-    heads_ref, ag_ref, state_ref, later_ref, decay_ref, out_ref, sdq_ref, traded_ref,
-    dq_ref, dk_ref, dv_ref, soft_out_ref, soft_dq_ref, scratch,
+    heads_ref, ag_ref, state_ref, later_ref, decay_ref, dq_ref, dk_ref, dv_ref, scratch
 ):
-    for n, (own, target) in enumerate(((out_ref, soft_out_ref), (sdq_ref, soft_dq_ref))):
-        target[0 : ROWS // 2] = own[...]
-        target[ROWS // 2 :] = traded_ref[n * (ROWS // 2) : (n + 1) * (ROWS // 2)]
     as_rows, as_cols, row, col = run_sums(decay_ref[...])
     query_grads, key_grads, value_grads = [], [], []
     for h in range(OWN):
@@ -367,14 +363,34 @@
         out_ref[(z + shift + KVH) % KVH] = ref[at * LB : (at + 1) * LB, :]
 
 
-def spread_kernel(mine_ref, other_ref, dk_ref, dv_ref, scratch):
+def fill_rows(source_ref, scratch):
+    filled = []
+    for part in range(2):
+        for z in range(KVH):
+            rows = source_ref[z, part * HALF : (part + 1) * HALF, :]
+            scratch[pl.ds(z, HALF, stride=KVH), :] = rows.astype(f32)
+        filled.append(scratch[...].astype(bf16))
+    return filled
+
+
+def near_kernel(mine_ref, rows_ref, scratch):
+    for part, rows in enumerate(fill_rows(mine_ref, scratch)):
+        rows_ref[part] = rows
+
+
+def spread_kernel(
+    near_ref, other_ref, out_ref, sdq_ref, traded_ref, dk_ref, dv_ref, soft_out_ref, soft_dq_ref, scratch
+):
     side = lax.axis_index("head") % 2
-    for part, target in ((0, dk_ref), (1, dv_ref)):
-        for z in range(KVH):
-            rows = slice(part * HALF, (part + 1) * HALF)
-            scratch[pl.ds(side * (HALF * KVH) + z, HALF, stride=KVH), :] = mine_ref[z, rows, :].astype(f32)
-            scratch[pl.ds((1 - side) * (HALF * KVH) + z, HALF, stride=KVH), :] = other_ref[z, rows, :].astype(f32)
-        target[...] = scratch[...].astype(bf16)
+    here = pl.ds(pl.multiple_of(side * (HALF * KVH), HALF * KVH), HALF * KVH)
+    there = pl.ds(pl.multiple_of((1 - side) * (HALF * KVH), HALF * KVH), HALF * KVH)
+    for n, (own, target) in enumerate(((out_ref, soft_out_ref), (sdq_ref, soft_dq_ref))):
+        target[0 : ROWS // 2] = own[...]
+        target[ROWS // 2 :] = traded_ref[n * (ROWS // 2) : (n + 1) * (ROWS // 2)]
+    for part, rows in enumerate(fill_rows(other_ref, scratch)):
+        target = (dk_ref, dv_ref)[part]
+        target[here, :] = near_ref[part]
+        target[there, :] = rows
 
 
 def call(kernel, outs, scratch=(), smem=(), hbm=(), hbm_out=(), count=0, flops=0, limit=8):
@@ -488,24 +504,31 @@
     )(got_back, mine)
     along = lambda x, k: lax.ppermute(x, "head", ALONG[k])
     below, above, far = along(block, 2), along(block, -2), along(block, 4)
-    traded = lax.ppermute(after(traded, block), "ctx", MIRROR)
     later = lax.all_to_all(suffixes, "ctx", 0, 0).reshape(OWN * HD, HD)
     up, down = call(pair_kernel, [((2 * LB, HD), bf16)] * 2, count=3, flops=10**8)(block, below, after(above, later))
     up, down = along(up, 1), along(down, -1)
-    lin_dq, lin_dk, lin_dv, soft_out, soft_dq = call(
-        inner_kernel, [FLAT] * 5, [WIDE], count=8, flops=4 * 10**9
-    )(heads, att_grad, state, later, decay, own_out, own_dq, traded)
+    traded = lax.ppermute(after(traded, block), "ctx", MIRROR)
+    lin_dq, lin_dk, lin_dv = call(inner_kernel, [FLAT] * 3, [WIDE], count=5, flops=4 * 10**9)(
+        heads, att_grad, state, later, decay
+    )
     (spread,) = call(gather_kernel, [((KVH, LB, HD), bf16)], count=6, flops=10**8)(
-        after(block, lin_dk), below, above, far, up, down
+        after(block, lin_dk, traded), below, above, far, up, down
     )
     spread_other = lax.ppermute(spread, "head", OTHER_CORE)
-    soft_dk, soft_dv = call(
+    (near,) = call(
+        near_kernel,
+        [((2, HALF * KVH, HD), bf16)],
+        [((HALF * KVH, HD), f32)],
+        count=1,
+        flops=10**8,
+    )(spread)
+    soft_dk, soft_dv, soft_out, soft_dq = call(
         spread_kernel,
-        [((LB * KVH, HD), bf16), ((LB * KVH, HD), bf16)],
-        [((LB * KVH, HD), f32)],
-        count=2,
+        [((LB * KVH, HD), bf16), ((LB * KVH, HD), bf16), FLAT, FLAT],
+        [((HALF * KVH, HD), f32)],
+        count=5,
         flops=10**8,
-    )(spread, spread_other)
+    )(near, spread_other, own_out, own_dq, traded)
     deep = lambda x: x.reshape(LB, OWN, HD)
     return (
         deep(lin_out),

time: 127 us -> 123 us (0.969)
  waiting for transfers between devices: 16.2 us -> 12.1 us
  blocking collectives: 48.7 us -> 47 us
    ppermute x1, starting transfers between devices: 1.31 us -> 4.61 us  [per_device(): traded = lax.ppermute(after(traded, block), 'ctx', MIRROR)]
    ppermute x5, waiting for transfers between devices: 2.68 us -> 0.44 us  [per_device(): along = lambda x, k: lax.ppermute(x, 'head', ALONG[k])]
    all_to_all x1, blocking collectives: 22.4 us -> 20.6 us  [per_device(): got_back = lax.all_to_all(pay_back, 'ctx', 0, 0)]
    all_to_all x1, waiting for transfers between devices: 1.65 us -> 0.01 us  [per_device(): later = lax.all_to_all(suffixes, 'ctx', 0, 0).reshape(OWN * HD, HD)]
    all_to_all x1, starting transfers between devices: 4.85 us -> 3.53 us  [per_device(): later = lax.all_to_all(suffixes, 'ctx', 0, 0).reshape(OWN * HD, HD)]
    pallas_call x2 -> x3, Pallas kernels: 4.14 us -> 4.24 us  [the longest x1 2.51 us: per_device(): call(inner_kernel, [FLAT] * 3, [WIDE], count=5, flops=4 * 10 ** 9)]
  transfers between devices with their start and end apart: 12 -> 12, of which waited for: 6 -> 4; matrix products, arithmetic and copies ran while one was open for 0% -> 0% of each run, Pallas kernels for 7% -> 7%
where the time goes in v6:
time: 123 us; the launch traced here: 122 us
  blocking collectives  47 us (38%)
  starting transfers between devices  36.1 us (29%)
  Pallas kernels  26.2 us (21%)
  waiting for transfers between devices  12.1 us (10%)
    all_to_all x1, blocking collectives, per_device(): got_back = lax.all_to_all(pay_back, 'ctx', 0, 0)  20.6 us
    all_to_all x1, blocking collectives, per_device(): total = lax.all_to_all(after(sums, trade), 'head', 0, 0)  15.8 us
    pallas_call x1, Pallas kernels, per_device(): call(soft_kernel, [HALF_FLAT, HALF_FLAT, FLAT, KEY_PARTS, KEY_PARTS], [FL...  11.3 us
    all_to_all x1, blocking collectives, per_device(): state = lax.all_to_all(prefixes, 'ctx', 0, 0).reshape(OWN * HD, HD)  10.6 us
    all_to_all x1, waiting for transfers between devices, per_device(): mine = lax.all_to_all(pay, 'ctx', 0, 0)  9.81 us
    all_to_all x1, starting transfers between devices, per_device(): mine = lax.all_to_all(pay, 'ctx', 0, 0)  7.59 us
    ppermute x5, starting transfers between devices, per_device(): along = lambda x, k: lax.ppermute(x, 'head', ALONG[k])  6.59 us
    ppermute x1, starting transfers between devices, per_device(): other = lax.ppermute(after(mine, sums, trade), 'head', OTHER_CORE)  4.79 us
  transfers between devices with their start and end apart: 12, of which 4 were waited for; matrix products, arithmetic and copies ran while one was open for 0% of the time, Pallas kernels for 7%

profile of v6, /device:TPU:1, one launch (start us, length us, event | category | flops | bytes accessed | tf_op | source)
XLA Modules:
  0.0 122.3 jit_solution(13704552587946555412)
XLA Ops:
  0.6 3.5 %shard_map.170 = (bf16[16,304,128]{2,1,0:T(8,128)(2,1)}, bf16[1024,128]{1,0:T(8,128)(2,1)}) custom-call(bf16[1024,128]{1,0:T(8,128)(2,1)} %bitcast.33, bf16[1024,128]{1,0:T(8,128)(2,1)} %bitcast.35, f32[4,256]{1,0:T(4,128)} %decay_ref.6, bf16[2048,128]{1,0:T(8,128)(2,1)} %bitcast.28, bf16[2048,128]{1,0:T(8,128)(2,1)} %bitcast.29, ...), custom_call_target="tpu_custom_call" | custom-call | flops 1000000000 | bytes 1048576 | tf_op jit(solution)/shard_map/pallas_call | solution.py:433
  4.2 7.6 %all-to-all-start = ((bf16[16,304,128]{2,1,0:T(8,128)(2,1)}), bf16[16,304,128]{2,1,0:T(8,128)(2,1)S(1)}, u32[]{:S(2)}, u32[]{:S(2)}) async-start(bf16[16,304,128]{2,1,0:T(8,128)(2,1)} %get-tuple-element.43), calls=%async_computation | async-start | bytes 2490368 | tf_op jit(solution)/shard_map/all_to_all | solution.py:457
  11.8 4.7 %collective-permute-start = (bf16[1024,128]{1,0:T(8,128)(2,1)}, bf16[1024,128]{1,0:T(8,128)(2,1)S(1)}, u32[]{:S(2)}, u32[]{:S(2)}) collective-permute-start(bf16[1024,128]{1,0:T(8,128)(2,1)} %get-tuple-element.51), channel_id=1, source_target_pairs={{0,240},{16,224},{32,208},{48,192},{64,176},{80,160},{96,144},{112... | collective-permute-start | bytes 786440 | tf_op jit(solution)/shard_map/ppermute | solution.py:456
  16.5 3.0 %shard_map.171 = (f32[4,256,128]{2,1,0:T(8,128)}, bf16[3,4,256,128]{3,2,1,0:T(8,128)(2,1)}) custom-call(bf16[1024,128]{1,0:T(8,128)(2,1)} %bitcast.32, bf16[1024,128]{1,0:T(8,128)(2,1)} %bitcast.34, bf16[1024,128]{1,0:T(8,128)(2,1)} %bitcast.36, f32[4,256]{1,0:T(4,128)} %decay_ref.6), custom_call_target="tpu_custom_call" | custom-call | flops 1000000000 | bytes 1048576 | tf_op jit(solution)/shard_map/pallas_call | solution.py:453
  19.5 0.0 copy-start.6
  19.5 0.0 copy-start.7
  19.5 9.8 %all-to-all-done.got_ref.mine_ref.first_ref = bf16[16,304,128]{2,1,0:T(8,128)(2,1)S(1)} async-done(((bf16[16,304,128]{2,1,0:T(8,128)(2,1)}), bf16[16,304,128]{2,1,0:T(8,128)(2,1)S(1)}, u32[]{:S(2)}, u32[]{:S(2)}) %all-to-all-start) | async-done | bytes 1245216 | tf_op jit(solution)/shard_map/all_to_all | solution.py:457
  29.4 10.6 %all_to_all.25 = bf16[16,32,128]{2,1,0:T(8,128)(2,1)S(1)} all-to-all(bf16[16,32,128]{2,1,0:T(8,128)(2,1)S(1)} %shard_map.172), channel_id=1, replica_groups=mesh['ctx'=16,'head'=16] {'ctx'}, dimensions={0} | all-to-all | bytes 262144 | tf_op jit(solution)/shard_map/all_to_all | solution.py:461
  40.0 0.0 copy-done
  40.0 0.0 copy-done.3
  40.0 0.0 copy-done.4
  40.0 0.0 copy-done.6
  40.0 0.0 copy-done.7
  40.1 0.0 copy-start.1
  40.1 0.0 copy-start.2
  40.1 0.0 copy-start.5
  40.1 1.2 %shard_map.173 = (f32[4,256,128]{2,1,0:T(8,128)S(1)}, f32[4,256,128]{2,1,0:T(8,128)S(1)}, f32[16,4,128]{2,1,0:T(4,128)S(1)}) custom-call(f32[4,256,128]{2,1,0:T(8,128)S(1)} %copy-done.7, bf16[3,4,256,128]{3,2,1,0:T(8,128)(2,1)S(1)} %copy-done.6, bf16[512,128]{1,0:T(8,128)(2,1)S(1)} %bitcast.19, f32[4,256]{1,0:T(4,128)S(1)} %copy-done.3, ...), custom_call_target="tpu_custom_call" | custom-call | flops 1000000000 | bytes 1048576 | tf_op jit(solution)/shard_map/pallas_call | solution.py:462
  41.3 0.0 collective-permute-done.trade_ref
  41.4 4.8 %collective-permute-start.1 = (bf16[16,304,128]{2,1,0:T(8,128)(2,1)S(1)}, bf16[16,304,128]{2,1,0:T(8,128)(2,1)S(1)}, u32[]{:S(2)}, u32[]{:S(2)}) collective-permute-start(bf16[16,304,128]{2,1,0:T(8,128)(2,1)S(1)} %all-to-all-done.got_ref.mine_ref.first_ref), channel_id=1, source_target_pairs={{0,1},{1,0},{2,3},{3,2},{4,5},{5,4},{6,7},{7,6},{8,9},{9,8},{10,11... | collective-permute-start | bytes 3735560 | tf_op jit(solution)/shard_map/ppermute | solution.py:469
  46.2 15.8 %all_to_all.26.got_ref = f32[16,4,128]{2,1,0:T(4,128)S(1)} all-to-all(f32[16,4,128]{2,1,0:T(4,128)S(1)} %get-tuple-element.52), channel_id=1, replica_groups=mesh['ctx'=16,'head'=16] {'head'}, dimensions={0} | all-to-all | bytes 65536 | tf_op jit(solution)/shard_map/all_to_all | solution.py:470
  61.9 0.0 collective-permute-done.1.other_ref
  61.9 0.0 copy-done.2
  61.9 11.3 %shard_map.174 = (bf16[512,128]{1,0:T(8,128)(2,1)S(1)}, bf16[512,128]{1,0:T(8,128)(2,1)S(1)}, bf16[1024,128]{1,0:T(8,128)(2,1)S(1)}, bf16[16,256,128]{2,1,0:T(8,128)(2,1)S(1)}, bf16[16,256,128]{2,1,0:T(8,128)(2,1)S(1)}) custom-call(s32[32]{0:T(128)S(1)} %copy-done.5, bf16[1024,128]{1,0:T(8,128)(2,1)S(1)} %bitcast.25, bf16[1024,128]{1,0:T(8,128)(2,1)S(1)} %bitcast.27, ...), custom_call_target="tpu_custom_call" | custom-call | flops 10000000000 | bytes 1048576 | tf_op jit(solution)/shard_map/pallas_call | solution.py:471
  73.3 0.7 collective-permute-start.2
  73.9 1.7 %shard_map.175 = (bf16[1024,128]{1,0:T(8,128)(2,1)}, bf16[4,256,128]{2,1,0:T(8,128)(2,1)S(1)}, bf16[512,128]{1,0:T(8,128)(2,1)S(1)}) custom-call(f32[4,256,128]{2,1,0:T(8,128)S(1)} %get-tuple-element.48.att_ref, f32[4,256,128]{2,1,0:T(8,128)S(1)} %get-tuple-element.49.up_ref, f32[16,4,128]{2,1,0:T(4,128)S(1)} %all_to_all.26.got_ref, ...), custom_call_target="tpu_custom_call" | custom-call | flops 2000000000 | bytes 1048576 | tf_op jit(solution)/shard_map/pallas_call | solution.py:491
  75.7 0.5 collective-permute-done.2.got_ref
  76.2 0.2 shard_map.176
  76.5 20.6 %all_to_all.27.got_ref = bf16[16,288,128]{2,1,0:T(8,128)(2,1)S(1)} all-to-all(bf16[16,288,128]{2,1,0:T(8,128)(2,1)S(1)} %shard_map.176), channel_id=1, replica_groups=mesh['ctx'=16,'head'=16] {'ctx'}, dimensions={0} | all-to-all | bytes 2359296 | tf_op jit(solution)/shard_map/all_to_all | solution.py:501
  97.1 0.7 shard_map.177
  97.8 3.5 %all-to-all-start.4 = ((bf16[16,32,128]{2,1,0:T(8,128)(2,1)}), bf16[16,32,128]{2,1,0:T(8,128)(2,1)S(1)}, u32[]{:S(2)}, u32[]{:S(2)}) async-start(bf16[16,32,128]{2,1,0:T(8,128)(2,1)} %get-tuple-element.62), calls=%async_computation.4 | async-start | bytes 262144 | tf_op jit(solution)/shard_map/all_to_all | solution.py:507
  101.4 0.4 collective-permute-start.5
  101.8 2.0 %collective-permute-start.4 = (bf16[256,128]{1,0:T(8,128)(2,1)S(1)}, bf16[256,128]{1,0:T(8,128)(2,1)S(1)}, u32[]{:S(2)}, u32[]{:S(2)}) collective-permute-start(bf16[256,128]{1,0:T(8,128)(2,1)S(1)} %get-tuple-element.69.own_ref), channel_id=1, source_target_pairs={{0,4},{1,5},{2,6},{3,7},{4,8},{5,9},{6,10},{7,11},{8,12},{9,13},{1... | collective-permute-start | bytes 196616 | tf_op jit(solution)/shard_map/ppermute | solution.py:505
  103.8 1.3 %collective-permute-start.6 = (bf16[256,128]{1,0:T(8,128)(2,1)S(1)}, bf16[256,128]{1,0:T(8,128)(2,1)S(1)}, u32[]{:S(2)}, u32[]{:S(2)}) collective-permute-start(bf16[256,128]{1,0:T(8,128)(2,1)S(1)} %get-tuple-element.69.own_ref), channel_id=1, source_target_pairs={{0,8},{1,9},{2,10},{3,11},{4,12},{5,13},{6,14},{7,15},{8,0},{9,1},... | collective-permute-start | bytes 196616 | tf_op jit(solution)/shard_map/ppermute | solution.py:505
  105.1 4.6 %collective-permute-start.3 = (bf16[1024,128]{1,0:T(8,128)(2,1)S(1)}, bf16[1024,128]{1,0:T(8,128)(2,1)S(1)}, u32[]{:S(2)}, u32[]{:S(2)}) collective-permute-start(bf16[1024,128]{1,0:T(8,128)(2,1)S(1)} %get-tuple-element.68), channel_id=1, source_target_pairs={{0,240},{16,224},{32,208},{48,192},{64,176},{80,160},{96,144},{112... | collective-permute-start | bytes 786440 | tf_op jit(solution)/shard_map/ppermute | solution.py:510
  109.7 0.0 collective-permute-done.5.above_ref
  109.7 0.0 all-to-all-done.4
  109.7 0.0 collective-permute-done.4.below_ref
  109.7 0.5 collective-permute-start.7
  110.2 2.4 %collective-permute-start.8 = (bf16[512,128]{1,0:T(8,128)(2,1)S(1)}, bf16[512,128]{1,0:T(8,128)(2,1)S(1)}, u32[]{:S(2)}, u32[]{:S(2)}) collective-permute-start(bf16[512,128]{1,0:T(8,128)(2,1)S(1)} %get-tuple-element.72), channel_id=1, source_target_pairs={{0,14},{1,15},{2,0},{3,1},{4,2},{5,3},{6,4},{7,5},{8,6},{9,7},{10,... | collective-permute-start | bytes 393224 | tf_op jit(solution)/shard_map/ppermute | solution.py:505
  112.6 2.5 %shard_map.178 = (bf16[1024,128]{1,0:T(8,128)(2,1)}, bf16[1024,128]{1,0:T(8,128)(2,1)}, bf16[1024,128]{1,0:T(8,128)(2,1)}) custom-call(bf16[3,4,256,128]{3,2,1,0:T(8,128)(2,1)S(1)} %copy-done.6, bf16[4,256,128]{2,1,0:T(8,128)(2,1)S(1)} %get-tuple-element.58.ag_ref, bf16[512,128]{1,0:T(8,128)(2,1)S(1)} %bitcast.20, bf16[512,128]{1,0:T(8,128)(2,1)S(1)} %bitcast.21, ...), custom_call_target="tpu_custom_call" | custom-call | flops 4000000000 | bytes 1048576 | tf_op jit(solution)/shard_map/pallas_call | solution.py:511
  115.1 0.0 collective-permute-done.3.traded_ref
  115.1 0.0 collective-permute-done.6.far_ref
  115.1 0.4 collective-permute-done.7.up_ref
  115.6 0.0 collective-permute-done.8.down_ref
  115.6 3.7 %collective-permute-start.9 = (bf16[8,256,128]{2,1,0:T(8,128)(2,1)S(1)}, bf16[8,256,128]{2,1,0:T(8,128)(2,1)S(1)}, u32[]{:S(2)}, u32[]{:S(2)}) collective-permute-start(bf16[8,256,128]{2,1,0:T(8,128)(2,1)S(1)} %shard_map.180.mine_ref), channel_id=1, source_target_pairs={{0,1},{1,0},{2,3},{3,2},{4,5},{5,4},{6,7},{7,6},{8,9},{9,8},{10,11... | collective-permute-start | bytes 1572872 | tf_op jit(solution)/shard_map/ppermute | solution.py:517
  119.3 0.3 shard_map.181.near_ref
  119.6 1.2 %collective-permute-done.9.other_ref = bf16[8,256,128]{2,1,0:T(8,128)(2,1)S(1)} collective-permute-done((bf16[8,256,128]{2,1,0:T(8,128)(2,1)S(1)}, bf16[8,256,128]{2,1,0:T(8,128)(2,1)S(1)}, u32[]{:S(2)}, u32[]{:S(2)}) %collective-permute-start.9) | collective-permute-done | bytes 524320 | tf_op jit(solution)/shard_map/ppermute | solution.py:517
  120.8 1.4 %shard_map.182 = (bf16[2048,128]{1,0:T(8,128)(2,1)}, bf16[2048,128]{1,0:T(8,128)(2,1)}, bf16[1024,128]{1,0:T(8,128)(2,1)}, bf16[1024,128]{1,0:T(8,128)(2,1)}) custom-call(bf16[2,1024,128]{2,1,0:T(8,128)(2,1)S(1)} %shard_map.181.near_ref, bf16[8,256,128]{2,1,0:T(8,128)(2,1)S(1)} %collective-permute-done.9.other_ref, ...), custom_call_target="tpu_custom_call" | custom-call | flops 100000000 | bytes 1048576 | tf_op jit(solution)/shard_map/pallas_call | solution.py:525
  (8 shorter events, 0.1 us)
Async XLA Ops:
  4.2 25.2 %all-to-all-start = ((bf16[16,304,128]{2,1,0:T(8,128)(2,1)}), bf16[16,304,128]{2,1,0:T(8,128)(2,1)S(1)}, u32[]{:S(2)}, u32[]{:S(2)}) async-start(bf16[16,304,128]{2,1,0:T(8,128)(2,1)} %get-tuple-element.43), calls=%async_computation | async-start | bytes 2490368 | tf_op jit(solution)/shard_map/all_to_all | solution.py:457
  11.8 29.6 %collective-permute-start = (bf16[1024,128]{1,0:T(8,128)(2,1)}, bf16[1024,128]{1,0:T(8,128)(2,1)S(1)}, u32[]{:S(2)}, u32[]{:S(2)}) collective-permute-start(bf16[1024,128]{1,0:T(8,128)(2,1)} %get-tuple-element.51), channel_id=1, source_target_pairs={{0,240},{16,224},{32,208},{48,192},{64,176},{80,160},{96,144},{112... | collective-permute-start | bytes 786440 | tf_op jit(solution)/shard_map/ppermute | solution.py:456
  19.5 20.5 %copy-start = (bf16[256,4,128]{2,1,0:T(4,128)(2,1)S(1)}, bf16[256,4,128]{2,1,0:T(4,128)(2,1)}, u32[]{:S(2)}) copy-start(bf16[256,4,128]{2,1,0:T(4,128)(2,1)} %param.16) | copy-start | bytes 786436
  19.5 20.5 %copy-start.3 = (f32[4,256]{1,0:T(4,128)S(1)}, f32[4,256]{1,0:T(4,128)}, u32[]{:S(2)}) copy-start(f32[4,256]{1,0:T(4,128)} %decay_ref.6) | copy-start | bytes 12292
  19.5 20.5 %copy-start.4 = (f32[4,128]{1,0:T(4,128)S(1)}, f32[4,128]{1,0:T(4,128)}, u32[]{:S(2)}) copy-start(f32[4,128]{1,0:T(4,128)} %gain_ref.2) | copy-start | bytes 6148
  19.5 20.5 %copy-start.6 = (bf16[3,4,256,128]{3,2,1,0:T(8,128)(2,1)S(1)}, bf16[3,4,256,128]{3,2,1,0:T(8,128)(2,1)}, u32[]{:S(2)}) copy-start(bf16[3,4,256,128]{3,2,1,0:T(8,128)(2,1)} %get-tuple-element.46.heads_ref) | copy-start | bytes 2359300
  19.5 20.5 %copy-start.7 = (f32[4,256,128]{2,1,0:T(8,128)S(1)}, f32[4,256,128]{2,1,0:T(8,128)}, u32[]{:S(2)}) copy-start(f32[4,256,128]{2,1,0:T(8,128)} %get-tuple-element.45.within_ref) | copy-start | bytes 1572868
  40.1 21.9 %copy-start.1 = (bf16[256,4,128]{2,1,0:T(4,128)(2,1)S(1)}, bf16[256,4,128]{2,1,0:T(4,128)(2,1)}, u32[]{:S(2)}) copy-start(bf16[256,4,128]{2,1,0:T(4,128)(2,1)} %param.17) | copy-start | bytes 786436
  40.1 21.9 %copy-start.2 = (bf16[256,4,128]{2,1,0:T(4,128)(2,1)S(1)}, bf16[256,4,128]{2,1,0:T(4,128)(2,1)}, u32[]{:S(2)}) copy-start(bf16[256,4,128]{2,1,0:T(4,128)(2,1)} %param.20) | copy-start | bytes 786436
  40.1 21.9 %copy-start.5 = (s32[32]{0:T(128)S(1)}, s32[32]{0:T(128)}, u32[]{:S(2)}) copy-start(s32[32]{0:T(128)} %reach_ref.1) | copy-start | bytes 388
  41.4 20.6 %collective-permute-start.1 = (bf16[16,304,128]{2,1,0:T(8,128)(2,1)S(1)}, bf16[16,304,128]{2,1,0:T(8,128)(2,1)S(1)}, u32[]{:S(2)}, u32[]{:S(2)}) collective-permute-start(bf16[16,304,128]{2,1,0:T(8,128)(2,1)S(1)} %all-to-all-done.got_ref.mine_ref.first_ref), channel_id=1, source_target_pairs={{0,1},{1,0},{2,3},{3,2},{4,5},{5,4},{6,7},{7,6},{8,9},{9,8},{10,11... | collective-permute-start | bytes 3735560 | tf_op jit(solution)/shard_map/ppermute | solution.py:469
  73.3 3.0 %collective-permute-start.2 = (bf16[16,256,128]{2,1,0:T(8,128)(2,1)S(1)}, bf16[16,256,128]{2,1,0:T(8,128)(2,1)S(1)}, u32[]{:S(2)}, u32[]{:S(2)}) collective-permute-start(bf16[16,256,128]{2,1,0:T(8,128)(2,1)S(1)} %get-tuple-element.60), channel_id=1, source_target_pairs={{0,1},{1,0},{2,3},{3,2},{4,5},{5,4},{6,7},{7,6},{8,9},{9,8},{10,11... | collective-permute-start | bytes 3145736 | tf_op jit(solution)/shard_map/ppermute | solution.py:490
  97.8 11.9 %all-to-all-start.4 = ((bf16[16,32,128]{2,1,0:T(8,128)(2,1)}), bf16[16,32,128]{2,1,0:T(8,128)(2,1)S(1)}, u32[]{:S(2)}, u32[]{:S(2)}) async-start(bf16[16,32,128]{2,1,0:T(8,128)(2,1)} %get-tuple-element.62), calls=%async_computation.4 | async-start | bytes 262144 | tf_op jit(solution)/shard_map/all_to_all | solution.py:507
  101.4 8.3 %collective-permute-start.5 = (bf16[256,128]{1,0:T(8,128)(2,1)S(1)}, bf16[256,128]{1,0:T(8,128)(2,1)S(1)}, u32[]{:S(2)}, u32[]{:S(2)}) collective-permute-start(bf16[256,128]{1,0:T(8,128)(2,1)S(1)} %get-tuple-element.69.own_ref), channel_id=1, source_target_pairs={{0,12},{1,13},{2,14},{3,15},{4,0},{5,1},{6,2},{7,3},{8,4},{9,5},{1... | collective-permute-start | bytes 196616 | tf_op jit(solution)/shard_map/ppermute | solution.py:505
  101.8 7.9 %collective-permute-start.4 = (bf16[256,128]{1,0:T(8,128)(2,1)S(1)}, bf16[256,128]{1,0:T(8,128)(2,1)S(1)}, u32[]{:S(2)}, u32[]{:S(2)}) collective-permute-start(bf16[256,128]{1,0:T(8,128)(2,1)S(1)} %get-tuple-element.69.own_ref), channel_id=1, source_target_pairs={{0,4},{1,5},{2,6},{3,7},{4,8},{5,9},{6,10},{7,11},{8,12},{9,13},{1... | collective-permute-start | bytes 196616 | tf_op jit(solution)/shard_map/ppermute | solution.py:505
  103.8 11.3 %collective-permute-start.6 = (bf16[256,128]{1,0:T(8,128)(2,1)S(1)}, bf16[256,128]{1,0:T(8,128)(2,1)S(1)}, u32[]{:S(2)}, u32[]{:S(2)}) collective-permute-start(bf16[256,128]{1,0:T(8,128)(2,1)S(1)} %get-tuple-element.69.own_ref), channel_id=1, source_target_pairs={{0,8},{1,9},{2,10},{3,11},{4,12},{5,13},{6,14},{7,15},{8,0},{9,1},... | collective-permute-start | bytes 196616 | tf_op jit(solution)/shard_map/ppermute | solution.py:505
  105.1 10.1 %collective-permute-start.3 = (bf16[1024,128]{1,0:T(8,128)(2,1)S(1)}, bf16[1024,128]{1,0:T(8,128)(2,1)S(1)}, u32[]{:S(2)}, u32[]{:S(2)}) collective-permute-start(bf16[1024,128]{1,0:T(8,128)(2,1)S(1)} %get-tuple-element.68), channel_id=1, source_target_pairs={{0,240},{16,224},{32,208},{48,192},{64,176},{80,160},{96,144},{112... | collective-permute-start | bytes 786440 | tf_op jit(solution)/shard_map/ppermute | solution.py:510
  109.7 5.8 %collective-permute-start.7 = (bf16[512,128]{1,0:T(8,128)(2,1)S(1)}, bf16[512,128]{1,0:T(8,128)(2,1)S(1)}, u32[]{:S(2)}, u32[]{:S(2)}) collective-permute-start(bf16[512,128]{1,0:T(8,128)(2,1)S(1)} %get-tuple-element.71), channel_id=1, source_target_pairs={{0,2},{1,3},{2,4},{3,5},{4,6},{5,7},{6,8},{7,9},{8,10},{9,11},{10,... | collective-permute-start | bytes 393224 | tf_op jit(solution)/shard_map/ppermute | solution.py:505
  110.2 5.3 %collective-permute-start.8 = (bf16[512,128]{1,0:T(8,128)(2,1)S(1)}, bf16[512,128]{1,0:T(8,128)(2,1)S(1)}, u32[]{:S(2)}, u32[]{:S(2)}) collective-permute-start(bf16[512,128]{1,0:T(8,128)(2,1)S(1)} %get-tuple-element.72), channel_id=1, source_target_pairs={{0,14},{1,15},{2,0},{3,1},{4,2},{5,3},{6,4},{7,5},{8,6},{9,7},{10,... | collective-permute-start | bytes 393224 | tf_op jit(solution)/shard_map/ppermute | solution.py:505
  115.6 5.2 %collective-permute-start.9 = (bf16[8,256,128]{2,1,0:T(8,128)(2,1)S(1)}, bf16[8,256,128]{2,1,0:T(8,128)(2,1)S(1)}, u32[]{:S(2)}, u32[]{:S(2)}) collective-permute-start(bf16[8,256,128]{2,1,0:T(8,128)(2,1)S(1)} %shard_map.180.mine_ref), channel_id=1, source_target_pairs={{0,1},{1,0},{2,3},{3,2},{4,5},{5,4},{6,7},{7,6},{8,9},{9,8},{10,11... | collective-permute-start | bytes 1572872 | tf_op jit(solution)/shard_map/ppermute | solution.py:517

commit v7 on v6

--- a/solution.py
+++ b/solution.py
@@ -55,13 +55,16 @@
     target[...] = scratch[...].astype(bf16)
 
 
+def to_columns(rows):
+    return jnp.concatenate([rows, jnp.zeros((HD - rows.shape[0], LB), f32)], axis=0).T
+
+
 def run_sums(log_decay):
     row = lax.broadcasted_iota(jnp.int32, (LB, LB), 0)
     col = lax.broadcasted_iota(jnp.int32, (LB, LB), 1)
     upto = (row <= col).astype(f32)
     as_rows = dot(log_decay, upto, NN, PRECISE)
-    as_cols = dot((row >= col).astype(f32), log_decay, NT, PRECISE)
-    return as_rows, as_cols, row, col
+    return as_rows, to_columns(as_rows), row, col
 
 
 def local_kernel(
@@ -172,11 +175,9 @@
     for j in range(1, HEADS):
         total = total + got_ref[j]
     wide = jnp.concatenate(
-        [jnp.concatenate([total[n : n + 1], total[n + 1 : n + 2]], axis=1) for n in (0, 2)]
-        + [jnp.zeros((6, LB), f32)],
-        axis=0,
-    )
-    cols = dot((row == col).astype(f32), wide, NT, PRECISE)
+        [jnp.concatenate([total[n : n + 1], total[n + 1 : n + 2]], axis=1) for n in (0, 2)], axis=0
+    )
+    cols = to_columns(wide)
     inverse = lax.rsqrt(cols[:, 0:1] / (HEAD_TOTAL * HD) + EPSILON)
     pull = inverse * inverse * inverse * (cols[:, 1:2] / (HEAD_TOTAL * HD))
     outs = []
@@ -373,20 +374,18 @@
     return filled
 
 
-def near_kernel(mine_ref, rows_ref, scratch):
+def near_kernel(mine_ref, out_ref, sdq_ref, traded_ref, rows_ref, soft_out_ref, soft_dq_ref, scratch):
+    for n, (own, target) in enumerate(((out_ref, soft_out_ref), (sdq_ref, soft_dq_ref))):
+        target[0 : ROWS // 2] = own[...]
+        target[ROWS // 2 :] = traded_ref[n * (ROWS // 2) : (n + 1) * (ROWS // 2)]
     for part, rows in enumerate(fill_rows(mine_ref, scratch)):
         rows_ref[part] = rows
 
 
-def spread_kernel(
-    near_ref, other_ref, out_ref, sdq_ref, traded_ref, dk_ref, dv_ref, soft_out_ref, soft_dq_ref, scratch
-):
+def spread_kernel(near_ref, other_ref, dk_ref, dv_ref, scratch):
     side = lax.axis_index("head") % 2
     here = pl.ds(pl.multiple_of(side * (HALF * KVH), HALF * KVH), HALF * KVH)
     there = pl.ds(pl.multiple_of((1 - side) * (HALF * KVH), HALF * KVH), HALF * KVH)
-    for n, (own, target) in enumerate(((out_ref, soft_out_ref), (sdq_ref, soft_dq_ref))):
-        target[0 : ROWS // 2] = own[...]
-        target[ROWS // 2 :] = traded_ref[n * (ROWS // 2) : (n + 1) * (ROWS // 2)]
     for part, rows in enumerate(fill_rows(other_ref, scratch)):
         target = (dk_ref, dv_ref)[part]
         target[here, :] = near_ref[part]
@@ -515,20 +514,20 @@
         after(block, lin_dk, traded), below, above, far, up, down
     )
     spread_other = lax.ppermute(spread, "head", OTHER_CORE)
-    (near,) = call(
+    near, soft_out, soft_dq = call(
         near_kernel,
-        [((2, HALF * KVH, HD), bf16)],
+        [((2, HALF * KVH, HD), bf16), FLAT, FLAT],
         [((HALF * KVH, HD), f32)],
-        count=1,
+        count=4,
         flops=10**8,
-    )(spread)
-    soft_dk, soft_dv, soft_out, soft_dq = call(
+    )(spread, own_out, own_dq, traded)
+    soft_dk, soft_dv = call(
         spread_kernel,
-        [((LB * KVH, HD), bf16), ((LB * KVH, HD), bf16), FLAT, FLAT],
+        [((LB * KVH, HD), bf16), ((LB * KVH, HD), bf16)],
         [((HALF * KVH, HD), f32)],
-        count=5,
+        count=2,
         flops=10**8,
-    )(near, spread_other, own_out, own_dq, traded)
+    )(near, spread_other)
     deep = lambda x: x.reshape(LB, OWN, HD)
     return (
         deep(lin_out),

time: 123 us -> 124 us (level)
  no operation moved by 1% of the time
where the time goes in v7:
time: 124 us; the launch traced here: 123 us
  blocking collectives  47.7 us (38%)
  starting transfers between devices  36.4 us (29%)
  Pallas kernels  26 us (21%)
  waiting for transfers between devices  11.8 us (10%)
    all_to_all x1, blocking collectives, per_device(): got_back = lax.all_to_all(pay_back, 'ctx', 0, 0)  21.3 us
    all_to_all x1, blocking collectives, per_device(): total = lax.all_to_all(after(sums, trade), 'head', 0, 0)  15.8 us
    pallas_call x1, Pallas kernels, per_device(): call(soft_kernel, [HALF_FLAT, HALF_FLAT, FLAT, KEY_PARTS, KEY_PARTS], [FL...  11.3 us
    all_to_all x1, blocking collectives, per_device(): state = lax.all_to_all(prefixes, 'ctx', 0, 0).reshape(OWN * HD, HD)  10.6 us
    all_to_all x1, waiting for transfers between devices, per_device(): mine = lax.all_to_all(pay, 'ctx', 0, 0)  9.68 us
    all_to_all x1, starting transfers between devices, per_device(): mine = lax.all_to_all(pay, 'ctx', 0, 0)  7.73 us
    ppermute x5, starting transfers between devices, per_device(): along = lambda x, k: lax.ppermute(x, 'head', ALONG[k])  6.59 us
    ppermute x1, starting transfers between devices, per_device(): other = lax.ppermute(after(mine, sums, trade), 'head', OTHER_CORE)  4.79 us
  transfers between devices with their start and end apart: 12, of which 4 were waited for; matrix products, arithmetic and copies ran while one was open for 0% of the time, Pallas kernels for 7%

profile of v7, /device:TPU:1, one launch (start us, length us, event | category | flops | bytes accessed | tf_op | source)
XLA Modules:
  0.0 122.7 jit_solution(18374091809576306749)
XLA Ops:
  0.6 3.4 %shard_map.170 = (bf16[16,304,128]{2,1,0:T(8,128)(2,1)}, bf16[1024,128]{1,0:T(8,128)(2,1)}) custom-call(bf16[1024,128]{1,0:T(8,128)(2,1)} %bitcast.33, bf16[1024,128]{1,0:T(8,128)(2,1)} %bitcast.35, f32[4,256]{1,0:T(4,128)} %decay_ref.6, bf16[2048,128]{1,0:T(8,128)(2,1)} %bitcast.28, bf16[2048,128]{1,0:T(8,128)(2,1)} %bitcast.29, ...), custom_call_target="tpu_custom_call" | custom-call | flops 1000000000 | bytes 1048576 | tf_op jit(solution)/shard_map/pallas_call | solution.py:432
  4.1 0.0 copy-start.8
  4.1 7.7 %all-to-all-start = ((bf16[16,304,128]{2,1,0:T(8,128)(2,1)}), bf16[16,304,128]{2,1,0:T(8,128)(2,1)S(1)}, u32[]{:S(2)}, u32[]{:S(2)}) async-start(bf16[16,304,128]{2,1,0:T(8,128)(2,1)} %get-tuple-element.44), calls=%async_computation | async-start | bytes 2490368 | tf_op jit(solution)/shard_map/all_to_all | solution.py:456
  11.8 0.0 copy-done.8
  11.8 4.8 %collective-permute-start = (bf16[1024,128]{1,0:T(8,128)(2,1)S(1)}, bf16[1024,128]{1,0:T(8,128)(2,1)S(1)}, u32[]{:S(2)}, u32[]{:S(2)}) collective-permute-start(bf16[1024,128]{1,0:T(8,128)(2,1)S(1)} %copy-done.8), channel_id=1, source_target_pairs={{0,240},{16,224},{32,208},{48,192},{64,176},{80,160},{96,144},{112... | collective-permute-start | bytes 786440 | tf_op jit(solution)/shard_map/ppermute | solution.py:455
  16.6 3.1 %shard_map.171 = (f32[4,256,128]{2,1,0:T(8,128)}, bf16[3,4,256,128]{3,2,1,0:T(8,128)(2,1)}) custom-call(bf16[1024,128]{1,0:T(8,128)(2,1)} %bitcast.32, bf16[1024,128]{1,0:T(8,128)(2,1)} %bitcast.34, bf16[1024,128]{1,0:T(8,128)(2,1)} %bitcast.36, f32[4,256]{1,0:T(4,128)} %decay_ref.6), custom_call_target="tpu_custom_call" | custom-call | flops 1000000000 | bytes 1048576 | tf_op jit(solution)/shard_map/pallas_call | solution.py:452
  19.7 0.0 copy-start.6
  19.7 0.0 copy-start.7
  19.7 9.7 %all-to-all-done.got_ref.mine_ref.first_ref = bf16[16,304,128]{2,1,0:T(8,128)(2,1)S(1)} async-done(((bf16[16,304,128]{2,1,0:T(8,128)(2,1)}), bf16[16,304,128]{2,1,0:T(8,128)(2,1)S(1)}, u32[]{:S(2)}, u32[]{:S(2)}) %all-to-all-start) | async-done | bytes 1245216 | tf_op jit(solution)/shard_map/all_to_all | solution.py:456
  29.5 10.6 %all_to_all.25 = bf16[16,32,128]{2,1,0:T(8,128)(2,1)S(1)} all-to-all(bf16[16,32,128]{2,1,0:T(8,128)(2,1)S(1)} %shard_map.172), channel_id=1, replica_groups=mesh['ctx'=16,'head'=16] {'ctx'}, dimensions={0} | all-to-all | bytes 262144 | tf_op jit(solution)/shard_map/all_to_all | solution.py:460
  40.1 0.0 copy-done
  40.1 0.0 copy-done.3
  40.1 0.0 copy-done.4
  40.1 0.0 copy-start.1
  40.1 0.0 copy-start.2
  40.1 0.0 copy-start.5
  40.2 1.1 shard_map.173
  41.3 0.0 collective-permute-done.trade_ref
  41.3 4.8 %collective-permute-start.1 = (bf16[16,304,128]{2,1,0:T(8,128)(2,1)S(1)}, bf16[16,304,128]{2,1,0:T(8,128)(2,1)S(1)}, u32[]{:S(2)}, u32[]{:S(2)}) collective-permute-start(bf16[16,304,128]{2,1,0:T(8,128)(2,1)S(1)} %all-to-all-done.got_ref.mine_ref.first_ref), channel_id=1, source_target_pairs={{0,1},{1,0},{2,3},{3,2},{4,5},{5,4},{6,7},{7,6},{8,9},{9,8},{10,11... | collective-permute-start | bytes 3735560 | tf_op jit(solution)/shard_map/ppermute | solution.py:468
  46.1 15.8 %all_to_all.26.got_ref = f32[16,4,128]{2,1,0:T(4,128)S(1)} all-to-all(f32[16,4,128]{2,1,0:T(4,128)S(1)} %get-tuple-element.53), channel_id=1, replica_groups=mesh['ctx'=16,'head'=16] {'head'}, dimensions={0} | all-to-all | bytes 65536 | tf_op jit(solution)/shard_map/all_to_all | solution.py:469
  61.8 0.0 collective-permute-done.1.other_ref
  61.8 0.0 copy-done.5
  61.9 11.3 %shard_map.174 = (bf16[512,128]{1,0:T(8,128)(2,1)S(1)}, bf16[512,128]{1,0:T(8,128)(2,1)S(1)}, bf16[1024,128]{1,0:T(8,128)(2,1)S(1)}, bf16[16,256,128]{2,1,0:T(8,128)(2,1)S(1)}, bf16[16,256,128]{2,1,0:T(8,128)(2,1)S(1)}) custom-call(s32[32]{0:T(128)S(1)} %copy-done.5, bf16[1024,128]{1,0:T(8,128)(2,1)S(1)} %bitcast.25, bf16[1024,128]{1,0:T(8,128)(2,1)S(1)} %bitcast.27, ...), custom_call_target="tpu_custom_call" | custom-call | flops 10000000000 | bytes 1048576 | tf_op jit(solution)/shard_map/pallas_call | solution.py:470
  73.2 0.7 collective-permute-start.2
  73.9 1.1 shard_map.175
  75.0 1.1 collective-permute-done.2.got_ref
  76.1 0.2 shard_map.176
  76.4 21.3 %all_to_all.27.got_ref = bf16[16,288,128]{2,1,0:T(8,128)(2,1)S(1)} all-to-all(bf16[16,288,128]{2,1,0:T(8,128)(2,1)S(1)} %shard_map.176), channel_id=1, replica_groups=mesh['ctx'=16,'head'=16] {'ctx'}, dimensions={0} | all-to-all | bytes 2359296 | tf_op jit(solution)/shard_map/all_to_all | solution.py:500
  97.7 0.7 shard_map.177
  98.4 3.5 %all-to-all-start.4 = ((bf16[16,32,128]{2,1,0:T(8,128)(2,1)}), bf16[16,32,128]{2,1,0:T(8,128)(2,1)S(1)}, u32[]{:S(2)}, u32[]{:S(2)}) async-start(bf16[16,32,128]{2,1,0:T(8,128)(2,1)} %get-tuple-element.63), calls=%async_computation.4 | async-start | bytes 262144 | tf_op jit(solution)/shard_map/all_to_all | solution.py:506
  101.9 0.4 collective-permute-start.5
  102.3 2.0 %collective-permute-start.4 = (bf16[256,128]{1,0:T(8,128)(2,1)S(1)}, bf16[256,128]{1,0:T(8,128)(2,1)S(1)}, u32[]{:S(2)}, u32[]{:S(2)}) collective-permute-start(bf16[256,128]{1,0:T(8,128)(2,1)S(1)} %get-tuple-element.70.own_ref), channel_id=1, source_target_pairs={{0,4},{1,5},{2,6},{3,7},{4,8},{5,9},{6,10},{7,11},{8,12},{9,13},{1... | collective-permute-start | bytes 196616 | tf_op jit(solution)/shard_map/ppermute | solution.py:504
  104.4 1.3 %collective-permute-start.6 = (bf16[256,128]{1,0:T(8,128)(2,1)S(1)}, bf16[256,128]{1,0:T(8,128)(2,1)S(1)}, u32[]{:S(2)}, u32[]{:S(2)}) collective-permute-start(bf16[256,128]{1,0:T(8,128)(2,1)S(1)} %get-tuple-element.70.own_ref), channel_id=1, source_target_pairs={{0,8},{1,9},{2,10},{3,11},{4,12},{5,13},{6,14},{7,15},{8,0},{9,1},... | collective-permute-start | bytes 196616 | tf_op jit(solution)/shard_map/ppermute | solution.py:504
  105.6 4.6 %collective-permute-start.3 = (bf16[1024,128]{1,0:T(8,128)(2,1)S(1)}, bf16[1024,128]{1,0:T(8,128)(2,1)S(1)}, u32[]{:S(2)}, u32[]{:S(2)}) collective-permute-start(bf16[1024,128]{1,0:T(8,128)(2,1)S(1)} %get-tuple-element.69), channel_id=1, source_target_pairs={{0,240},{16,224},{32,208},{48,192},{64,176},{80,160},{96,144},{112... | collective-permute-start | bytes 786440 | tf_op jit(solution)/shard_map/ppermute | solution.py:509
  110.2 0.0 collective-permute-done.5.above_ref
  110.2 0.0 all-to-all-done.4
  110.2 0.0 collective-permute-done.4.below_ref
  110.3 0.5 collective-permute-start.7
  110.8 2.4 %collective-permute-start.8 = (bf16[512,128]{1,0:T(8,128)(2,1)S(1)}, bf16[512,128]{1,0:T(8,128)(2,1)S(1)}, u32[]{:S(2)}, u32[]{:S(2)}) collective-permute-start(bf16[512,128]{1,0:T(8,128)(2,1)S(1)} %get-tuple-element.73), channel_id=1, source_target_pairs={{0,14},{1,15},{2,0},{3,1},{4,2},{5,3},{6,4},{7,5},{8,6},{9,7},{10,... | collective-permute-start | bytes 393224 | tf_op jit(solution)/shard_map/ppermute | solution.py:504
  113.2 2.6 %shard_map.178 = (bf16[1024,128]{1,0:T(8,128)(2,1)}, bf16[1024,128]{1,0:T(8,128)(2,1)}, bf16[1024,128]{1,0:T(8,128)(2,1)}) custom-call(bf16[3,4,256,128]{3,2,1,0:T(8,128)(2,1)S(1)} %copy-done.6, bf16[4,256,128]{2,1,0:T(8,128)(2,1)S(1)} %get-tuple-element.59.ag_ref, bf16[512,128]{1,0:T(8,128)(2,1)S(1)} %bitcast.20, bf16[512,128]{1,0:T(8,128)(2,1)S(1)} %bitcast.21, ...), custom_call_target="tpu_custom_call" | custom-call | flops 4000000000 | bytes 1048576 | tf_op jit(solution)/shard_map/pallas_call | solution.py:510
  115.7 0.0 collective-permute-done.3.traded_ref
  115.7 0.0 collective-permute-done.6.far_ref
  115.7 0.4 collective-permute-done.7.up_ref
  116.1 0.0 collective-permute-done.8.down_ref
  116.2 3.7 %collective-permute-start.9 = (bf16[8,256,128]{2,1,0:T(8,128)(2,1)S(1)}, bf16[8,256,128]{2,1,0:T(8,128)(2,1)S(1)}, u32[]{:S(2)}, u32[]{:S(2)}) collective-permute-start(bf16[8,256,128]{2,1,0:T(8,128)(2,1)S(1)} %shard_map.180.mine_ref), channel_id=1, source_target_pairs={{0,1},{1,0},{2,3},{3,2},{4,5},{5,4},{6,7},{7,6},{8,9},{9,8},{10,11... | collective-permute-start | bytes 1572872 | tf_op jit(solution)/shard_map/ppermute | solution.py:516
  119.9 1.0 shard_map.181
  120.8 0.6 collective-permute-done.9.other_ref
  121.4 1.3 %shard_map.182 = (bf16[2048,128]{1,0:T(8,128)(2,1)}, bf16[2048,128]{1,0:T(8,128)(2,1)}) custom-call(bf16[2,1024,128]{2,1,0:T(8,128)(2,1)S(1)} %get-tuple-element.77.near_ref, bf16[8,256,128]{2,1,0:T(8,128)(2,1)S(1)} %collective-permute-done.9.other_ref), custom_call_target="tpu_custom_call" | custom-call | flops 100000000 | bytes 1048576 | tf_op jit(solution)/shard_map/pallas_call | solution.py:524
  (10 shorter events, 0.1 us)
Async XLA Ops:
  4.1 7.8 %copy-start.8 = (bf16[1024,128]{1,0:T(8,128)(2,1)S(1)}, bf16[1024,128]{1,0:T(8,128)(2,1)}, u32[]{:S(2)}) copy-start(bf16[1024,128]{1,0:T(8,128)(2,1)} %get-tuple-element.52) | copy-start | bytes 786436
  4.1 25.3 %all-to-all-start = ((bf16[16,304,128]{2,1,0:T(8,128)(2,1)}), bf16[16,304,128]{2,1,0:T(8,128)(2,1)S(1)}, u32[]{:S(2)}, u32[]{:S(2)}) async-start(bf16[16,304,128]{2,1,0:T(8,128)(2,1)} %get-tuple-element.44), calls=%async_computation | async-start | bytes 2490368 | tf_op jit(solution)/shard_map/all_to_all | solution.py:456
  11.8 29.4 %collective-permute-start = (bf16[1024,128]{1,0:T(8,128)(2,1)S(1)}, bf16[1024,128]{1,0:T(8,128)(2,1)S(1)}, u32[]{:S(2)}, u32[]{:S(2)}) collective-permute-start(bf16[1024,128]{1,0:T(8,128)(2,1)S(1)} %copy-done.8), channel_id=1, source_target_pairs={{0,240},{16,224},{32,208},{48,192},{64,176},{80,160},{96,144},{112... | collective-permute-start | bytes 786440 | tf_op jit(solution)/shard_map/ppermute | solution.py:455
  19.7 20.4 %copy-start = (bf16[256,4,128]{2,1,0:T(4,128)(2,1)S(1)}, bf16[256,4,128]{2,1,0:T(4,128)(2,1)}, u32[]{:S(2)}) copy-start(bf16[256,4,128]{2,1,0:T(4,128)(2,1)} %param.16) | copy-start | bytes 786436
  19.7 20.4 %copy-start.3 = (f32[4,256]{1,0:T(4,128)S(1)}, f32[4,256]{1,0:T(4,128)}, u32[]{:S(2)}) copy-start(f32[4,256]{1,0:T(4,128)} %decay_ref.6) | copy-start | bytes 12292
  19.7 20.4 %copy-start.4 = (f32[4,128]{1,0:T(4,128)S(1)}, f32[4,128]{1,0:T(4,128)}, u32[]{:S(2)}) copy-start(f32[4,128]{1,0:T(4,128)} %gain_ref.2) | copy-start | bytes 6148
  19.7 20.4 %copy-start.6 = (bf16[3,4,256,128]{3,2,1,0:T(8,128)(2,1)S(1)}, bf16[3,4,256,128]{3,2,1,0:T(8,128)(2,1)}, u32[]{:S(2)}) copy-start(bf16[3,4,256,128]{3,2,1,0:T(8,128)(2,1)} %get-tuple-element.47.heads_ref) | copy-start | bytes 2359300
  19.7 20.4 %copy-start.7 = (f32[4,256,128]{2,1,0:T(8,128)S(1)}, f32[4,256,128]{2,1,0:T(8,128)}, u32[]{:S(2)}) copy-start(f32[4,256,128]{2,1,0:T(8,128)} %get-tuple-element.46.within_ref) | copy-start | bytes 1572868
  40.1 21.7 %copy-start.1 = (bf16[256,4,128]{2,1,0:T(4,128)(2,1)S(1)}, bf16[256,4,128]{2,1,0:T(4,128)(2,1)}, u32[]{:S(2)}) copy-start(bf16[256,4,128]{2,1,0:T(4,128)(2,1)} %param.17) | copy-start | bytes 786436
  40.1 21.7 %copy-start.2 = (bf16[256,4,128]{2,1,0:T(4,128)(2,1)S(1)}, bf16[256,4,128]{2,1,0:T(4,128)(2,1)}, u32[]{:S(2)}) copy-start(bf16[256,4,128]{2,1,0:T(4,128)(2,1)} %param.20) | copy-start | bytes 786436
  40.1 21.7 %copy-start.5 = (s32[32]{0:T(128)S(1)}, s32[32]{0:T(128)}, u32[]{:S(2)}) copy-start(s32[32]{0:T(128)} %reach_ref.1) | copy-start | bytes 388
  41.3 20.6 %collective-permute-start.1 = (bf16[16,304,128]{2,1,0:T(8,128)(2,1)S(1)}, bf16[16,304,128]{2,1,0:T(8,128)(2,1)S(1)}, u32[]{:S(2)}, u32[]{:S(2)}) collective-permute-start(bf16[16,304,128]{2,1,0:T(8,128)(2,1)S(1)} %all-to-all-done.got_ref.mine_ref.first_ref), channel_id=1, source_target_pairs={{0,1},{1,0},{2,3},{3,2},{4,5},{5,4},{6,7},{7,6},{8,9},{9,8},{10,11... | collective-permute-start | bytes 3735560 | tf_op jit(solution)/shard_map/ppermute | solution.py:468
  73.2 3.0 %collective-permute-start.2 = (bf16[16,256,128]{2,1,0:T(8,128)(2,1)S(1)}, bf16[16,256,128]{2,1,0:T(8,128)(2,1)S(1)}, u32[]{:S(2)}, u32[]{:S(2)}) collective-permute-start(bf16[16,256,128]{2,1,0:T(8,128)(2,1)S(1)} %get-tuple-element.61), channel_id=1, source_target_pairs={{0,1},{1,0},{2,3},{3,2},{4,5},{5,4},{6,7},{7,6},{8,9},{9,8},{10,11... | collective-permute-start | bytes 3145736 | tf_op jit(solution)/shard_map/ppermute | solution.py:489
  98.4 11.9 %all-to-all-start.4 = ((bf16[16,32,128]{2,1,0:T(8,128)(2,1)}), bf16[16,32,128]{2,1,0:T(8,128)(2,1)S(1)}, u32[]{:S(2)}, u32[]{:S(2)}) async-start(bf16[16,32,128]{2,1,0:T(8,128)(2,1)} %get-tuple-element.63), calls=%async_computation.4 | async-start | bytes 262144 | tf_op jit(solution)/shard_map/all_to_all | solution.py:506
  101.9 8.3 %collective-permute-start.5 = (bf16[256,128]{1,0:T(8,128)(2,1)S(1)}, bf16[256,128]{1,0:T(8,128)(2,1)S(1)}, u32[]{:S(2)}, u32[]{:S(2)}) collective-permute-start(bf16[256,128]{1,0:T(8,128)(2,1)S(1)} %get-tuple-element.70.own_ref), channel_id=1, source_target_pairs={{0,12},{1,13},{2,14},{3,15},{4,0},{5,1},{6,2},{7,3},{8,4},{9,5},{1... | collective-permute-start | bytes 196616 | tf_op jit(solution)/shard_map/ppermute | solution.py:504
  102.3 7.9 %collective-permute-start.4 = (bf16[256,128]{1,0:T(8,128)(2,1)S(1)}, bf16[256,128]{1,0:T(8,128)(2,1)S(1)}, u32[]{:S(2)}, u32[]{:S(2)}) collective-permute-start(bf16[256,128]{1,0:T(8,128)(2,1)S(1)} %get-tuple-element.70.own_ref), channel_id=1, source_target_pairs={{0,4},{1,5},{2,6},{3,7},{4,8},{5,9},{6,10},{7,11},{8,12},{9,13},{1... | collective-permute-start | bytes 196616 | tf_op jit(solution)/shard_map/ppermute | solution.py:504
  104.4 11.4 %collective-permute-start.6 = (bf16[256,128]{1,0:T(8,128)(2,1)S(1)}, bf16[256,128]{1,0:T(8,128)(2,1)S(1)}, u32[]{:S(2)}, u32[]{:S(2)}) collective-permute-start(bf16[256,128]{1,0:T(8,128)(2,1)S(1)} %get-tuple-element.70.own_ref), channel_id=1, source_target_pairs={{0,8},{1,9},{2,10},{3,11},{4,12},{5,13},{6,14},{7,15},{8,0},{9,1},... | collective-permute-start | bytes 196616 | tf_op jit(solution)/shard_map/ppermute | solution.py:504
  105.6 10.1 %collective-permute-start.3 = (bf16[1024,128]{1,0:T(8,128)(2,1)S(1)}, bf16[1024,128]{1,0:T(8,128)(2,1)S(1)}, u32[]{:S(2)}, u32[]{:S(2)}) collective-permute-start(bf16[1024,128]{1,0:T(8,128)(2,1)S(1)} %get-tuple-element.69), channel_id=1, source_target_pairs={{0,240},{16,224},{32,208},{48,192},{64,176},{80,160},{96,144},{112... | collective-permute-start | bytes 786440 | tf_op jit(solution)/shard_map/ppermute | solution.py:509
  110.3 5.8 %collective-permute-start.7 = (bf16[512,128]{1,0:T(8,128)(2,1)S(1)}, bf16[512,128]{1,0:T(8,128)(2,1)S(1)}, u32[]{:S(2)}, u32[]{:S(2)}) collective-permute-start(bf16[512,128]{1,0:T(8,128)(2,1)S(1)} %get-tuple-element.72), channel_id=1, source_target_pairs={{0,2},{1,3},{2,4},{3,5},{4,6},{5,7},{6,8},{7,9},{8,10},{9,11},{10,... | collective-permute-start | bytes 393224 | tf_op jit(solution)/shard_map/ppermute | solution.py:504
  110.8 5.3 %collective-permute-start.8 = (bf16[512,128]{1,0:T(8,128)(2,1)S(1)}, bf16[512,128]{1,0:T(8,128)(2,1)S(1)}, u32[]{:S(2)}, u32[]{:S(2)}) collective-permute-start(bf16[512,128]{1,0:T(8,128)(2,1)S(1)} %get-tuple-element.73), channel_id=1, source_target_pairs={{0,14},{1,15},{2,0},{3,1},{4,2},{5,3},{6,4},{7,5},{8,6},{9,7},{10,... | collective-permute-start | bytes 393224 | tf_op jit(solution)/shard_map/ppermute | solution.py:504
  116.2 5.2 %collective-permute-start.9 = (bf16[8,256,128]{2,1,0:T(8,128)(2,1)S(1)}, bf16[8,256,128]{2,1,0:T(8,128)(2,1)S(1)}, u32[]{:S(2)}, u32[]{:S(2)}) collective-permute-start(bf16[8,256,128]{2,1,0:T(8,128)(2,1)S(1)} %shard_map.180.mine_ref), channel_id=1, source_target_pairs={{0,1},{1,0},{2,3},{3,2},{4,5},{5,4},{6,7},{7,6},{8,9},{9,8},{10,11... | collective-permute-start | bytes 1572872 | tf_op jit(solution)/shard_map/ppermute | solution.py:516

commit v8 on v7

--- a/solution.py
+++ b/solution.py
@@ -504,7 +504,7 @@
     along = lambda x, k: lax.ppermute(x, "head", ALONG[k])
     below, above, far = along(block, 2), along(block, -2), along(block, 4)
     later = lax.all_to_all(suffixes, "ctx", 0, 0).reshape(OWN * HD, HD)
-    up, down = call(pair_kernel, [((2 * LB, HD), bf16)] * 2, count=3, flops=10**8)(block, below, after(above, later))
+    up, down = call(pair_kernel, [((2 * LB, HD), bf16)] * 2, count=3, flops=10**8)(block, below, above)
     up, down = along(up, 1), along(down, -1)
     traded = lax.ppermute(after(traded, block), "ctx", MIRROR)
     lin_dq, lin_dk, lin_dv = call(inner_kernel, [FLAT] * 3, [WIDE], count=5, flops=4 * 10**9)(

time: 124 us -> 124 us (level)
  no operation moved by 1% of the time
where the time goes in v8:
time: 124 us
  blocking collectives  48.6 us (39%)
  starting transfers between devices  36.4 us (29%)
  Pallas kernels  26 us (21%)
  waiting for transfers between devices  11.8 us (10%)
    all_to_all x1, blocking collectives, per_device(): got_back = lax.all_to_all(pay_back, 'ctx', 0, 0)  22.2 us
    all_to_all x1, blocking collectives, per_device(): total = lax.all_to_all(after(sums, trade), 'head', 0, 0)  15.8 us
    pallas_call x1, Pallas kernels, per_device(): call(soft_kernel, [HALF_FLAT, HALF_FLAT, FLAT, KEY_PARTS, KEY_PARTS], [FL...  11.3 us
    all_to_all x1, blocking collectives, per_device(): state = lax.all_to_all(prefixes, 'ctx', 0, 0).reshape(OWN * HD, HD)  10.6 us
    all_to_all x1, waiting for transfers between devices, per_device(): mine = lax.all_to_all(pay, 'ctx', 0, 0)  9.68 us
    all_to_all x1, starting transfers between devices, per_device(): mine = lax.all_to_all(pay, 'ctx', 0, 0)  7.73 us
    ppermute x5, starting transfers between devices, per_device(): along = lambda x, k: lax.ppermute(x, 'head', ALONG[k])  6.59 us
    ppermute x1, starting transfers between devices, per_device(): other = lax.ppermute(after(mine, sums, trade), 'head', OTHER_CORE)  4.79 us
  transfers between devices with their start and end apart: 12, of which 4 were waited for; matrix products, arithmetic and copies ran while one was open for 0% of the time, Pallas kernels for 7%

profile of v8, /device:TPU:1, one launch (start us, length us, event | category | flops | bytes accessed | tf_op | source)
XLA Modules:
  0.0 123.6 jit_solution(9107678315699151647)
XLA Ops:
  0.6 3.4 %shard_map.170 = (bf16[16,304,128]{2,1,0:T(8,128)(2,1)}, bf16[1024,128]{1,0:T(8,128)(2,1)}) custom-call(bf16[1024,128]{1,0:T(8,128)(2,1)} %bitcast.33, bf16[1024,128]{1,0:T(8,128)(2,1)} %bitcast.35, f32[4,256]{1,0:T(4,128)} %decay_ref.6, bf16[2048,128]{1,0:T(8,128)(2,1)} %bitcast.28, bf16[2048,128]{1,0:T(8,128)(2,1)} %bitcast.29, ...), custom_call_target="tpu_custom_call" | custom-call | flops 1000000000 | bytes 1048576 | tf_op jit(solution)/shard_map/pallas_call | solution.py:432
  4.1 0.0 copy-start.8
  4.1 7.7 %all-to-all-start = ((bf16[16,304,128]{2,1,0:T(8,128)(2,1)}), bf16[16,304,128]{2,1,0:T(8,128)(2,1)S(1)}, u32[]{:S(2)}, u32[]{:S(2)}) async-start(bf16[16,304,128]{2,1,0:T(8,128)(2,1)} %get-tuple-element.43), calls=%async_computation | async-start | bytes 2490368 | tf_op jit(solution)/shard_map/all_to_all | solution.py:456
  11.8 0.0 copy-done.8
  11.8 4.8 %collective-permute-start = (bf16[1024,128]{1,0:T(8,128)(2,1)S(1)}, bf16[1024,128]{1,0:T(8,128)(2,1)S(1)}, u32[]{:S(2)}, u32[]{:S(2)}) collective-permute-start(bf16[1024,128]{1,0:T(8,128)(2,1)S(1)} %copy-done.8), channel_id=1, source_target_pairs={{0,240},{16,224},{32,208},{48,192},{64,176},{80,160},{96,144},{112... | collective-permute-start | bytes 786440 | tf_op jit(solution)/shard_map/ppermute | solution.py:455
  16.6 3.1 %shard_map.171 = (f32[4,256,128]{2,1,0:T(8,128)}, bf16[3,4,256,128]{3,2,1,0:T(8,128)(2,1)}) custom-call(bf16[1024,128]{1,0:T(8,128)(2,1)} %bitcast.32, bf16[1024,128]{1,0:T(8,128)(2,1)} %bitcast.34, bf16[1024,128]{1,0:T(8,128)(2,1)} %bitcast.36, f32[4,256]{1,0:T(4,128)} %decay_ref.6), custom_call_target="tpu_custom_call" | custom-call | flops 1000000000 | bytes 1048576 | tf_op jit(solution)/shard_map/pallas_call | solution.py:452
  19.7 0.0 copy-start.6
  19.7 0.0 copy-start.7
  19.7 9.7 %all-to-all-done.got_ref.mine_ref.first_ref = bf16[16,304,128]{2,1,0:T(8,128)(2,1)S(1)} async-done(((bf16[16,304,128]{2,1,0:T(8,128)(2,1)}), bf16[16,304,128]{2,1,0:T(8,128)(2,1)S(1)}, u32[]{:S(2)}, u32[]{:S(2)}) %all-to-all-start) | async-done | bytes 1245216 | tf_op jit(solution)/shard_map/all_to_all | solution.py:456
  29.5 10.6 %all_to_all.25 = bf16[16,32,128]{2,1,0:T(8,128)(2,1)S(1)} all-to-all(bf16[16,32,128]{2,1,0:T(8,128)(2,1)S(1)} %shard_map.172), channel_id=1, replica_groups=mesh['ctx'=16,'head'=16] {'ctx'}, dimensions={0} | all-to-all | bytes 262144 | tf_op jit(solution)/shard_map/all_to_all | solution.py:460
  40.1 0.0 copy-done
  40.1 0.0 copy-done.3
  40.1 0.0 copy-done.4
  40.1 0.0 copy-done.6
  40.1 0.0 copy-start.1
  40.1 0.0 copy-start.2
  40.1 0.0 copy-start.5
  40.2 1.1 shard_map.173
  41.3 0.0 collective-permute-done.trade_ref
  41.3 4.8 %collective-permute-start.1 = (bf16[16,304,128]{2,1,0:T(8,128)(2,1)S(1)}, bf16[16,304,128]{2,1,0:T(8,128)(2,1)S(1)}, u32[]{:S(2)}, u32[]{:S(2)}) collective-permute-start(bf16[16,304,128]{2,1,0:T(8,128)(2,1)S(1)} %all-to-all-done.got_ref.mine_ref.first_ref), channel_id=1, source_target_pairs={{0,1},{1,0},{2,3},{3,2},{4,5},{5,4},{6,7},{7,6},{8,9},{9,8},{10,11... | collective-permute-start | bytes 3735560 | tf_op jit(solution)/shard_map/ppermute | solution.py:468
  46.1 15.8 %all_to_all.26.got_ref = f32[16,4,128]{2,1,0:T(4,128)S(1)} all-to-all(f32[16,4,128]{2,1,0:T(4,128)S(1)} %get-tuple-element.52), channel_id=1, replica_groups=mesh['ctx'=16,'head'=16] {'head'}, dimensions={0} | all-to-all | bytes 65536 | tf_op jit(solution)/shard_map/all_to_all | solution.py:469
  61.8 0.0 collective-permute-done.1.other_ref
  61.9 11.3 %shard_map.174 = (bf16[512,128]{1,0:T(8,128)(2,1)S(1)}, bf16[512,128]{1,0:T(8,128)(2,1)S(1)}, bf16[1024,128]{1,0:T(8,128)(2,1)S(1)}, bf16[16,256,128]{2,1,0:T(8,128)(2,1)S(1)}, bf16[16,256,128]{2,1,0:T(8,128)(2,1)S(1)}) custom-call(s32[32]{0:T(128)S(1)} %copy-done.5, bf16[1024,128]{1,0:T(8,128)(2,1)S(1)} %bitcast.25, bf16[1024,128]{1,0:T(8,128)(2,1)S(1)} %bitcast.27, ...), custom_call_target="tpu_custom_call" | custom-call | flops 10000000000 | bytes 1048576 | tf_op jit(solution)/shard_map/pallas_call | solution.py:470
  73.2 0.7 collective-permute-start.2
  73.9 1.1 shard_map.175
  75.0 1.1 collective-permute-done.2.got_ref
  76.1 0.2 shard_map.176
  76.4 22.2 %all_to_all.27.got_ref = bf16[16,288,128]{2,1,0:T(8,128)(2,1)S(1)} all-to-all(bf16[16,288,128]{2,1,0:T(8,128)(2,1)S(1)} %shard_map.176), channel_id=1, replica_groups=mesh['ctx'=16,'head'=16] {'ctx'}, dimensions={0} | all-to-all | bytes 2359296 | tf_op jit(solution)/shard_map/all_to_all | solution.py:500
  98.6 0.7 shard_map.177
  99.3 3.5 %all-to-all-start.4 = ((bf16[16,32,128]{2,1,0:T(8,128)(2,1)}), bf16[16,32,128]{2,1,0:T(8,128)(2,1)S(1)}, u32[]{:S(2)}, u32[]{:S(2)}) async-start(bf16[16,32,128]{2,1,0:T(8,128)(2,1)} %get-tuple-element.62), calls=%async_computation.4 | async-start | bytes 262144 | tf_op jit(solution)/shard_map/all_to_all | solution.py:506
  102.8 0.4 collective-permute-start.5
  103.2 2.0 %collective-permute-start.4 = (bf16[256,128]{1,0:T(8,128)(2,1)S(1)}, bf16[256,128]{1,0:T(8,128)(2,1)S(1)}, u32[]{:S(2)}, u32[]{:S(2)}) collective-permute-start(bf16[256,128]{1,0:T(8,128)(2,1)S(1)} %get-tuple-element.69.own_ref), channel_id=1, source_target_pairs={{0,4},{1,5},{2,6},{3,7},{4,8},{5,9},{6,10},{7,11},{8,12},{9,13},{1... | collective-permute-start | bytes 196616 | tf_op jit(solution)/shard_map/ppermute | solution.py:504
  105.2 1.3 %collective-permute-start.6 = (bf16[256,128]{1,0:T(8,128)(2,1)S(1)}, bf16[256,128]{1,0:T(8,128)(2,1)S(1)}, u32[]{:S(2)}, u32[]{:S(2)}) collective-permute-start(bf16[256,128]{1,0:T(8,128)(2,1)S(1)} %get-tuple-element.69.own_ref), channel_id=1, source_target_pairs={{0,8},{1,9},{2,10},{3,11},{4,12},{5,13},{6,14},{7,15},{8,0},{9,1},... | collective-permute-start | bytes 196616 | tf_op jit(solution)/shard_map/ppermute | solution.py:504
  106.5 4.6 %collective-permute-start.3 = (bf16[1024,128]{1,0:T(8,128)(2,1)S(1)}, bf16[1024,128]{1,0:T(8,128)(2,1)S(1)}, u32[]{:S(2)}, u32[]{:S(2)}) collective-permute-start(bf16[1024,128]{1,0:T(8,128)(2,1)S(1)} %get-tuple-element.68), channel_id=1, source_target_pairs={{0,240},{16,224},{32,208},{48,192},{64,176},{80,160},{96,144},{112... | collective-permute-start | bytes 786440 | tf_op jit(solution)/shard_map/ppermute | solution.py:509
  111.1 0.0 collective-permute-done.5.above_ref
  111.1 0.0 collective-permute-done.4.below_ref
  111.2 0.5 collective-permute-start.7
  111.7 2.4 %collective-permute-start.8 = (bf16[512,128]{1,0:T(8,128)(2,1)S(1)}, bf16[512,128]{1,0:T(8,128)(2,1)S(1)}, u32[]{:S(2)}, u32[]{:S(2)}) collective-permute-start(bf16[512,128]{1,0:T(8,128)(2,1)S(1)} %get-tuple-element.71), channel_id=1, source_target_pairs={{0,14},{1,15},{2,0},{3,1},{4,2},{5,3},{6,4},{7,5},{8,6},{9,7},{10,... | collective-permute-start | bytes 393224 | tf_op jit(solution)/shard_map/ppermute | solution.py:504
  114.0 0.0 all-to-all-done.4
  114.0 2.6 %shard_map.178 = (bf16[1024,128]{1,0:T(8,128)(2,1)}, bf16[1024,128]{1,0:T(8,128)(2,1)}, bf16[1024,128]{1,0:T(8,128)(2,1)}) custom-call(bf16[3,4,256,128]{3,2,1,0:T(8,128)(2,1)S(1)} %copy-done.6, bf16[4,256,128]{2,1,0:T(8,128)(2,1)S(1)} %get-tuple-element.58.ag_ref, bf16[512,128]{1,0:T(8,128)(2,1)S(1)} %bitcast.20, bf16[512,128]{1,0:T(8,128)(2,1)S(1)} %bitcast.21, ...), custom_call_target="tpu_custom_call" | custom-call | flops 4000000000 | bytes 1048576 | tf_op jit(solution)/shard_map/pallas_call | solution.py:510
  116.6 0.0 collective-permute-done.3.traded_ref
  116.6 0.0 collective-permute-done.6.far_ref
  116.6 0.4 collective-permute-done.7.up_ref
  117.0 0.0 collective-permute-done.8.down_ref
  117.0 3.7 %collective-permute-start.9 = (bf16[8,256,128]{2,1,0:T(8,128)(2,1)S(1)}, bf16[8,256,128]{2,1,0:T(8,128)(2,1)S(1)}, u32[]{:S(2)}, u32[]{:S(2)}) collective-permute-start(bf16[8,256,128]{2,1,0:T(8,128)(2,1)S(1)} %shard_map.180.mine_ref), channel_id=1, source_target_pairs={{0,1},{1,0},{2,3},{3,2},{4,5},{5,4},{6,7},{7,6},{8,9},{9,8},{10,11... | collective-permute-start | bytes 1572872 | tf_op jit(solution)/shard_map/ppermute | solution.py:516
  120.7 1.0 shard_map.181
  121.7 0.6 collective-permute-done.9.other_ref
  122.3 1.3 %shard_map.182 = (bf16[2048,128]{1,0:T(8,128)(2,1)}, bf16[2048,128]{1,0:T(8,128)(2,1)}) custom-call(bf16[2,1024,128]{2,1,0:T(8,128)(2,1)S(1)} %get-tuple-element.75.near_ref, bf16[8,256,128]{2,1,0:T(8,128)(2,1)S(1)} %collective-permute-done.9.other_ref), custom_call_target="tpu_custom_call" | custom-call | flops 100000000 | bytes 1048576 | tf_op jit(solution)/shard_map/pallas_call | solution.py:524
  (10 shorter events, 0.1 us)
Async XLA Ops:
  4.1 7.8 %copy-start.8 = (bf16[1024,128]{1,0:T(8,128)(2,1)S(1)}, bf16[1024,128]{1,0:T(8,128)(2,1)}, u32[]{:S(2)}) copy-start(bf16[1024,128]{1,0:T(8,128)(2,1)} %get-tuple-element.51) | copy-start | bytes 786436
  4.1 25.3 %all-to-all-start = ((bf16[16,304,128]{2,1,0:T(8,128)(2,1)}), bf16[16,304,128]{2,1,0:T(8,128)(2,1)S(1)}, u32[]{:S(2)}, u32[]{:S(2)}) async-start(bf16[16,304,128]{2,1,0:T(8,128)(2,1)} %get-tuple-element.43), calls=%async_computation | async-start | bytes 2490368 | tf_op jit(solution)/shard_map/all_to_all | solution.py:456
  11.8 29.4 %collective-permute-start = (bf16[1024,128]{1,0:T(8,128)(2,1)S(1)}, bf16[1024,128]{1,0:T(8,128)(2,1)S(1)}, u32[]{:S(2)}, u32[]{:S(2)}) collective-permute-start(bf16[1024,128]{1,0:T(8,128)(2,1)S(1)} %copy-done.8), channel_id=1, source_target_pairs={{0,240},{16,224},{32,208},{48,192},{64,176},{80,160},{96,144},{112... | collective-permute-start | bytes 786440 | tf_op jit(solution)/shard_map/ppermute | solution.py:455
  19.7 20.4 %copy-start = (bf16[256,4,128]{2,1,0:T(4,128)(2,1)S(1)}, bf16[256,4,128]{2,1,0:T(4,128)(2,1)}, u32[]{:S(2)}) copy-start(bf16[256,4,128]{2,1,0:T(4,128)(2,1)} %param.16) | copy-start | bytes 786436
  19.7 20.4 %copy-start.3 = (f32[4,256]{1,0:T(4,128)S(1)}, f32[4,256]{1,0:T(4,128)}, u32[]{:S(2)}) copy-start(f32[4,256]{1,0:T(4,128)} %decay_ref.6) | copy-start | bytes 12292
  19.7 20.4 %copy-start.4 = (f32[4,128]{1,0:T(4,128)S(1)}, f32[4,128]{1,0:T(4,128)}, u32[]{:S(2)}) copy-start(f32[4,128]{1,0:T(4,128)} %gain_ref.2) | copy-start | bytes 6148
  19.7 20.4 %copy-start.6 = (bf16[3,4,256,128]{3,2,1,0:T(8,128)(2,1)S(1)}, bf16[3,4,256,128]{3,2,1,0:T(8,128)(2,1)}, u32[]{:S(2)}) copy-start(bf16[3,4,256,128]{3,2,1,0:T(8,128)(2,1)} %get-tuple-element.46.heads_ref) | copy-start | bytes 2359300
  19.7 20.4 %copy-start.7 = (f32[4,256,128]{2,1,0:T(8,128)S(1)}, f32[4,256,128]{2,1,0:T(8,128)}, u32[]{:S(2)}) copy-start(f32[4,256,128]{2,1,0:T(8,128)} %get-tuple-element.45.within_ref) | copy-start | bytes 1572868
  40.1 21.7 %copy-start.1 = (bf16[256,4,128]{2,1,0:T(4,128)(2,1)S(1)}, bf16[256,4,128]{2,1,0:T(4,128)(2,1)}, u32[]{:S(2)}) copy-start(bf16[256,4,128]{2,1,0:T(4,128)(2,1)} %param.17) | copy-start | bytes 786436
  40.1 21.7 %copy-start.2 = (bf16[256,4,128]{2,1,0:T(4,128)(2,1)S(1)}, bf16[256,4,128]{2,1,0:T(4,128)(2,1)}, u32[]{:S(2)}) copy-start(bf16[256,4,128]{2,1,0:T(4,128)(2,1)} %param.20) | copy-start | bytes 786436
  40.1 21.7 %copy-start.5 = (s32[32]{0:T(128)S(1)}, s32[32]{0:T(128)}, u32[]{:S(2)}) copy-start(s32[32]{0:T(128)} %reach_ref.1) | copy-start | bytes 388
  41.3 20.6 %collective-permute-start.1 = (bf16[16,304,128]{2,1,0:T(8,128)(2,1)S(1)}, bf16[16,304,128]{2,1,0:T(8,128)(2,1)S(1)}, u32[]{:S(2)}, u32[]{:S(2)}) collective-permute-start(bf16[16,304,128]{2,1,0:T(8,128)(2,1)S(1)} %all-to-all-done.got_ref.mine_ref.first_ref), channel_id=1, source_target_pairs={{0,1},{1,0},{2,3},{3,2},{4,5},{5,4},{6,7},{7,6},{8,9},{9,8},{10,11... | collective-permute-start | bytes 3735560 | tf_op jit(solution)/shard_map/ppermute | solution.py:468
  73.2 3.0 %collective-permute-start.2 = (bf16[16,256,128]{2,1,0:T(8,128)(2,1)S(1)}, bf16[16,256,128]{2,1,0:T(8,128)(2,1)S(1)}, u32[]{:S(2)}, u32[]{:S(2)}) collective-permute-start(bf16[16,256,128]{2,1,0:T(8,128)(2,1)S(1)} %get-tuple-element.60), channel_id=1, source_target_pairs={{0,1},{1,0},{2,3},{3,2},{4,5},{5,4},{6,7},{7,6},{8,9},{9,8},{10,11... | collective-permute-start | bytes 3145736 | tf_op jit(solution)/shard_map/ppermute | solution.py:489
  99.3 14.8 %all-to-all-start.4 = ((bf16[16,32,128]{2,1,0:T(8,128)(2,1)}), bf16[16,32,128]{2,1,0:T(8,128)(2,1)S(1)}, u32[]{:S(2)}, u32[]{:S(2)}) async-start(bf16[16,32,128]{2,1,0:T(8,128)(2,1)} %get-tuple-element.62), calls=%async_computation.4 | async-start | bytes 262144 | tf_op jit(solution)/shard_map/all_to_all | solution.py:506
  102.8 8.3 %collective-permute-start.5 = (bf16[256,128]{1,0:T(8,128)(2,1)S(1)}, bf16[256,128]{1,0:T(8,128)(2,1)S(1)}, u32[]{:S(2)}, u32[]{:S(2)}) collective-permute-start(bf16[256,128]{1,0:T(8,128)(2,1)S(1)} %get-tuple-element.69.own_ref), channel_id=1, source_target_pairs={{0,12},{1,13},{2,14},{3,15},{4,0},{5,1},{6,2},{7,3},{8,4},{9,5},{1... | collective-permute-start | bytes 196616 | tf_op jit(solution)/shard_map/ppermute | solution.py:504
  103.2 7.9 %collective-permute-start.4 = (bf16[256,128]{1,0:T(8,128)(2,1)S(1)}, bf16[256,128]{1,0:T(8,128)(2,1)S(1)}, u32[]{:S(2)}, u32[]{:S(2)}) collective-permute-start(bf16[256,128]{1,0:T(8,128)(2,1)S(1)} %get-tuple-element.69.own_ref), channel_id=1, source_target_pairs={{0,4},{1,5},{2,6},{3,7},{4,8},{5,9},{6,10},{7,11},{8,12},{9,13},{1... | collective-permute-start | bytes 196616 | tf_op jit(solution)/shard_map/ppermute | solution.py:504
  105.2 11.4 %collective-permute-start.6 = (bf16[256,128]{1,0:T(8,128)(2,1)S(1)}, bf16[256,128]{1,0:T(8,128)(2,1)S(1)}, u32[]{:S(2)}, u32[]{:S(2)}) collective-permute-start(bf16[256,128]{1,0:T(8,128)(2,1)S(1)} %get-tuple-element.69.own_ref), channel_id=1, source_target_pairs={{0,8},{1,9},{2,10},{3,11},{4,12},{5,13},{6,14},{7,15},{8,0},{9,1},... | collective-permute-start | bytes 196616 | tf_op jit(solution)/shard_map/ppermute | solution.py:504
  106.5 10.1 %collective-permute-start.3 = (bf16[1024,128]{1,0:T(8,128)(2,1)S(1)}, bf16[1024,128]{1,0:T(8,128)(2,1)S(1)}, u32[]{:S(2)}, u32[]{:S(2)}) collective-permute-start(bf16[1024,128]{1,0:T(8,128)(2,1)S(1)} %get-tuple-element.68), channel_id=1, source_target_pairs={{0,240},{16,224},{32,208},{48,192},{64,176},{80,160},{96,144},{112... | collective-permute-start | bytes 786440 | tf_op jit(solution)/shard_map/ppermute | solution.py:509
  111.2 5.8 %collective-permute-start.7 = (bf16[512,128]{1,0:T(8,128)(2,1)S(1)}, bf16[512,128]{1,0:T(8,128)(2,1)S(1)}, u32[]{:S(2)}, u32[]{:S(2)}) collective-permute-start(bf16[512,128]{1,0:T(8,128)(2,1)S(1)} %get-tuple-element.70), channel_id=1, source_target_pairs={{0,2},{1,3},{2,4},{3,5},{4,6},{5,7},{6,8},{7,9},{8,10},{9,11},{10,... | collective-permute-start | bytes 393224 | tf_op jit(solution)/shard_map/ppermute | solution.py:504
  111.7 5.3 %collective-permute-start.8 = (bf16[512,128]{1,0:T(8,128)(2,1)S(1)}, bf16[512,128]{1,0:T(8,128)(2,1)S(1)}, u32[]{:S(2)}, u32[]{:S(2)}) collective-permute-start(bf16[512,128]{1,0:T(8,128)(2,1)S(1)} %get-tuple-element.71), channel_id=1, source_target_pairs={{0,14},{1,15},{2,0},{3,1},{4,2},{5,3},{6,4},{7,5},{8,6},{9,7},{10,... | collective-permute-start | bytes 393224 | tf_op jit(solution)/shard_map/ppermute | solution.py:504
  117.0 5.2 %collective-permute-start.9 = (bf16[8,256,128]{2,1,0:T(8,128)(2,1)S(1)}, bf16[8,256,128]{2,1,0:T(8,128)(2,1)S(1)}, u32[]{:S(2)}, u32[]{:S(2)}) collective-permute-start(bf16[8,256,128]{2,1,0:T(8,128)(2,1)S(1)} %shard_map.180.mine_ref), channel_id=1, source_target_pairs={{0,1},{1,0},{2,3},{3,2},{4,5},{5,4},{6,7},{7,6},{8,9},{9,8},{10,11... | collective-permute-start | bytes 1572872 | tf_op jit(solution)/shard_map/ppermute | solution.py:516
